TPU v7x, 32 devices: a whole 2x2x4 slice. The times are simulated.
32 devices in a mesh: dp: 4 (over x, core), row: 4 (over z), col: 2 (over y).
Axes of the slice: x: 2, y: 2, z: 4, core: 2. Of those that a mesh axis runs over, the one named last changes fastest.
Arguments:
- hidden_in: bfloat16 [8192, 1024], P(('dp', 'col'), 'row'), may hold values from -6 to 6
- norm1_gain: float32 [1024], P('row'), may hold values from 0.25 to 1.75
- query_weight: bfloat16 [1024, 1024], P('row', 'col'), may hold values from -0.75 to 0.75
- key_weight: bfloat16 [1024, 512], P('row', 'col'), may hold values from -0.75 to 0.75
- value_weight: bfloat16 [1024, 512], P('row', 'col'), may hold values from -0.1875 to 0.1875
- output_weight: bfloat16 [1024, 1024], P('col', 'row'), may hold values from -0.375 to 0.375
- norm2_gain: float32 [1024], P('row'), may hold values from 0.25 to 1.75
- router_weight: bfloat16 [1024, 32], P('row'), may hold values from -0.09375 to 0.09375
- gate_weight: bfloat16 [32, 1024, 512], P(None, 'row', 'col'), may hold values from -0.1875 to 0.1875
- up_weight: bfloat16 [32, 1024, 512], P(None, 'row', 'col'), may hold values from -0.1875 to 0.1875
- down_weight: bfloat16 [32, 512, 1024], P(None, 'col', 'row'), may hold values from -1 to 1
- segment_ids: int32 [16, 512], P('dp'), may hold values from 0 to 3, never falling along the last dimension, each value on 1 to 256 neighbouring positions
- expert_ids: int32 [8192, 8], P('dp'), may hold values from 0 to 31, all different within a row; in each aligned block of 2048 rows (0 to 2047, 2048 to 4095, ...) at most 640 rows name the same one
- grad_out: bfloat16 [8192, 1024], P(('dp', 'col'), 'row'), may hold values from -6 to 6
Outputs:
- mixed_out: bfloat16 [8192, 1024], P(('dp', 'col'), 'row')
- grad_in: float32 [8192, 1024], P(('dp', 'col'), 'row')
- grad_norm1: float32 [1024], P('row')
- grad_query: float32 [1024, 1024], P('row', 'col')
- grad_key: float32 [1024, 512], P('row', 'col')
- grad_value: float32 [1024, 512], P('row', 'col')
- grad_output: float32 [1024, 1024], P('col', 'row')
- grad_norm2: float32 [1024], P('row')
- grad_router: float32 [1024, 32], P('row')
- grad_gate: float32 [32, 1024, 512], P('dp', 'row', 'col')
- grad_up: float32 [32, 1024, 512], P('dp', 'row', 'col')
- grad_down: float32 [32, 512, 1024], P('dp', 'col', 'row')
Inputs may be any that keep to these rules, and one draw needn't show every extreme that they name: `segment_ids`: segment numbers never fall along a sequence; each document has at most 256 tokens. `expert_ids`: each row names 8 different experts; among the 2048 rows of one index of dp no expert is named more than 640 times, a bound that some block reaches.
All inputs are finite; a program needn't handle non-finite values.
Results may differ from a plain program's by a relative error of at most 0.02.
Values may be sent and summed in bfloat16 or wider, within the bound.
No kernel may reach another device: no remote copies, remote signals or barrier semaphores. Data moves between devices by JAX's collectives and lax.ppermute only.
A program may use at most 256 MiB of HBM per device.

v0:
```python
import jax
import jax.numpy as jnp
from jax import lax
from jax.sharding import PartitionSpec as P

HEAD_DIM = 64


epsilon = 1e-06
rope_base = 10000.0
masked_score = -1e30


def rope_tables(seq_len, head_dim):
    midpoint = head_dim // 2
    frequency = rope_base ** (-2.0 * jnp.arange(midpoint, dtype=jnp.float32) / head_dim)
    angles = jnp.arange(seq_len, dtype=jnp.float32)[:, None] * frequency[None, :]
    return (jnp.cos(angles), jnp.sin(angles))


def rotate(values, cosines, sines):
    midpoint = values.shape[-1] // 2
    first = values[..., :midpoint]
    second = values[..., midpoint:]
    return jnp.concatenate([first * cosines - second * sines, second * cosines + first * sines], -1)


def rotate_back(grads, cosines, sines):
    midpoint = grads.shape[-1] // 2
    first = grads[..., :midpoint]
    second = grads[..., midpoint:]
    return jnp.concatenate([first * cosines + second * sines, second * cosines - first * sines], -1)


def block_mask(segments):
    positions = jnp.arange(segments.shape[0], dtype=jnp.int32)
    return (positions[None, :] <= positions[:, None]) & (segments[None, :] == segments[:, None])


def slot_tables(expert_ids, capacity, experts):
    count_rows, chosen = expert_ids.shape
    assigned = count_rows * chosen
    flat_ids = expert_ids.reshape(-1)
    member = (flat_ids[:, None] == jnp.arange(experts, dtype=jnp.int32)[None, :]).astype(jnp.int32)
    earlier = jnp.cumsum(member, 0) - member
    place = jnp.sum(earlier * member, 1)
    slot_of = flat_ids * capacity + place
    owner = (
        jnp.full((experts * capacity,), assigned, jnp.int32)
        .at[slot_of]
        .set(jnp.arange(assigned, dtype=jnp.int32))
    )
    filled = owner < assigned
    token_of = jnp.where(filled, owner // chosen, 0)
    return (slot_of.reshape(count_rows, chosen), owner, filled, token_of)


def token_blocks(piece):
    return lax.all_gather(piece, "col", axis=0, tiled=True)


def column_sums(term, rows):
    return lax.psum_scatter(
        term(jnp.int32(0), rows * lax.axis_size("col")), "col", scatter_dimension=0, tiled=True
    )


def row_stats(values):
    return lax.psum(values, "row")


def head_sums(partial_value):
    return lax.psum_scatter(partial_value, "row", scatter_dimension=1, tiled=True)


def head_gather(piece):
    return lax.all_gather(piece, "row", axis=1, tiled=True)


def slot_sums(term, rows):
    return lax.psum_scatter(
        term(jnp.int32(0), rows * lax.axis_size("row")), "row", scatter_dimension=0, tiled=True
    )


def slot_gather(piece):
    return lax.all_gather(piece, "row", axis=0, tiled=True)


def rms_forward(residual, gain, width):
    inv_rms = lax.rsqrt(row_stats(jnp.sum(residual * residual, -1))[:, None] / width + epsilon)
    return (residual * inv_rms * gain, inv_rms)


def norm_back(grad, values, inv_rms, gain, width):
    scaled = grad * gain
    inner = row_stats(jnp.sum(scaled * values, -1))[:, None]
    grad_gain = jnp.sum(grad * values * inv_rms, 0)
    return (inv_rms * scaled - values * inv_rms * inv_rms * inv_rms * inner / width, grad_gain)


def expert_term(left, right, pattern):

    def term(start, count):
        return jnp.einsum(pattern, left, right, preferred_element_type=jnp.float32).reshape(
            count, -1
        )

    return term


def token_term(values, slot_of, gates):

    def term(start, count):
        if gates is None:
            return jnp.sum(values[slot_of], 1)
        return jnp.einsum("tk,tkd->td", gates, values[slot_of])

    return term


def attend_forward(block):
    query, key, value, segments = block
    products = jnp.einsum("qgjd,kgd->gjqk", query, key, preferred_element_type=jnp.float32)
    scores = jnp.where(block_mask(segments), products * (1.0 / query.shape[-1]), masked_score)
    row_max = jnp.max(scores, -1, keepdims=True)
    powers = jnp.exp(scores - row_max)
    total = jnp.sum(powers, -1, keepdims=True)
    attention = (powers / total).astype(jnp.bfloat16)
    result = jnp.einsum("gjqk,kgd->qgjd", attention, value, preferred_element_type=jnp.float32)
    return (result.astype(jnp.bfloat16), (row_max + jnp.log(total))[..., 0])


def attend_backward(block):
    query, key, value, segments, log_sums, grad_heads = block
    scale = 1.0 / query.shape[-1]
    products = jnp.einsum("qgjd,kgd->gjqk", query, key, preferred_element_type=jnp.float32)
    scores = jnp.where(block_mask(segments), products * scale, masked_score)
    attention = jnp.exp(scores - log_sums[..., None])
    grad_value = jnp.einsum(
        "gjqk,qgjd->kgd",
        attention.astype(jnp.bfloat16),
        grad_heads,
        preferred_element_type=jnp.float32,
    )
    grad_probs = jnp.einsum("qgjd,kgd->gjqk", grad_heads, value, preferred_element_type=jnp.float32)
    row_dots = jnp.sum(grad_probs * attention, -1, keepdims=True)
    grad_scores = (attention * (grad_probs - row_dots) * scale).astype(jnp.bfloat16)
    grad_query = jnp.einsum("gjqk,kgd->qgjd", grad_scores, key, preferred_element_type=jnp.float32)
    grad_key = jnp.einsum("gjqk,qgjd->kgd", grad_scores, query, preferred_element_type=jnp.float32)
    return (grad_query, grad_key, grad_value)


def per_device(
    hidden_in,
    norm1_gain,
    query_weight,
    key_weight,
    value_weight,
    output_weight,
    norm2_gain,
    router_weight,
    gate_weight,
    up_weight,
    down_weight,
    segment_ids,
    expert_ids,
    grad_out,
):
    row_count = lax.axis_size("row")
    local_rows, local_width = hidden_in.shape
    group = expert_ids.shape[0]
    chosen = expert_ids.shape[1]
    width = local_width * row_count
    experts = gate_weight.shape[0]
    hidden_cols = gate_weight.shape[2]
    capacity = group * chosen * 5 // (4 * experts)
    slot_rows = experts * capacity // row_count
    sequences, seq_len = segment_ids.shape
    head_dim = HEAD_DIM
    query_cols = query_weight.shape[1] // row_count
    key_cols = key_weight.shape[1] // row_count
    kv_local = key_cols // head_dim
    ratio = query_cols // key_cols
    cosines, sines = rope_tables(seq_len, head_dim)
    cos_query, sin_query = (cosines[:, None, None, :], sines[:, None, None, :])
    cos_key, sin_key = (cosines[:, None, :], sines[:, None, :])
    residual = hidden_in.astype(jnp.float32)
    normed_one, inv_one = rms_forward(residual, norm1_gain, width)
    gathered_one = token_blocks(normed_one.astype(jnp.bfloat16))
    part_query = jnp.dot(gathered_one, query_weight, preferred_element_type=jnp.float32)
    part_key = jnp.dot(gathered_one, key_weight, preferred_element_type=jnp.float32)
    part_value = jnp.dot(gathered_one, value_weight, preferred_element_type=jnp.float32)
    stacked = jnp.concatenate(
        [
            part_query.reshape(group, row_count, query_cols),
            part_key.reshape(group, row_count, key_cols),
            part_value.reshape(group, row_count, key_cols),
        ],
        2,
    ).reshape(group, -1)
    summed = head_sums(stacked)
    query_raw = summed[:, :query_cols].reshape(sequences, seq_len, kv_local, ratio, head_dim)
    key_raw = summed[:, query_cols : query_cols + key_cols].reshape(
        sequences, seq_len, kv_local, head_dim
    )
    value_low = (
        summed[:, query_cols + key_cols :]
        .reshape(sequences, seq_len, kv_local, head_dim)
        .astype(jnp.bfloat16)
    )
    query_low = rotate(query_raw, cos_query, sin_query).astype(jnp.bfloat16)
    key_low = rotate(key_raw, cos_key, sin_key).astype(jnp.bfloat16)
    attended, log_sums = lax.map(attend_forward, (query_low, key_low, value_low, segment_ids))
    gathered_out = head_gather(attended.reshape(group, query_cols))

    def attn_term(start, count):
        return jnp.dot(gathered_out, output_weight, preferred_element_type=jnp.float32)

    middle = residual + column_sums(attn_term, local_rows)
    normed_two, inv_two = rms_forward(middle, norm2_gain, width)
    gathered_two = token_blocks(normed_two.astype(jnp.bfloat16))
    logits = row_stats(jnp.dot(gathered_two, router_weight, preferred_element_type=jnp.float32))
    member = (expert_ids[:, :, None] == jnp.arange(experts, dtype=jnp.int32)[None, None, :]).astype(
        jnp.float32
    )
    gates = jax.nn.softmax(jnp.sum(member * logits[:, None, :], -1), -1)
    slot_of, owner, filled, token_of = slot_tables(expert_ids, capacity, experts)
    dispatched = jnp.where(
        filled[:, None], gathered_two[token_of], jnp.zeros((), jnp.bfloat16)
    ).reshape(experts, capacity, local_width)
    paired = jnp.concatenate([gate_weight, up_weight], 2)
    gate_up = slot_sums(expert_term(dispatched, paired, "ecd,edh->ech"), slot_rows)
    gate_part = gate_up[:, :hidden_cols]
    up_part = gate_up[:, hidden_cols:]
    sigmoid_gate = jax.nn.sigmoid(gate_part)
    silu_gate = gate_part * sigmoid_gate
    gathered_hidden = slot_gather((silu_gate * up_part).astype(jnp.bfloat16)).reshape(
        experts, capacity, hidden_cols
    )
    expert_out = jnp.einsum(
        "ech,ehd->ecd", gathered_hidden, down_weight, preferred_element_type=jnp.float32
    ).reshape(experts * capacity, local_width)
    routed = column_sums(token_term(expert_out, slot_of, gates), local_rows)
    mixed_out = (middle + routed).astype(jnp.bfloat16)
    grad_tokens = token_blocks(grad_out)
    assigned = group * chosen
    weight_of = jnp.where(filled, gates.reshape(-1)[jnp.minimum(owner, assigned - 1)], 0.0)
    grad_slots = grad_tokens[token_of]
    grad_expert = (
        (grad_slots.astype(jnp.float32) * weight_of[:, None])
        .astype(jnp.bfloat16)
        .reshape(experts, capacity, local_width)
    )
    slot_dots = jnp.sum(grad_slots.astype(jnp.float32) * expert_out, -1)
    grad_gates = lax.psum(slot_dots[slot_of].astype(jnp.bfloat16), ("row", "col")).astype(
        jnp.float32
    )
    grad_select = gates * (grad_gates - jnp.sum(gates * grad_gates, -1, keepdims=True))
    grad_logits = jnp.sum(member * grad_select[:, :, None], 1).astype(jnp.bfloat16)
    grad_router = jnp.einsum(
        "td,te->de", gathered_two, grad_logits, preferred_element_type=jnp.float32
    )
    own_logits = lax.dynamic_slice_in_dim(
        grad_logits, lax.axis_index("col") * local_rows, local_rows, 0
    )
    router_back = jnp.einsum(
        "te,de->td", own_logits, router_weight, preferred_element_type=jnp.float32
    )
    grad_hidden = slot_sums(expert_term(grad_expert, down_weight, "ecd,ehd->ech"), slot_rows)
    grad_down = jnp.einsum(
        "ech,ecd->ehd", gathered_hidden, grad_expert, preferred_element_type=jnp.float32
    )
    grad_pair = jnp.concatenate(
        [
            grad_hidden * up_part * sigmoid_gate * (1.0 + gate_part * (1.0 - sigmoid_gate)),
            grad_hidden * silu_gate,
        ],
        1,
    ).astype(jnp.bfloat16)
    gathered_pair = slot_gather(grad_pair).reshape(experts, capacity, 2 * hidden_cols)
    grad_rows = jnp.einsum(
        "ech,edh->ecd", gathered_pair, paired, preferred_element_type=jnp.float32
    ).reshape(experts * capacity, local_width)
    grad_paired = jnp.einsum(
        "ecd,ech->edh", dispatched, gathered_pair, preferred_element_type=jnp.float32
    )
    grad_two = column_sums(token_term(grad_rows, slot_of, None), local_rows) + router_back
    grad_norm_two, gain_two = norm_back(grad_two, middle, inv_two, norm2_gain, width)
    grad_middle = grad_out.astype(jnp.float32) + grad_norm_two
    grad_mid_tokens = token_blocks(grad_middle.astype(jnp.bfloat16))
    grad_output_w = jnp.einsum(
        "tc,td->cd", gathered_out, grad_mid_tokens, preferred_element_type=jnp.float32
    )
    grad_heads = head_sums(
        jnp.einsum("td,cd->tc", grad_mid_tokens, output_weight, preferred_element_type=jnp.float32)
    )
    grad_attn = grad_heads.astype(jnp.bfloat16).reshape(
        sequences, seq_len, kv_local, ratio, head_dim
    )
    grad_query, grad_key, grad_value = lax.map(
        attend_backward, (query_low, key_low, value_low, segment_ids, log_sums, grad_attn)
    )
    grad_query = (
        rotate_back(grad_query, cos_query, sin_query)
        .astype(jnp.bfloat16)
        .reshape(group, query_cols)
    )
    grad_key = rotate_back(grad_key, cos_key, sin_key).astype(jnp.bfloat16).reshape(group, key_cols)
    grad_value = grad_value.astype(jnp.bfloat16).reshape(group, key_cols)
    gathered_grads = head_gather(jnp.concatenate([grad_query, grad_key, grad_value], 1)).reshape(
        group, row_count, query_cols + 2 * key_cols
    )
    full_query = gathered_grads[:, :, :query_cols].reshape(group, -1)
    full_key = gathered_grads[:, :, query_cols : query_cols + key_cols].reshape(group, -1)
    full_value = gathered_grads[:, :, query_cols + key_cols :].reshape(group, -1)
    grad_query_w = jnp.einsum(
        "td,tc->dc", gathered_one, full_query, preferred_element_type=jnp.float32
    )
    grad_key_w = jnp.einsum("td,tc->dc", gathered_one, full_key, preferred_element_type=jnp.float32)
    grad_value_w = jnp.einsum(
        "td,tc->dc", gathered_one, full_value, preferred_element_type=jnp.float32
    )

    def input_term(start, count):
        total = jnp.einsum(
            "tc,dc->td", full_query, query_weight, preferred_element_type=jnp.float32
        )
        total = total + jnp.einsum(
            "tc,dc->td", full_key, key_weight, preferred_element_type=jnp.float32
        )
        return total + jnp.einsum(
            "tc,dc->td", full_value, value_weight, preferred_element_type=jnp.float32
        )

    grad_one = column_sums(input_term, local_rows)
    grad_norm_one, gain_one = norm_back(grad_one, residual, inv_one, norm1_gain, width)
    grad_in = grad_middle + grad_norm_one
    weight_sums = (
        lax.psum(grad_query_w.astype(jnp.bfloat16), "dp").astype(jnp.float32),
        lax.psum(grad_key_w.astype(jnp.bfloat16), "dp").astype(jnp.float32),
        lax.psum(grad_value_w.astype(jnp.bfloat16), "dp").astype(jnp.float32),
        lax.psum(grad_output_w.astype(jnp.bfloat16), "dp").astype(jnp.float32),
        lax.psum(grad_router.astype(jnp.bfloat16), "dp").astype(jnp.float32),
    )
    expert_sums = (
        lax.psum_scatter(
            grad_paired[:, :, :hidden_cols].astype(jnp.bfloat16),
            "dp",
            scatter_dimension=0,
            tiled=True,
        ).astype(jnp.float32),
        lax.psum_scatter(
            grad_paired[:, :, hidden_cols:].astype(jnp.bfloat16),
            "dp",
            scatter_dimension=0,
            tiled=True,
        ).astype(jnp.float32),
        lax.psum_scatter(
            grad_down.astype(jnp.bfloat16), "dp", scatter_dimension=0, tiled=True
        ).astype(jnp.float32),
    )
    gain_sums = lax.psum((gain_one, gain_two), ("dp", "col"))
    return (
        mixed_out,
        grad_in,
        gain_sums[0],
        weight_sums[0],
        weight_sums[1],
        weight_sums[2],
        weight_sums[3],
        gain_sums[1],
        weight_sums[4],
        expert_sums[0],
        expert_sums[1],
        expert_sums[2],
    )


def solution(mesh):
    return jax.shard_map(
        per_device,
        mesh=mesh,
        in_specs=(
            P(("dp", "col"), "row"),
            P("row"),
            P("row", "col"),
            P("row", "col"),
            P("row", "col"),
            P("col", "row"),
            P("row"),
            P("row", None),
            P(None, "row", "col"),
            P(None, "row", "col"),
            P(None, "col", "row"),
            P("dp", None),
            P("dp", None),
            P(("dp", "col"), "row"),
        ),
        out_specs=(
            P(("dp", "col"), "row"),
            P(("dp", "col"), "row"),
            P("row"),
            P("row", "col"),
            P("row", "col"),
            P("row", "col"),
            P("col", "row"),
            P("row"),
            P("row", None),
            P("dp", "row", "col"),
            P("dp", "row", "col"),
            P("dp", "col", "row"),
        ),
        check_vma=False,
    )
```

profile of v0, /device:TPU:0, one launch (start us, length us, event | category | flops | bytes accessed | tf_op | source)
XLA Modules:
  0.0 3145.1 jit_solution(11832407805937229177)
XLA Ops:
  8.6 13.5 psum.91
  24.8 19.6 all-gather.9.cloned.1.call-done
  51.5 144.2 %reduce-scatter.12.cloned.1.call-done = f32[2048,256]{0,1:T(8,128)} async-done(((f32[2048,1024]{0,1:T(8,128)}), f32[2048,256]{0,1:T(8,128)}) %reduce-scatter.12.cloned.1.call-update) | async-done | bytes 2097168 | tf_op jit(solution)/shard_map/reduce_scatter | solution.py:73
  202.8 18.8 while.26
  232.4 37.4 %all-gather.11.cloned.1.call-done = bf16[2048,512]{0,1:T(8,128)(2,1)} async-done(((bf16[2048,128]{0,1:T(8,128)(2,1)}), bf16[2048,512]{0,1:T(8,128)(2,1)}) %all-gather.11.cloned.1.call-update) | async-done | bytes 2097168 | tf_op jit(solution)/shard_map/all_gather | solution.py:77
  283.0 60.4 %scatter_custom_fusion = s32[20480]{0:T(1024)S(1)} fusion(s32[16384]{0:T(1024)S(1)} %bitcast.320, s32[16384]{0:T(1024)S(1)} %iota.84, s32[]{:T(128)} %constant.108.clone.1), kind=kCustom, calls=%fused_computation.176 | custom fusion | bytes 81924 | tf_op jit(solution)/shard_map/scatter | solution.py:51
  344.9 9.6 psum.92
  363.6 11.9 all-gather.13.cloned.1.call-done
  375.4 77.6 %gather_fusion = bf16[20480,256]{1,0:T(8,128)(2,1)} fusion(bf16[2048,256]{1,0:T(8,128)(2,1)} %all-gather.13.cloned.1.call-done, s32[20480]{0:T(1024)S(1)} %get-tuple-element.201), kind=kCustom, calls=%fused_computation | custom fusion | bytes 21053440 | tf_op jit(solution)/shard_map/gather | solution.py:230
  453.1 14.4 copy.77
  467.4 20.2 fusion.49
  490.0 684.1 %reduce-scatter.16.cloned.1.call-done = f32[5120,512]{1,0:T(8,128)} async-done(((f32[20480,512]{1,0:T(8,128)}), f32[5120,512]{1,0:T(8,128)}) %reduce-scatter.16.cloned.1.call-update) | async-done | bytes 10485776 | tf_op jit(solution)/shard_map/reduce_scatter | solution.py:81
  1181.0 17.4 all-gather.17.cloned.1.call-done
  1198.4 77.7 %gather_fusion.2 = bf16[20480,256]{1,0:T(8,128)(2,1)} fusion(bf16[2048,256]{1,0:T(8,128)(2,1)} %all-gather.17.cloned.1.call-done, s32[20480]{0:T(1024)S(1)} %get-tuple-element.201), kind=kCustom, calls=%fused_computation.2 | custom fusion | bytes 21053440 | tf_op jit(solution)/shard_map/gather | solution.py:249
  1278.2 143.8 %all-gather.15.cloned.1.call-done = bf16[20480,256]{1,0:T(8,128)(2,1)} async-done(((bf16[5120,256]{1,0:T(8,128)(2,1)}), bf16[20480,256]{1,0:T(8,128)(2,1)}) %all-gather.15.cloned.1.call-update) | async-done | bytes 10485776 | tf_op jit(solution)/shard_map/all_gather | solution.py:87
  1422.0 14.0 fusion.45
  1436.1 100.9 %gather_fusion.5 = bf16[16384]{0:T(1024)(128)(2,1)S(1)} fusion(bf16[20480]{0:T(1024)(128)(2,1)S(1)} %reduce_sum.150, s32[16384]{0:T(1024)S(1)} %broadcast_clamp_fusion), kind=kCustom, calls=%fused_computation.5 | custom fusion | bytes 131072 | tf_op jit(solution)/shard_map/gather | solution.py:256
  1537.8 34.3 %psum.94 = bf16[2048,8]{0,1:T(8,128)(2,1)S(1)} all-reduce(bf16[2048,8]{0,1:T(8,128)(2,1)S(1)} %copy.80), channel_id=1, replica_groups=mesh['dp'=4,'row'=4,'col'=2] {'row','col'}, use_global_device_ids=true, to_apply=%region_24.25 | all-reduce | flops 16384 | bytes 65536 | tf_op jit(solution)/shard_map/psum | solution.py:256
  1573.7 113.0 %gather_fusion.3 = f32[20480]{0:T(1024)S(1)} fusion(f32[16384]{0:T(1024)S(1)} %div.94, s32[20480]{0:T(1024)S(1)} %copy-done.32), kind=kCustom, calls=%fused_computation.3 | custom fusion | bytes 245760 | tf_op jit(solution)/shard_map/gather | solution.py:248
  1686.8 12.6 fusion.52
  1699.5 344.5 %reduce-scatter.20.cloned.1.call-done = f32[5120,256]{1,0:T(8,128)} async-done(((f32[20480,256]{1,0:T(8,128)}), f32[5120,256]{1,0:T(8,128)}) %reduce-scatter.20.cloned.1.call-update) | async-done | bytes 5242896 | tf_op jit(solution)/shard_map/reduce_scatter | solution.py:81
  2044.1 6.8 multiply_convert_fusion.1
  2053.9 358.2 %all-gather.19.cloned.1.call-done = bf16[20480,512]{1,0:T(8,128)(2,1)} async-done(((bf16[5120,512]{1,0:T(8,128)(2,1)}), bf16[20480,512]{1,0:T(8,128)(2,1)}) %all-gather.19.cloned.1.call-update) | async-done | bytes 20971536 | tf_op jit(solution)/shard_map/all_gather | solution.py:87
  2412.1 16.7 fusion.107
  2428.8 68.9 %gather_fusion.4 = f32[16384,256]{1,0:T(8,128)} fusion(f32[20480,256]{1,0:T(8,128)} %bitcast.282, s32[16384]{0:T(1024)S(1)} %broadcast_clamp_fusion), kind=kCustom, calls=%fused_computation.4 | custom fusion | bytes 33619968 | tf_op jit(solution)/shard_map/gather | solution.py:116
  2497.8 12.3 bitcast_reduce_fusion
  2510.1 66.6 %gather_fusion.1 = bf16[16384,256]{1,0:T(8,128)(2,1)} fusion(bf16[20480,256]{1,0:T(8,128)(2,1)} %bitcast.283, s32[16384]{0:T(1024)S(1)} %broadcast_clamp_fusion), kind=kCustom, calls=%fused_computation.1 | custom fusion | bytes 16842752 | tf_op jit(solution)/shard_map/gather | solution.py:117
  2577.7 7.0 fusion.46
  2590.2 9.0 psum.95
  2599.2 19.3 reduce-scatter.18.cloned.1.call-done
  2621.6 21.4 all-gather.21.cloned.1.call-done
  2647.3 76.6 %reduce-scatter.24.cloned.1.call-done = f32[2048,128]{1,0:T(8,128)} async-done(((f32[2048,512]{1,0:T(8,128)}), f32[2048,128]{1,0:T(8,128)}) %reduce-scatter.24.cloned.1.call-update) | async-done | bytes 1048592 | tf_op jit(solution)/shard_map/reduce_scatter | solution.py:73
  2727.4 83.1 %while.27 = (s32[]{:T(128)}, f32[4,512,1,2,64]{1,0,4,3,2:T(4,128)}, f32[4,512,1,64]{1,0,3,2:T(4,128)}, bf16[4,512,1,64]{1,3,2,0:T(8,128)(2,1)}, bf16[4,512,1,64]...) while((s32[]{:T(128)}, f32[4,512,1,2,64]{1,0,4,3,2:T(4,128)}, ...), condition=%wide.region_32.33_spmd, body=%wide.region_30.32_spmd.sunk | while | flops 341572608 | bytes 19101828 | solution.py:301
  2735.0 6.1 dynamic_update_slice.30
  2755.7 6.1 dynamic_update_slice.30
  2776.5 6.1 dynamic_update_slice.30
  2797.3 6.1 dynamic_update_slice.30
  2815.2 11.5 fusion.59
  2827.4 17.5 fusion.54
  2854.1 42.4 %all-gather.23.cloned.1.call-done = bf16[2048,1024]{0,1:T(8,128)(2,1)} async-done(((bf16[2048,256]{0,1:T(8,128)(2,1)}), bf16[2048,1024]{0,1:T(8,128)(2,1)}) %all-gather.23.cloned.1.call-update) | async-done | bytes 4194320 | tf_op jit(solution)/shard_map/all_gather | solution.py:77
  2912.3 11.8 psum.103
  2924.6 17.7 reduce-scatter.32.cloned.1.call-done
  2945.0 44.2 %reduce-scatter.28.cloned.1.call-done = bf16[8,256,256]{2,1,0:T(8,128)(2,1)} async-done(((bf16[32,256,256]{2,1,0:T(8,128)(2,1)}), bf16[8,256,256]{2,1,0:T(8,128)(2,1)}) %reduce-scatter.28.cloned.1.call-update) | async-done | bytes 1048592 | tf_op jit(solution)/shard_map/reduce_scatter | solution.py:347
  2991.9 44.5 %reduce-scatter.30.cloned.1.call-done = bf16[8,256,256]{2,1,0:T(8,128)(2,1)} async-done(((bf16[32,256,256]{2,1,0:T(8,128)(2,1)}), bf16[8,256,256]{2,1,0:T(8,128)(2,1)}) %reduce-scatter.30.cloned.1.call-update) | async-done | bytes 1048592 | tf_op jit(solution)/shard_map/reduce_scatter | solution.py:353
  3039.2 35.2 %all-reduce.7.cloned.1.call-done = (bf16[256,512]{1,0:T(8,128)(2,1)}, bf16[256,256]{1,0:T(8,128)(2,1)}, bf16[256,256]{1,0:T(8,128)(2,1)}, bf16[512,256]{1,0:T(8,128)(2,1)}) async-done(((bf16[256,512]{1,0:T(8,128)(2,1)}, bf16[256,256]{1,0:T(8,128)(2,1)}, bf16[256,256]{1,0:T(8,128)(2,1)}, bf16[512,256]{1,0:T(8,128)(2,1)}), (bf16[256,512]{1,0:T(8,128)(2,1)}, bf16[256,256]{1,0:T(8,128)(2,1)}, ...) | async-done | bytes 786448 | tf_op jit(solution)/shard_map/psum | solution.py:340
  3081.2 27.5 reduce-scatter.26.cloned.1.call-done
  3110.5 11.7 psum.96
  3122.2 13.0 all-reduce
  (333 shorter events, 213.6 us)
Async XLA Ops:
  7.2 262.6 %copy-start = (bf16[512,256]{1,0:T(8,128)(2,1)S(1)}, bf16[512,256]{1,0:T(8,128)(2,1)}, u32[]{:S(2)}) copy-start(bf16[512,256]{1,0:T(8,128)(2,1)} %param.23) | copy-start | bytes 786436
  7.2 39.3 %copy-start.27 = (bf16[256,256]{1,0:T(8,128)(2,1)S(1)}, bf16[256,256]{1,0:T(8,128)(2,1)}, u32[]{:S(2)}) copy-start(bf16[256,256]{1,0:T(8,128)(2,1)} %param.21) | copy-start | bytes 393220
  7.2 37.2 %all-gather.9.cloned.1.call-start = ((), (), s32[]{:S(2)}) async-start(), calls=%async_computation.11 | async-start | bytes 1572864 | tf_op jit(solution)/shard_map/all_gather | solution.py:59
  24.7 22.3 copy-start.29
  24.7 171.0 %reduce-scatter.12.cloned.1.call-start = ((), (), s32[]{:S(2)}) async-start(), calls=%async_computation.12 | async-start | bytes 10485760 | tf_op jit(solution)/shard_map/reduce_scatter | solution.py:73
  51.1 218.7 %all-gather.11.cloned.1.call-start = ((), (), s32[]{:S(2)}) async-start(), calls=%async_computation.13 | async-start | bytes 2621440 | tf_op jit(solution)/shard_map/all_gather | solution.py:77
  51.5 148.2 %copy-start.15 = (f32[512,32]{0,1:T(8,128)}, f32[512,32]{0,1:T(8,128)S(1)}, u32[]{:S(2)}) copy-start(f32[512,32]{0,1:T(8,128)S(1)} %get-tuple-element.227) | copy-start | bytes 196612
  51.5 148.2 %copy-start.17 = (f32[512,32]{0,1:T(8,128)}, f32[512,32]{0,1:T(8,128)S(1)}, u32[]{:S(2)}) copy-start(f32[512,32]{0,1:T(8,128)S(1)} %get-tuple-element.228) | copy-start | bytes 196612
  202.8 20.2 copy-start.25
  223.0 120.4 %reduce-scatter.14.cloned.1.call-start = ((), (), s32[]{:S(2)}) async-start(), calls=%async_computation.14 | async-start | bytes 3145728 | tf_op jit(solution)/shard_map/reduce_scatter | solution.py:63
  273.5 101.9 %all-gather.13.cloned.1.call-start = ((), (), s32[]{:S(2)}) async-start(), calls=%async_computation.15 | async-start | bytes 1572864 | tf_op jit(solution)/shard_map/all_gather | solution.py:59
  273.7 69.6 %copy-start.7 = (bf16[1024,256]{1,0:T(8,128)(2,1)S(1)}, bf16[1024,256]{1,0:T(8,128)(2,1)}, u32[]{:S(2)}) copy-start(bf16[1024,256]{1,0:T(8,128)(2,1)} %param.18) | copy-start | bytes 1572868
  278.7 75.7 %copy-start.50 = (f32[256]{0:T(256)S(1)}, f32[256]{0:T(256)}, u32[]{:S(2)}) copy-start(f32[256]{0:T(256)} %param.24) | copy-start | bytes 3076
  344.8 16.4 copy-start.5
  354.4 6.8 copy-start.42
  355.5 818.7 %reduce-scatter.16.cloned.1.call-start = ((), (), s32[]{:S(2)}) async-start(), calls=%async_computation.17 | async-start | bytes 52428800 | tf_op jit(solution)/shard_map/reduce_scatter | solution.py:81
  356.3 111.1 %copy-start.38 = (pred[32,640]{1,0:T(8,128)(4,1)}, pred[32,640]{1,0:T(8,128)(4,1)S(1)}, u32[]{:S(2)}) copy-start(pred[32,640]{1,0:T(8,128)(4,1)S(1)} %broadcast_in_dim.77) | copy-start | bytes 61444
  487.6 710.8 %all-gather.17.cloned.1.call-start = ((), (), s32[]{:S(2)}) async-start(), calls=%async_computation.20 | async-start | bytes 1572864 | tf_op jit(solution)/shard_map/all_gather | solution.py:59
  488.4 787.8 %all-reduce.5.cloned.1.call-start = ((), (), s32[]{:S(2)}) async-start(), calls=%async_computation.16 | async-start | bytes 524288 | tf_op jit(solution)/shard_map/psum | solution.py:69
  490.0 932.0 %all-gather.15.cloned.1.call-start = ((), (), s32[]{:S(2)}) async-start(), calls=%async_computation.18 | async-start | bytes 13107200 | tf_op jit(solution)/shard_map/all_gather | solution.py:87
  1180.1 864.0 %reduce-scatter.20.cloned.1.call-start = ((), (), s32[]{:S(2)}) async-start(), calls=%async_computation.21 | async-start | bytes 26214400 | tf_op jit(solution)/shard_map/reduce_scatter | solution.py:81
  1277.5 158.5 %copy-start.19 = (f32[2048,8]{0,1:T(8,128)}, f32[2048,8]{0,1:T(8,128)S(1)}, u32[]{:S(2)}) copy-start(f32[2048,8]{0,1:T(8,128)S(1)} %select_reduce_fusion.1) | copy-start | bytes 196612
  1277.5 158.5 %copy-start.40 = (f32[2048]{0:T(1024)}, f32[2048]{0:T(1024)S(1)}, u32[]{:S(2)}) copy-start(f32[2048]{0:T(1024)S(1)} %reduce_max.18) | copy-start | bytes 24580
  1436.1 136.1 %copy-start.20 = (f32[2048,8]{0,1:T(8,128)S(1)}, f32[2048,8]{0,1:T(8,128)}, u32[]{:S(2)}) copy-start(f32[2048,8]{0,1:T(8,128)} %copy-done.19) | copy-start | bytes 196612
  1436.1 136.1 %copy-start.41 = (f32[2048]{0:T(1024)S(1)}, f32[2048]{0:T(1024)}, u32[]{:S(2)}) copy-start(f32[2048]{0:T(1024)} %copy-done.40) | copy-start | bytes 24580
  1436.1 136.1 %copy-start.48 = (f32[2048]{0:T(1024)S(1)}, f32[2048]{0:T(1024)}, u32[]{:S(2)}) copy-start(f32[2048]{0:T(1024)} %fusion.91) | copy-start | bytes 24580
  1436.1 137.6 %copy-start.32 = (s32[20480]{0:T(1024)S(1)}, s32[20480]{0:T(1024)}, u32[]{:S(2)}) copy-start(s32[20480]{0:T(1024)} %get-tuple-element.226) | copy-start | bytes 245764
  1573.7 113.1 %copy-start.37 = (pred[20480]{0:T(1024)(128)(4,1)S(1)}, pred[20480]{0:T(1024)(128)(4,1)}, u32[]{:S(2)}) copy-start(pred[20480]{0:T(1024)(128)(4,1)} %copy-done.36) | copy-start | bytes 61444
  1686.8 12.6 copy-start.21
  1699.5 712.6 %all-gather.19.cloned.1.call-start = ((), (), s32[]{:S(2)}) async-start(), calls=%async_computation.22 | async-start | bytes 26214400 | tf_op jit(solution)/shard_map/all_gather | solution.py:87
  2053.7 534.7 %reduce-scatter.22.cloned.1.call-start = ((), (), s32[]{:S(2)}) async-start(), calls=%async_computation.23 | async-start | bytes 3145728 | tf_op jit(solution)/shard_map/reduce_scatter | solution.py:63
  2510.1 108.4 %reduce-scatter.18.cloned.1.call-start = ((), (), s32[]{:S(2)}) async-start(), calls=%async_computation.19 | async-start | bytes 3145728 | tf_op jit(solution)/shard_map/reduce_scatter | solution.py:63
  2584.7 33.7 %copy-start.14 = (bf16[1024,256]{1,0:T(8,128)(2,1)S(1)}, bf16[1024,256]{1,0:T(8,128)(2,1)}, u32[]{:S(2)}) copy-start(bf16[1024,256]{1,0:T(8,128)(2,1)} %param.31) | copy-start | bytes 1572868
  2587.9 55.0 %all-gather.21.cloned.1.call-start = ((), (), s32[]{:S(2)}) async-start(), calls=%async_computation.24 | async-start | bytes 1572864 | tf_op jit(solution)/shard_map/all_gather | solution.py:59
  2588.3 33.2 %copy-start.23 = (bf16[2048,32]{0,1:T(8,128)(2,1)}, bf16[2048,32]{0,1:T(8,128)(2,1)S(1)}, u32[]{:S(2)}) copy-start(bf16[2048,32]{0,1:T(8,128)(2,1)S(1)} %select_reduce_fusion) | copy-start | bytes 393220
  2621.5 102.4 %reduce-scatter.24.cloned.1.call-start = ((), (), s32[]{:S(2)}) async-start(), calls=%async_computation.25 | async-start | bytes 5242880 | tf_op jit(solution)/shard_map/reduce_scatter | solution.py:73
  2647.0 249.6 %all-gather.23.cloned.1.call-start = ((), (), s32[]{:S(2)}) async-start(), calls=%async_computation.26 | async-start | bytes 5242880 | tf_op jit(solution)/shard_map/all_gather | solution.py:77
  2727.4 83.1 %copy-start.16 = (f32[512,32]{0,1:T(8,128)S(1)}, f32[512,32]{0,1:T(8,128)}, u32[]{:S(2)}) copy-start(f32[512,32]{0,1:T(8,128)} %copy-done.15) | copy-start | bytes 196612
  2727.4 83.1 %copy-start.18 = (f32[512,32]{0,1:T(8,128)S(1)}, f32[512,32]{0,1:T(8,128)}, u32[]{:S(2)}) copy-start(f32[512,32]{0,1:T(8,128)} %copy-done.17) | copy-start | bytes 196612
  2815.1 127.2 %reduce-scatter.32.cloned.1.call-start = ((), (), s32[]{:S(2)}) async-start(), calls=%async_computation.30 | async-start | bytes 5242880 | tf_op jit(solution)/shard_map/reduce_scatter | solution.py:359
  2826.7 162.5 %reduce-scatter.28.cloned.1.call-start = ((), (), s32[]{:S(2)}) async-start(), calls=%async_computation.28 | async-start | bytes 5242880 | tf_op jit(solution)/shard_map/reduce_scatter | solution.py:347
  2850.9 185.6 %reduce-scatter.30.cloned.1.call-start = ((), (), s32[]{:S(2)}) async-start(), calls=%async_computation.29 | async-start | bytes 5242880 | tf_op jit(solution)/shard_map/reduce_scatter | solution.py:353
  2851.6 222.7 %all-reduce.7.cloned.1.call-start = ((), (), s32[]{:S(2)}) async-start(), calls=%async_computation.31 | async-start | bytes 1572864 | tf_op jit(solution)/shard_map/psum | solution.py:340
  2907.1 201.6 %reduce-scatter.26.cloned.1.call-start = ((), (), s32[]{:S(2)}) async-start(), calls=%async_computation.27 | async-start | bytes 3145728 | tf_op jit(solution)/shard_map/reduce_scatter | solution.py:63
  2945.0 163.6 %copy-start.8 = (bf16[1024,256]{1,0:T(8,128)(2,1)S(1)}, bf16[1024,256]{1,0:T(8,128)(2,1)}, u32[]{:S(2)}) copy-start(bf16[1024,256]{1,0:T(8,128)(2,1)} %param.18) | copy-start | bytes 1572868
  2945.0 163.6 %copy-start.47 = (f32[1024]{0:T(1024)S(1)}, f32[1024]{0:T(1024)}, u32[]{:S(2)}) copy-start(f32[1024]{0:T(1024)} %copy-done.46) | copy-start | bytes 12292
  2945.0 163.6 %copy-start.52 = (f32[256]{0:T(256)S(1)}, f32[256]{0:T(256)}, u32[]{:S(2)}) copy-start(f32[256]{0:T(256)} %param.19) | copy-start | bytes 3076
  2991.9 143.3 %copy-start.12 = (f32[1024,256]{1,0:T(8,128)S(1)}, f32[1024,256]{1,0:T(8,128)}, u32[]{:S(2)}) copy-start(f32[1024,256]{1,0:T(8,128)} %get-tuple-element.198) | copy-start | bytes 3145732
  (27 other events, 81.5 us)
Sparse Core Ops, SparseCore 0:
  24.8 19.5 all-gather.8
  51.2 144.4 reduce-scatter.11
  223.1 46.6 all-gather.10
  273.6 30.5 reduce-scatter.13
  355.6 19.7 all-gather.12
  487.8 686.3 reduce-scatter.15
  1175.7 22.7 all-gather.16
  1201.3 35.2 all-reduce.4
  1238.3 183.6 all-gather.14
  1699.6 344.4 reduce-scatter.19
  2053.8 358.2 all-gather.18
  2510.2 30.3 reduce-scatter.21
  2588.1 30.3 reduce-scatter.17
  2621.6 21.3 all-gather.20
  2647.1 76.7 reduce-scatter.23
  2815.2 81.2 all-gather.22
  2899.1 43.1 reduce-scatter.31
  2944.7 44.4 reduce-scatter.27
  2991.9 44.5 reduce-scatter.29
  3039.5 34.8 all-reduce.6
  3076.6 32.0 reduce-scatter.25
where the time goes:
time: 3160 us; the launch traced here: 3150 us
  waiting for transfers between devices  2090 us (66%)
  local copies, waits for them, and re-layouts  676 us (21%)
  matrix products  169 us (5%)
  blocking collectives  103 us (3%)
  other arithmetic  87.4 us (3%)
    reduce_scatter x2, waiting for transfers between devices, slot_sums(): lax.psum_scatter(term(jnp.int32(0), rows * lax.axis_size('row')), 'row',...  1030 us
    all_gather x2, waiting for transfers between devices, slot_gather(): return lax.all_gather(piece, 'row', axis=0, tiled=True)  502 us
    reduce_scatter x2, waiting for transfers between devices, head_sums(): lax.psum_scatter(partial_value, 'row', scatter_dimension=1, tiled=True)  221 us
    gather x1, local copies, waits for them, and re-layouts, per_device(): gates.reshape(-1)[jnp.minimum(owner, assigned - 1)]  113 us
    gather x1, local copies, waits for them, and re-layouts, per_device(): slot_dots[slot_of].astype(jnp.bfloat16)  101 us
    gather x2, local copies, waits for them, and re-layouts, per_device(): gathered_two[token_of]  92 us
    all_gather x2, waiting for transfers between devices, head_gather(): return lax.all_gather(piece, 'row', axis=1, tiled=True)  79.8 us
    gather x1, local copies, waits for them, and re-layouts, per_device(): grad_slots = grad_tokens[token_of]  77.7 us
  transfers between devices with their start and end apart: 21, of which 18 were waited for; matrix products, arithmetic and copies ran while one was open for 10% of the time, Pallas kernels for 0%

commit v1 on v0

v1 whole, which is shorter than its diff:
```python
import functools

import jax
import jax.numpy as jnp
from jax import lax
from jax.experimental import pallas as pl
from jax.experimental.pallas import tpu as pltpu
from jax.sharding import PartitionSpec as P

HEAD_DIM = 64
LANES = 128

epsilon = 1e-06
rope_base = 10000.0
masked_score = -1e30

f32 = jnp.float32
bf16 = jnp.bfloat16

BIG = pltpu.CompilerParams(vmem_limit_bytes=56 * 1024 * 1024)


def dot(left, right):
    return lax.dot_general(left, right, (((1,), (0,)), ((), ())), preferred_element_type=f32)


def dot_nt(left, right):
    return lax.dot_general(left, right, (((1,), (1,)), ((), ())), preferred_element_type=f32)


def dot_tn(left, right):
    return lax.dot_general(left, right, (((0,), (0,)), ((), ())), preferred_element_type=f32)


def rope_tables(seq_len):
    midpoint = HEAD_DIM // 2
    frequency = rope_base ** (-2.0 * jnp.arange(midpoint, dtype=f32) / HEAD_DIM)
    angles = jnp.arange(seq_len, dtype=f32)[:, None] * frequency[None, :]
    cosines, sines = jnp.cos(angles), jnp.sin(angles)
    return (
        jnp.tile(cosines, (1, LANES // midpoint)),
        jnp.tile(jnp.concatenate([-sines, sines], 1), (1, LANES // HEAD_DIM)),
    )


def partner(tile):
    lane = lax.broadcasted_iota(jnp.int32, tile.shape, 1)
    half = HEAD_DIM // 2
    return jnp.where(
        (lane % HEAD_DIM) < half,
        pltpu.roll(tile, LANES - half, 1),
        pltpu.roll(tile, half, 1),
    )


def spread_pair(tile):
    tile = tile.astype(f32)
    lane = lax.broadcasted_iota(jnp.int32, tile.shape, 1)
    swapped = pltpu.roll(tile, HEAD_DIM, 1)
    low = lane < HEAD_DIM
    return (
        jnp.where(low, tile, swapped).astype(bf16),
        jnp.where(low, swapped, tile).astype(bf16),
    )


def split_heads(tile):
    lane = lax.broadcasted_iota(jnp.int32, tile.shape, 1)
    low = lane < HEAD_DIM
    zero = jnp.zeros_like(tile)
    return jnp.where(low, tile, zero), jnp.where(low, zero, tile)


def block_mask(seg_col, seg_row, start, rows, keys):
    row = lax.broadcasted_iota(jnp.int32, (rows, keys), 0) + start
    key = lax.broadcasted_iota(jnp.int32, (rows, keys), 1)
    return (key <= row) & (seg_col[start : start + rows, :] == seg_row[:, :keys])


def attend_kernel(
    query_in, key_in, value_in, cos_ref, sin_ref, col_ref, row_ref,
    query_out, key_out, value_out, heads_out, sums_out, *, block
):
    seq_len = query_in.shape[0]
    cosines, sines = cos_ref[...], sin_ref[...]
    key = key_in[...]
    key_low = (key * cosines + partner(key) * sines).astype(bf16)
    key_out[...] = key_low
    value_low = value_in[...].astype(bf16)
    value_out[...] = value_low
    keys, values = spread_pair(key_low), spread_pair(value_low)
    lane = lax.broadcasted_iota(jnp.int32, (block, LANES), 1)
    scale = 1.0 / HEAD_DIM
    for group in range(2):
        cols = slice(group * LANES, (group + 1) * LANES)
        query = query_in[:, cols]
        query_low = (query * cosines + partner(query) * sines).astype(bf16)
        query_out[:, cols] = query_low
        parts = split_heads(query_low)
        value_parts = split_heads(values[group])
        for start in range(0, seq_len, block):
            reach = start + block
            mask = block_mask(col_ref[...], row_ref[...], start, block, reach)
            total = jnp.zeros((block, LANES), f32)
            for head in range(2):
                scores = dot_nt(parts[head][start:reach], keys[group][:reach]) * scale
                scores = jnp.where(mask, scores, masked_score)
                top = jnp.max(scores, -1, keepdims=True)
                powers = jnp.exp(scores - top)
                mass = jnp.sum(powers, -1, keepdims=True)
                attention = (powers / mass).astype(bf16)
                total += dot(attention, value_parts[head][:reach])
                place = group * 2 + head
                sums = jnp.broadcast_to(top + jnp.log(mass), (block, LANES))
                if place == 0:
                    sums_out[start:reach, :] = sums
                else:
                    sums_out[start:reach, :] = jnp.where(
                        lane == place, sums, sums_out[start:reach, :]
                    )
            heads_out[start:reach, cols] = total.astype(bf16)


def attend_forward(raw, tables, seg_col, seg_row, kv_heads, block):
    seq_len = raw.shape[0]
    pairs = kv_heads // 2
    width = pairs * LANES
    spec = lambda cols, at: pl.BlockSpec((seq_len, cols), at)
    return pl.pallas_call(
        functools.partial(attend_kernel, block=block),
        grid=(pairs,),
        in_specs=[
            spec(2 * LANES, lambda i: (0, i)),
            spec(LANES, lambda i: (0, 2 * pairs + i)),
            spec(LANES, lambda i: (0, 3 * pairs + i)),
            spec(LANES, lambda i: (0, 0)),
            spec(LANES, lambda i: (0, 0)),
            pl.BlockSpec((seq_len, 1), lambda i: (0, 0)),
            pl.BlockSpec((1, seq_len), lambda i: (0, 0)),
        ],
        out_specs=[
            spec(2 * LANES, lambda i: (0, i)),
            spec(LANES, lambda i: (0, i)),
            spec(LANES, lambda i: (0, i)),
            spec(2 * LANES, lambda i: (0, i)),
            spec(LANES, lambda i: (0, i)),
        ],
        out_shape=[
            jax.ShapeDtypeStruct((seq_len, 2 * width), bf16),
            jax.ShapeDtypeStruct((seq_len, width), bf16),
            jax.ShapeDtypeStruct((seq_len, width), bf16),
            jax.ShapeDtypeStruct((seq_len, 2 * width), bf16),
            jax.ShapeDtypeStruct((seq_len, width), f32),
        ],
        compiler_params=BIG,
        name="attend_forward",
    )(raw, raw, raw, *tables, seg_col, seg_row)


def attend_back_kernel(
    query_in, key_in, value_in, sums_in, grad_in, cos_ref, sin_ref, col_ref, row_ref,
    query_out, key_out, value_out, key_sum, value_sum, *, block
):
    seq_len = query_in.shape[0]
    keys, values = spread_pair(key_in[...]), spread_pair(value_in[...])
    lane = lax.broadcasted_iota(jnp.int32, (seq_len, LANES), 1)
    low = lane < HEAD_DIM
    scale = 1.0 / HEAD_DIM
    folded = []
    for group in range(2):
        cols = slice(group * LANES, (group + 1) * LANES)
        query_parts = split_heads(query_in[:, cols])
        grad_parts = split_heads(grad_in[:, cols])
        key_parts = split_heads(keys[group])
        key_sum[...] = jnp.zeros_like(key_sum)
        value_sum[...] = jnp.zeros_like(value_sum)
        for start in range(0, seq_len, block):
            reach = start + block
            rows = slice(start, reach)
            mask = block_mask(col_ref[...], row_ref[...], start, block, reach)
            total = jnp.zeros((block, LANES), f32)
            for head in range(2):
                place = group * 2 + head
                query, grad = query_parts[head][rows], grad_parts[head][rows]
                scores = dot_nt(query, keys[group][:reach]) * scale
                powers = jnp.exp(scores - sums_in[rows, place : place + 1])
                attention = jnp.where(mask, powers, 0.0)
                value_sum[:reach, :] += dot_tn(attention.astype(bf16), grad)
                grad_probs = dot_nt(grad, values[group][:reach])
                inner = jnp.sum(grad_probs * attention, -1, keepdims=True)
                grad_scores = (attention * (grad_probs - inner) * scale).astype(bf16)
                key_sum[:reach, :] += dot_tn(grad_scores, query)
                total += dot(grad_scores, key_parts[head][:reach])
            cosines, sines = cos_ref[rows, :], sin_ref[rows, :]
            query_out[rows, cols] = (total * cosines - partner(total) * sines).astype(bf16)
        grad_key, grad_value = key_sum[...], value_sum[...]
        folded.append(
            (
                grad_key + pltpu.roll(grad_key, HEAD_DIM, 1),
                grad_value + pltpu.roll(grad_value, HEAD_DIM, 1),
            )
        )
    grad_key = jnp.where(low, folded[0][0], folded[1][0])
    grad_value = jnp.where(low, folded[0][1], folded[1][1])
    key_out[...] = (grad_key * cos_ref[...] - partner(grad_key) * sin_ref[...]).astype(bf16)
    value_out[...] = grad_value.astype(bf16)


def attend_backward(query, key, value, sums, grad, tables, seg_col, seg_row, block):
    seq_len = query.shape[0]
    width = key.shape[1]
    pairs = width // LANES
    spec = lambda cols, at: pl.BlockSpec((seq_len, cols), at)
    here = lambda i: (0, i)
    first = lambda i: (0, 0)
    return pl.pallas_call(
        functools.partial(attend_back_kernel, block=block),
        grid=(pairs,),
        in_specs=[
            spec(2 * LANES, here),
            spec(LANES, here),
            spec(LANES, here),
            spec(LANES, here),
            spec(2 * LANES, here),
            spec(LANES, first),
            spec(LANES, first),
            pl.BlockSpec((seq_len, 1), first),
            pl.BlockSpec((1, seq_len), first),
        ],
        out_specs=[spec(2 * LANES, here), spec(LANES, here), spec(LANES, here)],
        out_shape=[
            jax.ShapeDtypeStruct((seq_len, 2 * width), bf16),
            jax.ShapeDtypeStruct((seq_len, width), bf16),
            jax.ShapeDtypeStruct((seq_len, width), bf16),
        ],
        scratch_shapes=[pltpu.VMEM((seq_len, LANES), f32), pltpu.VMEM((seq_len, LANES), f32)],
        compiler_params=BIG,
        name="attend_backward",
    )(query, key, value, sums, grad, *tables, seg_col, seg_row)


def dispatch_kernel(place_ref, *refs, capacity):
    out_ref = refs[-1]
    place = place_ref[0]
    slots = lax.broadcasted_iota(jnp.int32, (capacity, place.shape[1]), 0)
    chosen = jnp.where(slots == place, 1.0, 0.0).astype(bf16)
    start = 0
    for ref in refs[:-1]:
        for part in range(ref.shape[0]):
            width = ref.shape[2]
            out_ref[0, :, start : start + width] = dot(chosen, ref[part]).astype(bf16)
            start += width


def dispatch(places, pieces, capacity):
    count, _, tokens = places.shape
    width = sum(piece.shape[0] * piece.shape[2] for piece in pieces)
    return pl.pallas_call(
        functools.partial(dispatch_kernel, capacity=capacity),
        grid=(count,),
        in_specs=[pl.BlockSpec((1, 1, tokens), lambda i: (i, 0, 0))]
        + [pl.BlockSpec(piece.shape, lambda i: (0, 0, 0)) for piece in pieces],
        out_specs=pl.BlockSpec((1, capacity, width), lambda i: (i, 0, 0)),
        out_shape=jax.ShapeDtypeStruct((count, capacity, width), bf16),
        compiler_params=BIG,
        name="dispatch_rows",
    )(places, *pieces)


def picks(place_ref, count, capacity):
    rows = place_ref.shape[0]
    slots = lax.broadcasted_iota(jnp.int32, (rows, capacity), 1)
    return jnp.concatenate(
        [
            jnp.where(slots == place_ref[:, part : part + 1], 1.0, 0.0).astype(bf16)
            for part in range(count)
        ],
        1,
    )


def combine_kernel(place_ref, values_ref, out_ref, *, count, capacity):
    chosen = picks(place_ref, count, capacity)
    out_ref[...] = dot(chosen, values_ref[...]).astype(bf16)


def combine(places, values, capacity, block):
    tokens = places.shape[0]
    slots, width = values.shape
    return pl.pallas_call(
        functools.partial(combine_kernel, count=slots // capacity, capacity=capacity),
        grid=(tokens // block,),
        in_specs=[
            pl.BlockSpec((block, LANES), lambda i: (i, 0)),
            pl.BlockSpec((slots, width), lambda i: (0, 0)),
        ],
        out_specs=pl.BlockSpec((block, width), lambda i: (i, 0)),
        out_shape=jax.ShapeDtypeStruct((tokens, width), bf16),
        compiler_params=BIG,
        name="combine_rows",
    )(places, values)


def combine_add_kernel(own_ref, place_ref, values_ref, add_ref, out_ref, *, count, capacity):
    chosen = picks(place_ref, count, capacity)
    factor = jnp.where(pl.program_id(0) == own_ref[0], 1.0, 0.0)
    total = dot(chosen, values_ref[...]) + add_ref[...] * factor
    parts, _, width = out_ref.shape
    for part in range(parts):
        out_ref[part] = total[:, part * width : (part + 1) * width].astype(bf16)


def combine_add(own, places, values, addition, capacity, parts):
    tokens = places.shape[0]
    slots, width = values.shape
    block = addition.shape[0]
    return pl.pallas_call(
        functools.partial(combine_add_kernel, count=slots // capacity, capacity=capacity),
        grid=(tokens // block,),
        in_specs=[
            pl.BlockSpec(memory_space=pltpu.SMEM),
            pl.BlockSpec((block, LANES), lambda i: (i, 0)),
            pl.BlockSpec((slots, width), lambda i: (0, 0)),
            pl.BlockSpec((block, width), lambda i: (0, 0)),
        ],
        out_specs=pl.BlockSpec((parts, block, width // parts), lambda i: (0, i, 0)),
        out_shape=jax.ShapeDtypeStruct((parts, tokens, width // parts), bf16),
        compiler_params=BIG,
        name="combine_rows_add",
    )(own, places, values, addition)


def expert_kernel(
    slot_ref, grad_ref, up_ref, down_ref, router_ref, pick_ref,
    out_ref, back_ref, grad_up_ref, grad_down_ref,
):
    step = pl.program_id(0)
    width = slot_ref.shape[1]
    hidden_cols = down_ref.shape[0]
    slots = slot_ref[...]
    grads = grad_ref[:, :width].astype(f32)
    member = grad_ref[:, width:].astype(f32) > 0.5
    logits = jnp.where(member, dot(slots, router_ref[...]), masked_score)
    top = jnp.max(logits, -1, keepdims=True)
    powers = jnp.where(member, jnp.exp(logits - top), 0.0)
    mass = jnp.sum(powers, -1, keepdims=True)
    pick = pick_ref[...]
    gate = jnp.sum(powers * pick[0:1, :], -1, keepdims=True) / jnp.maximum(mass, 1e-30)
    both = dot(slots, up_ref[...])
    gate_part, up_part = both[:, :hidden_cols], both[:, hidden_cols:]
    sigmoid = 1.0 / (1.0 + jnp.exp(-gate_part))
    silu = gate_part * sigmoid
    hidden = (silu * up_part).astype(bf16)
    result = dot(hidden, down_ref[...])
    out_ref[...] = (result * gate).astype(bf16)
    dots = jnp.sum(result * grads, -1, keepdims=True)
    dots_high = dots.astype(bf16).astype(f32)
    back_ref[:, width:] = (dots_high * pick[0:1, :] + (dots - dots_high) * pick[1:2, :]).astype(
        bf16
    )
    grad_expert = (grads * gate).astype(bf16)
    grad_hidden = dot_nt(grad_expert, down_ref[...])
    grad_pair = jnp.concatenate(
        [
            grad_hidden * up_part * sigmoid * (1.0 + gate_part * (1.0 - sigmoid)),
            grad_hidden * silu,
        ],
        1,
    ).astype(bf16)
    back_ref[:, :width] = dot_nt(grad_pair, up_ref[...]).astype(bf16)

    @pl.when(step == 0)
    def _():
        grad_up_ref[...] = jnp.zeros_like(grad_up_ref)
        grad_down_ref[...] = jnp.zeros_like(grad_down_ref)

    grad_up_ref[...] += dot_tn(slots, grad_pair)
    grad_down_ref[...] += dot_tn(hidden, grad_expert)


def run_expert(slots, grads, up, down, router, pick, block):
    rows, width = slots.shape
    rest = grads.shape[1]
    hidden_cols = down.shape[0]
    whole = lambda shape: pl.BlockSpec(shape, lambda i: (0, 0))
    return pl.pallas_call(
        expert_kernel,
        grid=(rows // block,),
        in_specs=[
            pl.BlockSpec((block, width), lambda i: (i, 0)),
            pl.BlockSpec((block, rest), lambda i: (i, 0)),
            whole(up.shape),
            whole(down.shape),
            whole(router.shape),
            whole(pick.shape),
        ],
        out_specs=[
            pl.BlockSpec((block, width), lambda i: (i, 0)),
            pl.BlockSpec((block, rest), lambda i: (i, 0)),
            whole((width, 2 * hidden_cols)),
            whole((hidden_cols, width)),
        ],
        out_shape=[
            jax.ShapeDtypeStruct((rows, width), bf16),
            jax.ShapeDtypeStruct((rows, rest), bf16),
            jax.ShapeDtypeStruct((width, 2 * hidden_cols), f32),
            jax.ShapeDtypeStruct((hidden_cols, width), f32),
        ],
        compiler_params=BIG,
        name="expert_pass",
    )(slots, grads, up, down, router, pick)


def norm_back(grad, values, inv_rms, gain):
    scaled = grad * gain
    inner = jnp.mean(scaled * values, -1, keepdims=True)
    grad_gain = jnp.sum(grad * values * inv_rms, 0)
    return (inv_rms * scaled - values * inv_rms * inv_rms * inv_rms * inner, grad_gain)


def inverse_rms(values):
    return lax.rsqrt(jnp.mean(values * values, -1, keepdims=True) + epsilon)


def running_count(member):
    tokens, cols = member.shape
    chunk = LANES
    parts = member.reshape(tokens // chunk, chunk, cols)
    lower = jnp.tril(jnp.ones((chunk, chunk), f32))
    inside = jnp.einsum("ij,bjc->bic", lower, parts, preferred_element_type=f32)
    sums = jnp.sum(parts, 1)
    blocks = tokens // chunk
    before = jnp.sum(
        jnp.where(
            jnp.arange(blocks)[:, None, None] > jnp.arange(blocks)[None, :, None],
            sums[None, :, :],
            0.0,
        ),
        1,
    )
    return (inside + before[:, None, :]).reshape(tokens, cols).astype(jnp.int32)


def per_device(
    hidden_in,
    norm1_gain,
    query_weight,
    key_weight,
    value_weight,
    output_weight,
    norm2_gain,
    router_weight,
    gate_weight,
    up_weight,
    down_weight,
    segment_ids,
    expert_ids,
    grad_out,
):
    dp_count = lax.axis_size("dp")
    row_count = lax.axis_size("row")
    col_count = lax.axis_size("col")
    dp_at, row_at, col_at = (lax.axis_index(name) for name in ("dp", "row", "col"))
    cell = row_at * col_count + col_at
    cells = row_count * col_count
    local_rows, local_width = hidden_in.shape
    group, chosen = expert_ids.shape
    width = local_width * row_count
    experts = gate_weight.shape[0]
    hidden_part = gate_weight.shape[2]
    hidden_cols = hidden_part * col_count
    capacity = group * chosen * 5 // (4 * experts)
    sequences, seq_len = segment_ids.shape
    own_rows = seq_len // col_count
    query_cols, key_cols = query_weight.shape[1], key_weight.shape[1]
    kv_heads = key_cols // HEAD_DIM
    block = seq_len // 2
    spread = experts // cells
    copies = dp_count // spread
    per_dp = experts // dp_count
    assert sequences == row_count and spread * cells == experts and copies * spread == dp_count
    spread_at = dp_at % spread
    if copies == 1:
        near, far = None, None
    else:
        near = [[i * spread + j for j in range(spread)] for i in range(copies)]
        far = [[i * spread + j for i in range(copies)] for j in range(spread)]

    def exchange(rows):
        return lax.all_to_all(rows, "dp", 0, 0, axis_index_groups=near, tiled=True)

    def by_cell(array):
        lead = array.shape[:-1]
        split = array.reshape(lead + (copies, spread, per_dp))
        return jnp.swapaxes(split, -3, -2).reshape(lead + (spread, cells))

    qkv_own = jnp.concatenate([query_weight, key_weight, value_weight], 1)
    qkv_weight = lax.all_gather(qkv_own, "row", axis=0, tiled=True)
    columns = lax.all_gather(hidden_in, "col", axis=0, tiled=True)
    tokens_in = lax.all_to_all(columns, "row", 0, 1, tiled=True)
    gains = lax.all_gather(jnp.stack([norm1_gain, norm2_gain]), "row", axis=1, tiled=True)
    gain_one, gain_two = gains[0][None, :], gains[1][None, :]
    out_weight = lax.all_gather(output_weight, "row", axis=1, tiled=True)
    router = lax.all_gather(router_weight, "row", axis=0, tiled=True)
    router_pad = jnp.pad(router, ((0, 0), (0, LANES - experts)))
    grad_stack = lax.all_gather(grad_out, ("row", "col"), axis=0, tiled=True).reshape(
        row_count, group, local_width
    )

    def own_share(weight):
        split = weight.reshape((copies, spread, per_dp) + weight.shape[1:])
        return lax.dynamic_index_in_dim(split, spread_at, 1, keepdims=False).reshape(
            (cells,) + weight.shape[1:]
        )

    shares = jnp.concatenate(
        [own_share(gate_weight), own_share(up_weight), jnp.swapaxes(own_share(down_weight), 1, 2)],
        2,
    ).reshape(cells * local_width, 3 * hidden_part)
    got = lax.all_to_all(shares, ("row", "col"), 0, 0, tiled=True).reshape(
        row_count, col_count, local_width, 3, hidden_part
    )
    pair_weight = (
        got[:, :, :, :2, :].transpose(0, 2, 3, 1, 4).reshape(width, 2 * hidden_cols)
    )
    down_full = got[:, :, :, 2, :].transpose(1, 3, 0, 2).reshape(hidden_cols, width)

    member = jnp.any(
        expert_ids[:, :, None] == jnp.arange(experts, dtype=jnp.int32)[None, None, :], 1
    )
    mine = lax.dynamic_index_in_dim(
        by_cell(member.astype(f32)), cell, 2, keepdims=False
    )
    places = jnp.where(mine > 0.5, running_count(mine) - 1, -1)
    place_rows = places.T.reshape(spread, 1, group)
    place_cols = jnp.pad(places, ((0, 0), (0, LANES - spread)), constant_values=-1)
    member_pad = jnp.pad(member.astype(bf16), ((0, 0), (0, LANES - experts)))
    my_expert = ((cell // per_dp) * spread + spread_at) * per_dp + cell % per_dp
    lane = jnp.arange(LANES)[None, :]
    pick = jnp.concatenate(
        [
            (lane == my_expert).astype(f32),
            (lane == experts + my_expert).astype(f32),
            jnp.zeros((6, LANES), f32),
        ],
        0,
    )
    grad_slots = exchange(
        dispatch(place_rows, [grad_stack, member_pad[None]], capacity).reshape(
            spread * capacity, width + LANES
        )
    )

    tables = rope_tables(seq_len)
    segments = lax.dynamic_index_in_dim(segment_ids, row_at, 0, keepdims=True)
    seg_col = segments.reshape(seq_len, 1)
    residual = tokens_in.astype(f32)
    inv_one = inverse_rms(residual)
    normed_one = (residual * inv_one * gain_one).astype(bf16)
    raw = dot(normed_one, qkv_weight)
    query_low, key_low, value_low, heads, log_sums = attend_forward(
        raw, tables, seg_col, segments, kv_heads, block
    )
    attended = lax.psum_scatter(
        dot(heads, out_weight).astype(bf16), "col", scatter_dimension=0, tiled=True
    )
    own_start = col_at * own_rows
    middle = lax.dynamic_slice_in_dim(residual, own_start, own_rows, 0) + attended.astype(f32)
    inv_two = inverse_rms(middle)
    normed_two = (middle * inv_two * gain_two).astype(bf16)

    tokens_two = lax.all_gather(normed_two, ("row", "col"), axis=0, tiled=True)
    slots = exchange(
        dispatch(place_rows, [tokens_two[None]], capacity).reshape(spread * capacity, width)
    )
    results, back, grad_pair_w, grad_down_w = run_expert(
        slots, grad_slots, pair_weight, down_full, router_pad, pick, 256
    )
    back_rows = combine(place_cols, exchange(back), capacity, own_rows)
    grad_own = lax.psum_scatter(back_rows, ("row", "col"), scatter_dimension=0, tiled=True).astype(
        f32
    )
    mixed_rows = combine_add(
        cell.reshape(1), place_cols, exchange(results), middle, capacity, row_count
    )
    mixed_out = lax.psum_scatter(
        mixed_rows.reshape(cells * local_rows, local_width),
        ("row", "col"),
        scatter_dimension=0,
        tiled=True,
    )

    pair_split = grad_pair_w.reshape(row_count, local_width, 2, col_count, hidden_part)
    down_split = grad_down_w.reshape(col_count, hidden_part, row_count, local_width)
    grad_shares = jnp.concatenate(
        [
            pair_split.transpose(0, 3, 1, 2, 4).reshape(cells, local_width, 2 * hidden_part),
            down_split.transpose(2, 0, 3, 1).reshape(cells, local_width, hidden_part),
        ],
        2,
    ).astype(bf16)
    grad_got = lax.all_to_all(
        grad_shares.reshape(cells * local_width, 3 * hidden_part), ("row", "col"), 0, 0, tiled=True
    )
    if copies > 1:
        grad_got = lax.psum_scatter(
            grad_got, "dp", scatter_dimension=0, axis_index_groups=far, tiled=True
        )
    grad_got = grad_got.reshape(per_dp, local_width, 3, hidden_part).astype(f32)
    grad_gate, grad_up = grad_got[:, :, 0], grad_got[:, :, 1]
    grad_down = jnp.swapaxes(grad_got[:, :, 2], 1, 2)

    own_member = lax.dynamic_slice_in_dim(member, cell * own_rows, own_rows, 0)
    logits = jnp.where(own_member, dot(normed_two, router), masked_score)
    powers = jnp.where(own_member, jnp.exp(logits - jnp.max(logits, -1, keepdims=True)), 0.0)
    gates = powers / jnp.sum(powers, -1, keepdims=True)
    extra = grad_own[:, width:]
    grad_gates = extra[:, :experts] + extra[:, experts : 2 * experts]
    grad_logits = (
        gates * (grad_gates - jnp.sum(gates * grad_gates, -1, keepdims=True))
    ).astype(bf16)
    grad_router = dot_tn(normed_two, grad_logits)
    grad_two = grad_own[:, :width] + dot_nt(grad_logits, router)
    grad_norm, grad_gain_two = norm_back(grad_two, middle, inv_two, gain_two)
    own_grad = (
        lax.dynamic_slice_in_dim(grad_stack, cell * own_rows, own_rows, 1)
        .transpose(1, 0, 2)
        .reshape(own_rows, width)
    )
    grad_middle = own_grad.astype(f32) + grad_norm

    grad_mid = lax.all_gather(grad_middle.astype(bf16), "col", axis=0, tiled=True)
    grad_out_w = dot_tn(heads, grad_mid).astype(bf16)
    grad_heads = dot_nt(grad_mid, out_weight).astype(bf16)
    grad_qkv = jnp.concatenate(
        attend_backward(
            query_low, key_low, value_low, log_sums, grad_heads, tables, seg_col, segments, block
        ),
        1,
    )
    grad_qkv_w = dot_tn(normed_one, grad_qkv).astype(bf16)
    grad_one = dot_nt(grad_qkv, qkv_weight)
    grad_part, grad_gain_one = norm_back(grad_one, residual, inv_one, gain_one)
    at_own = lax.dynamic_slice_in_dim(grad_part, own_start, own_rows, 0) + grad_middle
    grad_part = lax.dynamic_update_slice_in_dim(grad_part, at_own, own_start, 0)
    grad_cols = lax.all_to_all(grad_part.astype(bf16), "row", 1, 0, tiled=True)
    grad_in = lax.psum_scatter(grad_cols, "col", scatter_dimension=0, tiled=True).astype(f32)

    qkv_sum = lax.psum(
        lax.psum_scatter(grad_qkv_w, "row", scatter_dimension=0, tiled=True), "dp"
    ).astype(f32)
    out_sum = lax.psum(
        lax.psum_scatter(grad_out_w, "row", scatter_dimension=1, tiled=True), "dp"
    ).astype(f32)
    small = lax.psum(
        (grad_gain_one, grad_gain_two, grad_router), ("dp", "row", "col")
    )
    mine_of = lambda array: lax.dynamic_slice_in_dim(array, row_at * local_width, local_width, 0)
    return (
        mixed_out,
        grad_in,
        mine_of(small[0]),
        qkv_sum[:, :query_cols],
        qkv_sum[:, query_cols : query_cols + key_cols],
        qkv_sum[:, query_cols + key_cols :],
        out_sum,
        mine_of(small[1]),
        mine_of(small[2]),
        grad_gate,
        grad_up,
        grad_down,
    )


def solution(mesh):
    return jax.shard_map(
        per_device,
        mesh=mesh,
        in_specs=(
            P(("dp", "col"), "row"),
            P("row"),
            P("row", "col"),
            P("row", "col"),
            P("row", "col"),
            P("col", "row"),
            P("row"),
            P("row", None),
            P(None, "row", "col"),
            P(None, "row", "col"),
            P(None, "col", "row"),
            P("dp", None),
            P("dp", None),
            P(("dp", "col"), "row"),
        ),
        out_specs=(
            P(("dp", "col"), "row"),
            P(("dp", "col"), "row"),
            P("row"),
            P("row", "col"),
            P("row", "col"),
            P("row", "col"),
            P("col", "row"),
            P("row"),
            P("row", None),
            P("dp", "row", "col"),
            P("dp", "row", "col"),
            P("dp", "col", "row"),
        ),
        check_vma=False,
    )
```

time: 3160 us -> 1090 us (0.34)
  waiting for transfers between devices: 2090 us -> 623 us
  local copies, waits for them, and re-layouts: 676 us -> 68.7 us
  matrix products: 169 us -> 22.1 us
  Pallas kernels: 0 us -> 126 us
  other arithmetic: 87.4 us -> 33.2 us
  blocking collectives: 103 us -> 155 us
  starting transfers between devices: 2.12 us -> 34.7 us
    reduce_scatter x11 -> x6, waiting for transfers between devices: 1400 us -> 190 us  [the longest x1 88 us: per_device(): lax.psum_scatter(mixed_rows.reshape(cells * local_rows, local_width), ('r...]
    gather x7 -> x0, local copies, waits for them, and re-layouts: 519 us -> none  [the longest x1 113 us: per_device(): gates.reshape(-1)[jnp.minimum(owner, assigned - 1)]]
    all_gather x8 -> x6, waiting for transfers between devices: 652 us -> 210 us  [the longest x1 93.5 us: per_device(): lax.all_gather(grad_out, ('row', 'col'), axis=0, tiled=True)]
    all_to_all x0 -> x7, waiting for transfers between devices: none -> 215 us  [the longest x4 144 us: exchange(): return lax.all_to_all(rows, 'dp', 0, 0, axis_index_groups=near, tiled=True)]
    dot_general x50 -> x10, matrix products: 169 us -> 22.1 us  [the longest x3 8.76 us: dot(): lax.dot_general(left, right, (((1,), (0,)), ((), ())), preferred_element_...]
    pallas_call x0 -> x7, Pallas kernels: none -> 126 us  [the longest x1 37.6 us: run_expert(): pl.pallas_call(expert_kernel, grid=(rows // block,), in_specs=[pl.BlockSp...]
    psum x7 -> x1, blocking collectives: 103 us -> 37.6 us  [per_device(): lax.psum((grad_gain_one, grad_gain_two, grad_router), ('dp', 'row', 'col'))]
    all_gather x0 -> x2, blocking collectives: none -> 63.7 us  [the longest x1 49.3 us: per_device(): lax.all_gather(jnp.stack([norm1_gain, norm2_gain]), 'row', axis=1, tiled=...]
  transfers between devices with their start and end apart: 21 -> 21, of which waited for: 18 -> 16; matrix products, arithmetic and copies ran while one was open for 10% -> 10% of each run, Pallas kernels for 0% -> 6%
where the time goes in v1:
time: 1090 us; the launch traced here: 1080 us
  waiting for transfers between devices  623 us (57%)
  blocking collectives  155 us (14%)
  Pallas kernels  126 us (12%)
  local copies, waits for them, and re-layouts  68.7 us (6%)
  starting transfers between devices  34.7 us (3%)
  other arithmetic  33.2 us (3%)
  matrix products  22.1 us (2%)
  between operations  16.6 us (2%)
    all_to_all x4, waiting for transfers between devices, exchange(): return lax.all_to_all(rows, 'dp', 0, 0, axis_index_groups=near, tiled=True)  144 us
    all_gather x1, waiting for transfers between devices, per_device(): lax.all_gather(grad_out, ('row', 'col'), axis=0, tiled=True)  93.5 us
    reduce_scatter x1, waiting for transfers between devices, per_device(): lax.psum_scatter(mixed_rows.reshape(cells * local_rows, local_width), ('r...  88 us
    reduce_scatter x1, waiting for transfers between devices, per_device(): lax.psum_scatter(back_rows, ('row', 'col'), scatter_dimension=0, tiled=True)  86.2 us
    all_to_all x1, waiting for transfers between devices, per_device(): lax.all_to_all(grad_shares.reshape(cells * local_width, 3 * hidden_part),...  71.6 us
    all_to_all x1, blocking collectives, per_device(): grad_cols = lax.all_to_all(grad_part.astype(bf16), 'row', 1, 0, tiled=True)  53.8 us
    all_gather x1, waiting for transfers between devices, per_device(): tokens_two = lax.all_gather(normed_two, ('row', 'col'), axis=0, tiled=True)  49.9 us
    all_gather x1, blocking collectives, per_device(): lax.all_gather(jnp.stack([norm1_gain, norm2_gain]), 'row', axis=1, tiled=...  49.3 us
  transfers between devices with their start and end apart: 21, of which 16 were waited for; matrix products, arithmetic and copies ran while one was open for 10% of the time, Pallas kernels for 6%

profile of v1, /device:TPU:0, one launch (start us, length us, event | category | flops | bytes accessed | tf_op | source)
XLA Modules:
  0.0 1079.5 jit_solution(3843259668317100222)
XLA Ops:
  10.8 23.7 %all-gather.7.cloned.1.call-done = bf16[2048,256]{1,0:T(8,128)(2,1)} async-done(((bf16[1024,256]{1,0:T(8,128)(2,1)}), bf16[2048,256]{1,0:T(8,128)(2,1)}) %all-gather.7.cloned.1.call-update) | async-done | bytes 1048592 | tf_op jit(solution)/shard_map/all_gather | solution.py:499
  34.5 4.7 all-to-all-start
  42.9 49.3 %all_gather.25 = f32[2,1024]{1,0:T(2,128)S(1)} all-gather(f32[2,256]{1,0:T(2,128)S(1)} %pad_maximum_fusion.4), channel_id=1, replica_groups=mesh['dp'=4,'row'=4,'col'=2] {'row'}, dimensions={1}, use_global_device_ids=true | all-gather | bytes 10240 | tf_op jit(solution)/shard_map/all_gather | solution.py:501
  93.5 5.7 all-gather.9.cloned.1.call-done
  99.3 4.3 fusion.19.query_in.key_in.value_in
  103.5 10.1 attend_forward.1
  113.6 16.3 %all-gather.11.cloned.1.call-done = bf16[512,1024]{1,0:T(8,128)(2,1)} async-done(((bf16[512,256]{1,0:T(8,128)(2,1)}), bf16[512,1024]{1,0:T(8,128)(2,1)}) %all-gather.11.cloned.1.call-update) | async-done | bytes 1048592 | tf_op jit(solution)/shard_map/all_gather | solution.py:503
  129.9 3.1 convolution_convert_fusion.2
  139.9 4.5 all-to-all-start.3
  144.4 14.1 %reduce-scatter.7.cloned.1.call-done = bf16[256,1024]{1,0:T(8,128)(2,1)} async-done(((bf16[512,1024]{1,0:T(8,128)(2,1)}), bf16[256,1024]{1,0:T(8,128)(2,1)}) %reduce-scatter.7.cloned.1.call-update) | async-done | bytes 524304 | tf_op jit(solution)/shard_map/reduce_scatter | solution.py:564
  166.1 2.6 bitcast_select_fusion
  171.9 93.5 %all-gather.15.cloned.1.call-done = bf16[8192,256]{1,0:T(8,128)(2,1)} async-done(((bf16[1024,256]{1,0:T(8,128)(2,1)}), bf16[8192,256]{1,0:T(8,128)(2,1)}) %all-gather.15.cloned.1.call-update) | async-done | bytes 4194320 | tf_op jit(solution)/shard_map/all_gather | solution.py:506
  265.3 17.7 %dispatch_rows.3 = bf16[4,640,1152]{2,1,0:T(8,128)(2,1)} custom-call(s32[4,1,2048]{2,1,0:T(1,128)} %copy.148.place_ref, bf16[4,2048,256]{2,1,0:T(8,128)(2,1)} %bitcast.120, bf16[1,2048,128]{2,1,0:T(8,128)(2,1)} %fusion.5.refs_1_), custom_call_target="tpu_custom_call" | custom-call | tf_op jit(solution)/shard_map/dispatch_rows/pallas_call | solution.py:258
  283.0 5.4 all-to-all-start.2
  288.4 49.9 %all-gather.13.cloned.1.call-done = bf16[2048,1024]{1,0:T(8,128)(2,1)} async-done(((bf16[256,1024]{1,0:T(8,128)(2,1)}), bf16[2048,1024]{1,0:T(8,128)(2,1)}) %all-gather.13.cloned.1.call-update) | async-done | bytes 4194320 | tf_op jit(solution)/shard_map/all_gather | solution.py:572
  338.3 14.8 %dispatch_rows.2 = bf16[4,640,1024]{2,1,0:T(8,128)(2,1)} custom-call(s32[4,1,2048]{2,1,0:T(1,128)} %copy.148.place_ref, bf16[1,2048,1024]{2,1,0:T(8,128)(2,1)} %bitcast.125), custom_call_target="tpu_custom_call" | custom-call | tf_op jit(solution)/shard_map/dispatch_rows/pallas_call | solution.py:258
  354.8 5.1 all-to-all-start.1
  360.2 14.5 %all_gather.30 = bf16[1024,32]{1,0:T(8,128)(2,1)S(1)} all-gather(bf16[256,32]{1,0:T(8,128)(2,1)S(1)} %copy.155), channel_id=1, replica_groups=mesh['dp'=4,'row'=4,'col'=2] {'row'}, dimensions={0}, use_global_device_ids=true | all-gather | bytes 81920 | tf_op jit(solution)/shard_map/all_gather | solution.py:504
  376.1 4.7 copy.152
  380.8 3.1 slice_bitcast_fusion.1
  383.9 6.2 copy.153
  390.0 4.4 reshape.257.up_ref
  397.8 21.6 %all-to-all-done.1 = bf16[4,640,1024]{2,1,0:T(8,128)(2,1)} async-done(((bf16[4,640,1024]{2,1,0:T(8,128)(2,1)}), bf16[4,640,1024]{2,1,0:T(8,128)(2,1)}, u32[]{:S(2)}, u32[]{:S(2)}) %all-to-all-start.1) | async-done | bytes 5242912 | tf_op jit(solution)/shard_map/all_to_all | solution.py:490
  419.4 37.6 %expert_pass.1 = (bf16[2560,1024]{1,0:T(8,128)(2,1)}, bf16[2560,1152]{1,0:T(8,128)(2,1)}, f32[1024,1024]{1,0:T(8,128)}, f32[512,1024]{1,0:T(8,128)}) custom-call(bf16[2560,1024]{1,0:T(8,128)(2,1)} %bitcast.19.slot_ref, bf16[2560,1152]{1,0:T(8,128)(2,1)} %bitcast.23.grad_ref, bf16[1024,1024]{1,0:T(8,128)(2,1)} %reshape.257.up_ref, ...), custom_call_target="tpu_custom_call" | custom-call | tf_op jit(solution)/shard_map/expert_pass/pallas_call | solution.py:386
  457.0 5.2 all-to-all-start.5
  464.5 64.2 %all-to-all-done.5 = bf16[4,640,1152]{2,1,0:T(8,128)(2,1)} async-done(((bf16[4,640,1152]{2,1,0:T(8,128)(2,1)}), bf16[4,640,1152]{2,1,0:T(8,128)(2,1)}, u32[]{:S(2)}, u32[]{:S(2)}) %all-to-all-start.5) | async-done | bytes 5898272 | tf_op jit(solution)/shard_map/all_to_all | solution.py:490
  528.7 18.9 %combine_rows.1 = bf16[2048,1152]{1,0:T(8,128)(2,1)} custom-call(s32[2048,128]{1,0:T(8,128)} %pad.13.place_ref, bf16[2560,1152]{1,0:T(8,128)(2,1)} %bitcast.40.values_ref), custom_call_target="tpu_custom_call" | custom-call | tf_op jit(solution)/shard_map/combine_rows/pallas_call | solution.py:290
  553.0 86.2 %reduce-scatter.11.cloned.1.call-done = bf16[256,1152]{1,0:T(8,128)(2,1)} async-done(((bf16[2048,1152]{1,0:T(8,128)(2,1)}), bf16[256,1152]{1,0:T(8,128)(2,1)}) %reduce-scatter.11.cloned.1.call-update) | async-done | bytes 589840 | tf_op jit(solution)/shard_map/reduce_scatter | solution.py:580
  644.9 20.8 %all-gather.17.cloned.1.call-done = bf16[512,1024]{1,0:T(8,128)(2,1)} async-done(((bf16[256,1024]{1,0:T(8,128)(2,1)}), bf16[512,1024]{1,0:T(8,128)(2,1)}) %all-gather.17.cloned.1.call-update) | async-done | bytes 1048592 | tf_op jit(solution)/shard_map/all_gather | solution.py:632
  665.7 3.1 convolution_convert_fusion.1
  668.9 2.8 convolution_convert_fusion.3.grad_in
  671.6 10.6 attend_backward.1
  685.4 2.7 convolution_convert_fusion
  688.1 3.2 multiply_reduce_fusion
  693.0 53.8 %all_to_all.82 = bf16[512,4,256]{2,0,1:T(8,128)(2,1)} all-to-all(bf16[512,4,256]{2,0,1:T(8,128)(2,1)S(1)} %bitcast.128), channel_id=1, replica_groups=mesh['dp'=4,'row'=4,'col'=2] {'row'}, dimensions={1} | all-to-all | bytes 2097152 | tf_op jit(solution)/shard_map/all_to_all | solution.py:646
  746.8 5.2 all-to-all-start.4
  755.9 56.1 %all-to-all-done.4 = bf16[4,640,1024]{2,1,0:T(8,128)(2,1)} async-done(((bf16[4,640,1024]{2,1,0:T(8,128)(2,1)}), bf16[4,640,1024]{2,1,0:T(8,128)(2,1)}, u32[]{:S(2)}, u32[]{:S(2)}) %all-to-all-start.4) | async-done | bytes 5242912 | tf_op jit(solution)/shard_map/all_to_all | solution.py:490
  812.0 16.4 %combine_rows_add.1 = bf16[4,2048,256]{2,1,0:T(8,128)(2,1)} custom-call(s32[1]{0:T(128)} %bitcast.own_ref, s32[2048,128]{1,0:T(8,128)} %pad.13.place_ref, bf16[2560,1024]{1,0:T(8,128)(2,1)} %bitcast.36.values_ref, f32[256,1024]{1,0:T(8,128)} %copy-done.2), custom_call_target="tpu_custom_call" | custom-call | tf_op jit(solution)/shard_map/combine_rows_add/pallas_call | solution.py:317
  833.6 2.8 reshape.260
  836.3 4.7 copy.163
  842.9 3.7 all-to-all-start.7
  846.5 71.6 %all-to-all-done.7 = bf16[8,256,768]{1,2,0:T(8,128)(2,1)S(1)} async-done(((bf16[8,256,768]{1,2,0:T(8,128)(2,1)}), bf16[8,256,768]{1,2,0:T(8,128)(2,1)S(1)}, u32[]{:S(2)}, u32[]{:S(2)}) %all-to-all-start.7) | async-done | bytes 3145760 | tf_op jit(solution)/shard_map/all_to_all | solution.py:602
  918.1 3.4 convert.22
  923.9 3.0 copy.167
  928.8 3.0 slice_bitcast_fusion
  933.2 37.6 %all-reduce.3 = (f32[1024]{0:T(1024)S(1)}, f32[1024]{0:T(1024)S(1)}) all-reduce(f32[1024]{0:T(1024)S(1)} %get-tuple-element.36, f32[1024]{0:T(1024)S(1)} %get-tuple-element.38), channel_id=1, replica_groups=mesh['dp'=4,'row'=4,'col'=2] {'dp','row','col'}, use_global_device_ids=true, to_apply=%region_15.16 | all-reduce | flops 2048 | bytes 16384 | tf_op jit(solution)/shard_map/psum | solution.py:655
  974.2 5.0 all-reduce.10.cloned.1.call-done
  983.7 88.0 %reduce-scatter.9.cloned.1.call-done = bf16[1024,256]{1,0:T(8,128)(2,1)} async-done(((bf16[8192,256]{1,0:T(8,128)(2,1)}), bf16[1024,256]{1,0:T(8,128)(2,1)}) %reduce-scatter.9.cloned.1.call-update) | async-done | bytes 524304 | tf_op jit(solution)/shard_map/reduce_scatter | solution.py:586
  (154 shorter events, 74.3 us)
Async XLA Ops:
  8.0 32.3 %copy-start = (s32[4,512]{1,0:T(4,128)S(1)}, s32[4,512]{1,0:T(4,128)}, u32[]{:S(2)}) copy-start(s32[4,512]{1,0:T(4,128)} %param.25) | copy-start | bytes 24580
  8.0 26.4 %all-gather.7.cloned.1.call-start = ((), (), s32[]{:S(2)}) async-start(), calls=%async_computation.14 | async-start | bytes 1572864 | tf_op jit(solution)/shard_map/all_gather | solution.py:499
  8.8 90.5 %all-gather.9.cloned.1.call-start = ((), (), s32[]{:S(2)}) async-start(), calls=%async_computation.15 | async-start | bytes 2621440 | tf_op jit(solution)/shard_map/all_gather | solution.py:498
  34.4 8.5 copy-start.17
  34.5 8.5 copy-start.18
  34.5 58.4 %all-to-all-start = ((bf16[4,512,256]{2,1,0:T(8,128)(2,1)}), bf16[4,512,256]{2,1,0:T(8,128)(2,1)S(1)}, u32[]{:S(2)}, u32[]{:S(2)}) async-start(bf16[4,512,256]{2,1,0:T(8,128)(2,1)} %bitcast.135), calls=%async_computation | async-start | bytes 2097152 | tf_op jit(solution)/shard_map/all_to_all | solution.py:500
  39.2 90.7 %all-gather.11.cloned.1.call-start = ((), (), s32[]{:S(2)}) async-start(), calls=%async_computation.16 | async-start | bytes 1310720 | tf_op jit(solution)/shard_map/all_gather | solution.py:503
  39.9 118.7 %reduce-scatter.7.cloned.1.call-start = ((), (), s32[]{:S(2)}) async-start(), calls=%async_computation.17 | async-start | bytes 1572864 | tf_op jit(solution)/shard_map/reduce_scatter | solution.py:564
  93.5 10.0 copy-start.15
  133.0 132.3 %all-gather.15.cloned.1.call-start = ((), (), s32[]{:S(2)}) async-start(), calls=%async_computation.19 | async-start | bytes 4718592 | tf_op jit(solution)/shard_map/all_gather | solution.py:506
  136.2 1.9 copy-start.7
  139.9 143.1 %all-to-all-start.3 = ((bf16[8,256,768]{2,1,0:T(8,128)(2,1)}), bf16[8,256,768]{2,1,0:T(8,128)(2,1)}, u32[]{:S(2)}, u32[]{:S(2)}) async-start(bf16[8,256,768]{2,1,0:T(8,128)(2,1)} %pad_maximum_fusion), calls=%async_computation.4 | async-start | bytes 6291456 | tf_op jit(solution)/shard_map/all_to_all | solution.py:520
  144.3 193.9 %all-gather.13.cloned.1.call-start = ((), (), s32[]{:S(2)}) async-start(), calls=%async_computation.18 | async-start | bytes 4718592 | tf_op jit(solution)/shard_map/all_gather | solution.py:572
  144.4 16.6 %copy-start.13 = (s32[2048,8]{0,1:T(8,128)S(1)}, s32[2048,8]{0,1:T(8,128)}, u32[]{:S(2)}) copy-start(s32[2048,8]{0,1:T(8,128)} %param.26) | copy-start | bytes 196612
  159.8 483.2 %copy-start.2 = (f32[256,1024]{1,0:T(8,128)}, f32[256,1024]{1,0:T(8,128)S(1)}, u32[]{:S(2)}) copy-start(f32[256,1024]{1,0:T(8,128)S(1)} %get-tuple-element.47.add_ref) | copy-start | bytes 3145732
  161.6 9.3 copy-start.10
  283.0 71.9 %all-to-all-start.2 = ((bf16[4,640,1152]{2,1,0:T(8,128)(2,1)}), bf16[4,640,1152]{2,1,0:T(8,128)(2,1)}, u32[]{:S(2)}, u32[]{:S(2)}) async-start(bf16[4,640,1152]{2,1,0:T(8,128)(2,1)} %dispatch_rows.3), calls=%async_computation.3 | async-start | bytes 11796480 | tf_op jit(solution)/shard_map/all_to_all | solution.py:490
  353.1 6.9 copy-start.14
  354.8 64.5 %all-to-all-start.1 = ((bf16[4,640,1024]{2,1,0:T(8,128)(2,1)}), bf16[4,640,1024]{2,1,0:T(8,128)(2,1)}, u32[]{:S(2)}, u32[]{:S(2)}) async-start(bf16[4,640,1024]{2,1,0:T(8,128)(2,1)} %dispatch_rows.2), calls=%async_computation.2 | async-start | bytes 10485760 | tf_op jit(solution)/shard_map/all_to_all | solution.py:490
  457.0 71.7 %all-to-all-start.5 = ((bf16[4,640,1152]{2,1,0:T(8,128)(2,1)}), bf16[4,640,1152]{2,1,0:T(8,128)(2,1)}, u32[]{:S(2)}, u32[]{:S(2)}) async-start(bf16[4,640,1152]{2,1,0:T(8,128)(2,1)} %bitcast.119), calls=%async_computation.7 | async-start | bytes 11796480 | tf_op jit(solution)/shard_map/all_to_all | solution.py:490
  462.2 177.0 %reduce-scatter.11.cloned.1.call-start = ((), (), s32[]{:S(2)}) async-start(), calls=%async_computation.21 | async-start | bytes 5308416 | tf_op jit(solution)/shard_map/reduce_scatter | solution.py:580
  547.6 118.1 %all-gather.17.cloned.1.call-start = ((), (), s32[]{:S(2)}) async-start(), calls=%async_computation.22 | async-start | bytes 1572864 | tf_op jit(solution)/shard_map/all_gather | solution.py:632
  641.3 1.7 copy-start.6
  642.4 0.6 copy-start.11
  644.6 24.3 %copy-start.19 = (bf16[512,1024]{1,0:T(8,128)(2,1)S(1)}, bf16[512,1024]{1,0:T(8,128)(2,1)}, u32[]{:S(2)}) copy-start(bf16[512,1024]{1,0:T(8,128)(2,1)} %all-gather.11.cloned.1.call-done) | copy-start | bytes 3145732
  644.6 109.2 %reduce-scatter.17.cloned.1.call-start = ((), (), s32[]{:S(2)}) async-start(), calls=%async_computation.25 | async-start | bytes 1310720 | tf_op jit(solution)/shard_map/reduce_scatter | solution.py:653
  668.8 86.7 %reduce-scatter.15.cloned.1.call-start = ((), (), s32[]{:S(2)}) async-start(), calls=%async_computation.24 | async-start | bytes 2621440 | tf_op jit(solution)/shard_map/reduce_scatter | solution.py:650
  671.6 13.7 %copy-start.16 = (f32[512]{0:T(512)S(1)}, f32[512]{0:T(512)}, u32[]{:S(2)}) copy-start(f32[512]{0:T(512)} %copy-done.15) | copy-start | bytes 6148
  691.3 1.2 copy-start.5
  746.8 5.3 copy-start.3
  746.8 5.3 copy-start.12
  746.8 65.1 %all-to-all-start.4 = ((bf16[4,640,1024]{2,1,0:T(8,128)(2,1)}), bf16[4,640,1024]{2,1,0:T(8,128)(2,1)}, u32[]{:S(2)}, u32[]{:S(2)}) async-start(bf16[4,640,1024]{2,1,0:T(8,128)(2,1)} %bitcast.122), calls=%async_computation.5 | async-start | bytes 10485760 | tf_op jit(solution)/shard_map/all_to_all | solution.py:490
  752.0 179.8 %all-reduce.8.cloned.1.call-start = ((), (), s32[]{:S(2)}) async-start(), calls=%async_computation.26 | async-start | bytes 262144 | tf_op jit(solution)/shard_map/psum | solution.py:655
  753.0 219.1 %reduce-scatter.13.cloned.1.call-start = ((), (), s32[]{:S(2)}) async-start(), calls=%async_computation.23 | async-start | bytes 1572864 | tf_op jit(solution)/shard_map/reduce_scatter | solution.py:647
  753.8 225.4 %all-reduce.10.cloned.1.call-start = ((), (), s32[]{:S(2)}) async-start(), calls=%async_computation.27 | async-start | bytes 1572864 | tf_op jit(solution)/shard_map/psum | solution.py:649
  755.6 316.1 %reduce-scatter.9.cloned.1.call-start = ((), (), s32[]{:S(2)}) async-start(), calls=%async_computation.20 | async-start | bytes 4718592 | tf_op jit(solution)/shard_map/reduce_scatter | solution.py:586
  828.3 1.6 copy-start.8
  842.9 75.2 %all-to-all-start.7 = ((bf16[8,256,768]{1,2,0:T(8,128)(2,1)}), bf16[8,256,768]{1,2,0:T(8,128)(2,1)S(1)}, u32[]{:S(2)}, u32[]{:S(2)}) async-start(bf16[8,256,768]{1,2,0:T(8,128)(2,1)} %pad_maximum_fusion.1), calls=%async_computation.13 | async-start | bytes 6291456 | tf_op jit(solution)/shard_map/all_to_all | solution.py:602
  923.9 3.0 copy-start.4
  971.5 100.2 %copy-start.1 = (s32[4,512]{1,0:T(4,128)S(1)}, s32[4,512]{1,0:T(4,128)}, u32[]{:S(2)}) copy-start(s32[4,512]{1,0:T(4,128)} %param.25) | copy-start | bytes 24580
  979.2 3.6 copy-start.9
Sparse Core Ops, SparseCore 0:
  10.4 23.9 all-gather.6
  36.6 62.6 all-gather.8
  100.8 29.0 all-gather.10
  133.1 25.4 reduce-scatter.6
  644.7 20.9 all-gather.16
  668.9 27.1 reduce-scatter.16
  699.0 56.5 reduce-scatter.14
  762.6 157.5 all-reduce.7
  922.5 19.4 reduce-scatter.12
  944.4 34.7 all-reduce.9
  983.4 88.2 reduce-scatter.8
Sparse Core Ops, SparseCore 1:
  135.8 129.5 all-gather.14
  267.5 70.7 all-gather.12
  547.7 91.4 reduce-scatter.10

commit v2 on v1

--- a/solution.py
+++ b/solution.py
@@ -239,104 +239,231 @@
     )(query, key, value, sums, grad, *tables, seg_col, seg_row)
 
 
-def dispatch_kernel(place_ref, *refs, capacity):
-    out_ref = refs[-1]
-    place = place_ref[0]
-    slots = lax.broadcasted_iota(jnp.int32, (capacity, place.shape[1]), 0)
-    chosen = jnp.where(slots == place, 1.0, 0.0).astype(bf16)
-    start = 0
-    for ref in refs[:-1]:
-        for part in range(ref.shape[0]):
-            width = ref.shape[2]
-            out_ref[0, :, start : start + width] = dot(chosen, ref[part]).astype(bf16)
-            start += width
-
-
-def dispatch(places, pieces, capacity):
+def place_rows_of(place_ref, starts_ref, which, tokens, window, capacity):
+    start = starts_ref[which]
+    start = pl.multiple_of(jnp.minimum(start - start % 16, capacity - window), 16)
+    slots = lax.broadcasted_iota(jnp.int32, (window, tokens), 0) + start
+    return start, jnp.where(slots == place_ref, 1.0, 0.0).astype(bf16)
+
+
+def store_at(step, refs, value):
+    for index, ref in enumerate(refs):
+
+        @pl.when(step == index)
+        def _():
+            ref[...] = value
+
+
+def dispatch_two_kernel(starts_ref, place_ref, *refs, count):
+    blocks, out_refs, total = refs[: -1 - count], refs[-1 - count : -1], refs[-1]
+    tokens = blocks[0].shape[0]
+    capacity = total.shape[0]
+    window = tokens + 16
+    expert = pl.program_id(0)
+    total[...] = jnp.zeros_like(total)
+    for index, block in enumerate(blocks):
+        start, chosen = place_rows_of(
+            place_ref[0, :, index * tokens : (index + 1) * tokens],
+            starts_ref,
+            expert * len(blocks) + index,
+            tokens,
+            window,
+            capacity,
+        )
+        total[pl.ds(start, window), :] += dot(chosen, block[...])
+    store_at(expert, out_refs, total[...].astype(bf16))
+
+
+def dispatch_grads_kernel(starts_ref, place_ref, stack_ref, member_ref, *refs, block):
+    *out_refs, total = refs
+    parts, tokens, width = stack_ref.shape
+    capacity = total.shape[0]
+    window = block + 16
+    expert = pl.program_id(0)
+    total[...] = jnp.zeros_like(total)
+    steps = tokens // block
+    for step in range(steps):
+        rows = slice(step * block, (step + 1) * block)
+        start, chosen = place_rows_of(
+            place_ref[0, :, rows], starts_ref, expert * steps + step, block, window, capacity
+        )
+        values = jnp.concatenate(
+            [stack_ref[part, rows, :] for part in range(parts)] + [member_ref[rows, :]], 1
+        )
+        total[pl.ds(start, window), :] += dot(chosen, values)
+    store_at(expert, out_refs, total[...].astype(bf16))
+
+
+def dispatch(kernel, name, starts, places, arrays, capacity, width):
     count, _, tokens = places.shape
-    width = sum(piece.shape[0] * piece.shape[2] for piece in pieces)
+    whole = lambda array: pl.BlockSpec(array.shape, lambda i: (0,) * array.ndim)
     return pl.pallas_call(
-        functools.partial(dispatch_kernel, capacity=capacity),
+        kernel,
         grid=(count,),
-        in_specs=[pl.BlockSpec((1, 1, tokens), lambda i: (i, 0, 0))]
-        + [pl.BlockSpec(piece.shape, lambda i: (0, 0, 0)) for piece in pieces],
-        out_specs=pl.BlockSpec((1, capacity, width), lambda i: (i, 0, 0)),
-        out_shape=jax.ShapeDtypeStruct((count, capacity, width), bf16),
+        in_specs=[
+            pl.BlockSpec(memory_space=pltpu.SMEM),
+            pl.BlockSpec((1, 1, tokens), lambda i: (i, 0, 0)),
+        ]
+        + [whole(array) for array in arrays],
+        out_specs=[pl.BlockSpec((capacity, width), lambda i: (0, 0))] * count,
+        out_shape=[jax.ShapeDtypeStruct((capacity, width), bf16)] * count,
+        scratch_shapes=[pltpu.VMEM((capacity, width), f32)],
         compiler_params=BIG,
-        name="dispatch_rows",
-    )(places, *pieces)
-
-
-def picks(place_ref, count, capacity):
-    rows = place_ref.shape[0]
-    slots = lax.broadcasted_iota(jnp.int32, (rows, capacity), 1)
-    return jnp.concatenate(
-        [
-            jnp.where(slots == place_ref[:, part : part + 1], 1.0, 0.0).astype(bf16)
-            for part in range(count)
+        name=name,
+    )(starts, places, *arrays)
+
+
+def dispatch_two(starts, places, blocks, capacity):
+    count = places.shape[0]
+    kernel = functools.partial(dispatch_two_kernel, count=count)
+    width = blocks[0].shape[1]
+    return dispatch(kernel, "dispatch_tokens", starts, places, blocks, capacity, width)
+
+
+def dispatch_grads(starts, places, stack, members, capacity, block):
+    kernel = functools.partial(dispatch_grads_kernel, block=block)
+    width = stack.shape[0] * stack.shape[2] + LANES
+    return dispatch(
+        kernel, "dispatch_grads", starts, places, [stack, members], capacity, width
+    )
+
+
+def gather_back(starts_ref, place_ref, value_refs, which, capacity):
+    tokens = place_ref.shape[0]
+    window = 2 * tokens
+    count = len(value_refs)
+    total = None
+    for expert, values_ref in enumerate(value_refs):
+        start = starts_ref[which * count + expert]
+        start = pl.multiple_of(jnp.minimum(start - start % 16, capacity - window), 16)
+        slots = lax.broadcasted_iota(jnp.int32, (tokens, window), 1) + start
+        chosen = jnp.where(slots == place_ref[:, expert : expert + 1], 1.0, 0.0).astype(bf16)
+        term = dot(chosen, values_ref[pl.ds(start, window), :])
+        total = term if total is None else total + term
+    return total
+
+
+def combine_kernel(starts_ref, place_ref, *refs, capacity):
+    *value_refs, own_ref, away_ref = refs
+    step = pl.program_id(0)
+    half = pl.num_programs(0) // 2
+    pieces = place_ref.shape[0] // LANES
+    for piece in range(pieces):
+        rows = slice(piece * LANES, (piece + 1) * LANES)
+        total = gather_back(
+            starts_ref, place_ref[rows, :], value_refs, step * pieces + piece, capacity
+        ).astype(bf16)
+
+        @pl.when(step < half)
+        def _():
+            away_ref[0, rows, :] = total
+
+        @pl.when(step >= half)
+        def _():
+            own_ref[0, rows, :] = total
+
+
+def combine(starts, places, values, block):
+    tokens = places.shape[0]
+    capacity, width = values[0].shape
+    half = tokens // block // 2
+    out = jax.ShapeDtypeStruct((half, block, width), bf16)
+    return pl.pallas_call(
+        functools.partial(combine_kernel, capacity=capacity),
+        grid=(2 * half,),
+        in_specs=[
+            pl.BlockSpec(memory_space=pltpu.SMEM),
+            pl.BlockSpec((block, LANES), lambda i: (i, 0)),
+        ]
+        + [pl.BlockSpec((capacity, width), lambda i: (0, 0)) for _ in values],
+        out_specs=[
+            pl.BlockSpec((1, block, width), lambda i: (jnp.maximum(i - half, 0), 0, 0)),
+            pl.BlockSpec((1, block, width), lambda i: (jnp.minimum(i, half - 1), 0, 0)),
         ],
-        1,
-    )
-
-
-def combine_kernel(place_ref, values_ref, out_ref, *, count, capacity):
-    chosen = picks(place_ref, count, capacity)
-    out_ref[...] = dot(chosen, values_ref[...]).astype(bf16)
-
-
-def combine(places, values, capacity, block):
-    tokens = places.shape[0]
-    slots, width = values.shape
-    return pl.pallas_call(
-        functools.partial(combine_kernel, count=slots // capacity, capacity=capacity),
-        grid=(tokens // block,),
-        in_specs=[
-            pl.BlockSpec((block, LANES), lambda i: (i, 0)),
-            pl.BlockSpec((slots, width), lambda i: (0, 0)),
-        ],
-        out_specs=pl.BlockSpec((block, width), lambda i: (i, 0)),
-        out_shape=jax.ShapeDtypeStruct((tokens, width), bf16),
+        out_shape=[out, out],
         compiler_params=BIG,
         name="combine_rows",
-    )(places, values)
-
-
-def combine_add_kernel(own_ref, place_ref, values_ref, add_ref, out_ref, *, count, capacity):
-    chosen = picks(place_ref, count, capacity)
-    factor = jnp.where(pl.program_id(0) == own_ref[0], 1.0, 0.0)
-    total = dot(chosen, values_ref[...]) + add_ref[...] * factor
-    parts, _, width = out_ref.shape
-    for part in range(parts):
-        out_ref[part] = total[:, part * width : (part + 1) * width].astype(bf16)
-
-
-def combine_add(own, places, values, addition, capacity, parts):
+    )(starts, places, *values)
+
+
+def combine_add_kernel(own_ref, starts_ref, place_ref, add_ref, *refs, capacity):
+    *value_refs, out_ref = refs
+    step = pl.program_id(0)
+    factor = jnp.where(step == own_ref[0], 1.0, 0.0)
+    parts, block, width = out_ref.shape
+    pieces = block // LANES
+    for piece in range(pieces):
+        rows = slice(piece * LANES, (piece + 1) * LANES)
+        total = gather_back(
+            starts_ref, place_ref[rows, :], value_refs, step * pieces + piece, capacity
+        )
+        total += add_ref[rows, :] * factor
+        for part in range(parts):
+            out_ref[part, rows, :] = total[:, part * width : (part + 1) * width].astype(bf16)
+
+
+def combine_add(own, starts, places, values, addition, parts):
     tokens = places.shape[0]
-    slots, width = values.shape
+    capacity, width = values[0].shape
     block = addition.shape[0]
     return pl.pallas_call(
-        functools.partial(combine_add_kernel, count=slots // capacity, capacity=capacity),
+        functools.partial(combine_add_kernel, capacity=capacity),
         grid=(tokens // block,),
         in_specs=[
             pl.BlockSpec(memory_space=pltpu.SMEM),
+            pl.BlockSpec(memory_space=pltpu.SMEM),
             pl.BlockSpec((block, LANES), lambda i: (i, 0)),
-            pl.BlockSpec((slots, width), lambda i: (0, 0)),
             pl.BlockSpec((block, width), lambda i: (0, 0)),
-        ],
+        ]
+        + [pl.BlockSpec((capacity, width), lambda i: (0, 0)) for _ in values],
         out_specs=pl.BlockSpec((parts, block, width // parts), lambda i: (0, i, 0)),
         out_shape=jax.ShapeDtypeStruct((parts, tokens, width // parts), bf16),
         compiler_params=BIG,
         name="combine_rows_add",
-    )(own, places, values, addition)
+    )(own, starts, places, addition, *values)
 
 
 def expert_kernel(
-    slot_ref, grad_ref, up_ref, down_ref, router_ref, pick_ref,
-    out_ref, back_ref, grad_up_ref, grad_down_ref,
+    weight_ref, router_ref, pick_ref, *refs, groups, row_count, col_count
 ):
-    step = pl.program_id(0)
+    slot_refs, grad_refs = refs[:groups], refs[groups : 2 * groups]
+    out_refs, back_a_refs, back_b_refs = (
+        refs[at * groups : (at + 1) * groups] for at in (2, 3, 4)
+    )
+    grad_weight_ref, up_ref, down_ref, grad_up_ref, grad_down_ref, slot_ref, grad_ref = refs[
+        5 * groups :
+    ]
+    step = pl.program_id(0) * pl.num_programs(1) + pl.program_id(1)
+    last = pl.num_programs(0) * pl.num_programs(1) - 1
     width = slot_ref.shape[1]
+    split = back_b_refs[0].shape[1]
+    for group in range(groups):
+
+        @pl.when(pl.program_id(0) == group)
+        def _():
+            slot_ref[...] = slot_refs[group][...]
+            grad_ref[...] = grad_refs[group][...]
+
     hidden_cols = down_ref.shape[0]
+    part = weight_ref.shape[2]
+
+    def blocks():
+        for row in range(row_count):
+            for col in range(col_count):
+                rows = slice(row * part, (row + 1) * part)
+                cols = slice(col * part, (col + 1) * part)
+                above = slice(hidden_cols + col * part, hidden_cols + (col + 1) * part)
+                yield row * col_count + col, rows, cols, above
+
+    @pl.when(step == 0)
+    def _():
+        for cell, rows, cols, above in blocks():
+            up_ref[rows, cols] = weight_ref[cell, :part, :]
+            up_ref[rows, above] = weight_ref[cell, part : 2 * part, :]
+            down_ref[cols, rows] = weight_ref[cell, 2 * part :, :]
+        grad_up_ref[...] = jnp.zeros_like(grad_up_ref)
+        grad_down_ref[...] = jnp.zeros_like(grad_down_ref)
+
     slots = slot_ref[...]
     grads = grad_ref[:, :width].astype(f32)
     member = grad_ref[:, width:].astype(f32) > 0.5
@@ -352,12 +479,11 @@
     silu = gate_part * sigmoid
     hidden = (silu * up_part).astype(bf16)
     result = dot(hidden, down_ref[...])
-    out_ref[...] = (result * gate).astype(bf16)
+    scaled = (result * gate).astype(bf16)
     dots = jnp.sum(result * grads, -1, keepdims=True)
     dots_high = dots.astype(bf16).astype(f32)
-    back_ref[:, width:] = (dots_high * pick[0:1, :] + (dots - dots_high) * pick[1:2, :]).astype(
-        bf16
-    )
+    dots_low = dots - dots_high
+    split_dots = (dots_high * pick[0:1, :] + dots_low * pick[1:2, :]).astype(bf16)
     grad_expert = (grads * gate).astype(bf16)
     grad_hidden = dot_nt(grad_expert, down_ref[...])
     grad_pair = jnp.concatenate(
@@ -367,48 +493,99 @@
         ],
         1,
     ).astype(bf16)
-    back_ref[:, :width] = dot_nt(grad_pair, up_ref[...]).astype(bf16)
-
-    @pl.when(step == 0)
-    def _():
-        grad_up_ref[...] = jnp.zeros_like(grad_up_ref)
-        grad_down_ref[...] = jnp.zeros_like(grad_down_ref)
+    back = dot_nt(grad_pair, up_ref[...]).astype(bf16)
+    for group in range(groups):
+
+        @pl.when(pl.program_id(0) == group)
+        def _():
+            out_refs[group][...] = scaled
+            back_a_refs[group][:, :LANES] = split_dots
+            back_a_refs[group][:, LANES:] = back[:, : width - split]
+            back_b_refs[group][...] = back[:, width - split :]
 
     grad_up_ref[...] += dot_tn(slots, grad_pair)
     grad_down_ref[...] += dot_tn(hidden, grad_expert)
 
-
-def run_expert(slots, grads, up, down, router, pick, block):
-    rows, width = slots.shape
-    rest = grads.shape[1]
-    hidden_cols = down.shape[0]
-    whole = lambda shape: pl.BlockSpec(shape, lambda i: (0, 0))
-    return pl.pallas_call(
-        expert_kernel,
-        grid=(rows // block,),
-        in_specs=[
-            pl.BlockSpec((block, width), lambda i: (i, 0)),
-            pl.BlockSpec((block, rest), lambda i: (i, 0)),
-            whole(up.shape),
-            whole(down.shape),
-            whole(router.shape),
-            whole(pick.shape),
-        ],
-        out_specs=[
-            pl.BlockSpec((block, width), lambda i: (i, 0)),
-            pl.BlockSpec((block, rest), lambda i: (i, 0)),
-            whole((width, 2 * hidden_cols)),
-            whole((hidden_cols, width)),
-        ],
-        out_shape=[
-            jax.ShapeDtypeStruct((rows, width), bf16),
-            jax.ShapeDtypeStruct((rows, rest), bf16),
-            jax.ShapeDtypeStruct((width, 2 * hidden_cols), f32),
-            jax.ShapeDtypeStruct((hidden_cols, width), f32),
+    @pl.when(step == last)
+    def _():
+        for cell, rows, cols, above in blocks():
+            grad_weight_ref[cell, :part, :] = grad_up_ref[rows, cols].astype(bf16)
+            grad_weight_ref[cell, part : 2 * part, :] = grad_up_ref[rows, above].astype(bf16)
+            grad_weight_ref[cell, 2 * part :, :] = grad_down_ref[cols, rows].astype(bf16)
+
+
+def run_expert(slots, grads, weights, router, pick, steps, row_count, col_count):
+    groups = len(slots)
+    capacity, width = slots[0].shape
+    rest = grads[0].shape[1]
+    half = width // 2
+    block = capacity // steps
+    hidden_cols = weights.shape[2] * col_count
+    whole = lambda shape: pl.BlockSpec(shape, lambda i, j: (0,) * len(shape))
+
+    def some(cols):
+        def spec(group):
+            return pl.BlockSpec(
+                (block, cols),
+                lambda i, j: (
+                    jnp.where(i < group, 0, jnp.where(i > group, steps - 1, j)),
+                    0,
+                ),
+            )
+
+        return [spec(group) for group in range(groups)]
+
+    shapes = lambda cols: [jax.ShapeDtypeStruct((capacity, cols), bf16)] * groups
+    outs = pl.pallas_call(
+        functools.partial(
+            expert_kernel, groups=groups, row_count=row_count, col_count=col_count
+        ),
+        grid=(groups, steps),
+        in_specs=[whole(weights.shape), whole(router.shape), whole(pick.shape)]
+        + some(width)
+        + some(rest),
+        out_specs=some(width) + some(half + LANES) + some(half) + [whole(weights.shape)],
+        out_shape=shapes(width)
+        + shapes(half + LANES)
+        + shapes(half)
+        + [jax.ShapeDtypeStruct(weights.shape, bf16)],
+        scratch_shapes=[
+            pltpu.VMEM((width, 2 * hidden_cols), bf16),
+            pltpu.VMEM((hidden_cols, width), bf16),
+            pltpu.VMEM((width, 2 * hidden_cols), f32),
+            pltpu.VMEM((hidden_cols, width), f32),
+            pltpu.VMEM((block, width), bf16),
+            pltpu.VMEM((block, rest), bf16),
         ],
         compiler_params=BIG,
         name="expert_pass",
-    )(slots, grads, up, down, router, pick)
+    )(weights, router, pick, *slots, *grads)
+    return (
+        outs[:groups],
+        outs[groups : 2 * groups],
+        outs[2 * groups : 3 * groups],
+        outs[3 * groups],
+    )
+
+
+def spread_kernel(block_ref, *out_refs):
+    part = out_refs[0].shape[1]
+    for index, out_ref in enumerate(out_refs):
+        out_ref[0] = block_ref[0, index * part : (index + 1) * part, :].astype(f32)
+
+
+def spread_blocks(blocks, count):
+    cells, rows, cols = blocks.shape
+    part = rows // count
+    return pl.pallas_call(
+        spread_kernel,
+        grid=(cells,),
+        in_specs=[pl.BlockSpec((1, rows, cols), lambda i: (i, 0, 0))],
+        out_specs=[pl.BlockSpec((1, part, cols), lambda i: (i, 0, 0))] * count,
+        out_shape=[jax.ShapeDtypeStruct((cells, part, cols), f32)] * count,
+        compiler_params=BIG,
+        name="spread_blocks",
+    )(blocks)
 
 
 def norm_back(grad, values, inv_rms, gain):
@@ -481,49 +658,147 @@
     assert sequences == row_count and spread * cells == experts and copies * spread == dp_count
     spread_at = dp_at % spread
     if copies == 1:
-        near, far = None, None
+        far = None
     else:
-        near = [[i * spread + j for j in range(spread)] for i in range(copies)]
         far = [[i * spread + j for i in range(copies)] for j in range(spread)]
 
-    def exchange(rows):
-        return lax.all_to_all(rows, "dp", 0, 0, axis_index_groups=near, tiled=True)
+    def exchange(arrays):
+        return [over_dp(array, turn) for turn, array in enumerate(arrays)]
 
     def by_cell(array):
         lead = array.shape[:-1]
         split = array.reshape(lead + (copies, spread, per_dp))
         return jnp.swapaxes(split, -3, -2).reshape(lead + (spread, cells))
 
-    qkv_own = jnp.concatenate([query_weight, key_weight, value_weight], 1)
-    qkv_weight = lax.all_gather(qkv_own, "row", axis=0, tiled=True)
-    columns = lax.all_gather(hidden_in, "col", axis=0, tiled=True)
-    tokens_in = lax.all_to_all(columns, "row", 0, 1, tiled=True)
-    gains = lax.all_gather(jnp.stack([norm1_gain, norm2_gain]), "row", axis=1, tiled=True)
-    gain_one, gain_two = gains[0][None, :], gains[1][None, :]
-    out_weight = lax.all_gather(output_weight, "row", axis=1, tiled=True)
-    router = lax.all_gather(router_weight, "row", axis=0, tiled=True)
-    router_pad = jnp.pad(router, ((0, 0), (0, LANES - experts)))
-    grad_stack = lax.all_gather(grad_out, ("row", "col"), axis=0, tiled=True).reshape(
+    per_col = sequences // col_count
+    part_at = (row_at // col_count) * col_count + col_at
+    sequence_of = lambda row: (row % col_count) * per_col + row // col_count
+    block_of = lambda row, col: sequence_of(row) * col_count + col
+    own_block = block_of(row_at, col_at)
+
+    def rounds():
+        for turn in range(row_count):
+            there, back = [], []
+            for row in range(row_count):
+                for col in range(col_count):
+                    part = (row - turn) % row_count
+                    other = ((part // col_count) * col_count + col) * col_count + part % col_count
+                    there.append((row * col_count + col, other))
+                    back.append((other, row * col_count + col))
+            yield turn, there, back
+
+    def to_sequences(array):
+        parts = array.reshape(per_col, seq_len, local_width)
+        got = []
+        for turn, there, _ in rounds():
+            part = (row_at - turn) % row_count
+            own = lax.dynamic_index_in_dim(parts, part // col_count, 0, keepdims=False)
+            got.append(lax.ppermute(own, ("row", "col"), there))
+        got = jnp.stack(got)
+        return jnp.concatenate(
+            [
+                lax.dynamic_index_in_dim(got, (row - part_at) % row_count, 0, keepdims=False)
+                for row in range(row_count)
+            ],
+            1,
+        )
+
+    def from_sequences(array):
+        parts = array.reshape(seq_len, row_count, local_width).transpose(1, 0, 2)
+        got = []
+        for turn, _, back in rounds():
+            own = lax.dynamic_index_in_dim(
+                parts, (turn + part_at) % row_count, 0, keepdims=False
+            )
+            got.append(lax.ppermute(own, ("row", "col"), back).astype(f32))
+        total = []
+        for index in range(per_col):
+            total.append(
+                sum(
+                    jnp.where(((row_at - turn) % row_count) // col_count == index, got[turn], 0.0)
+                    for turn in range(row_count)
+                )
+            )
+        return jnp.concatenate(total, 0)
+
+    own_start = col_at * own_rows
+    mirror = [(col, col_count - 1 - col) for col in range(col_count)]
+
+    def sum_halves(array):
+        parts = array.reshape(col_count, own_rows, array.shape[1])
+        away = lax.dynamic_index_in_dim(parts, 1 - col_at, 0, keepdims=False).astype(bf16)
+        own = lax.dynamic_index_in_dim(parts, col_at, 0, keepdims=False)
+        return own + lax.ppermute(away, "col", mirror).astype(f32)
+
+    def join_halves(array):
+        other = lax.ppermute(array, "col", mirror)
+        first = col_at == 0
+        return jnp.concatenate(
+            [jnp.where(first, array, other), jnp.where(first, other, array)], 0
+        )
+
+    def in_terms(array):
+        terms = []
+        for _ in range(3):
+            terms.append(array.astype(bf16))
+            array = array - terms[-1].astype(f32)
+        return terms
+
+    tokens_in = to_sequences(hidden_in)
+    extras = jnp.concatenate(
+        [router_weight, jnp.stack(in_terms(norm1_gain) + in_terms(norm2_gain), 1)], 1
+    )
+    def over_rows(array, turn):
+        pairs = [(row, row ^ turn) for row in range(row_count)]
+        return lax.ppermute(array, "row", pairs) if turn else array
+
+    def over_dp(array, turn):
+        pairs = [(at, at ^ turn) for at in range(dp_count)]
+        return lax.ppermute(array, "dp", pairs) if turn else array
+
+    def over_cells(array, turn):
+        pairs = [(at, at ^ turn) for at in range(cells)]
+        return lax.ppermute(array, ("row", "col"), pairs) if turn else array
+
+    pick_from = lambda array, at: lax.dynamic_index_in_dim(array, at, 0, keepdims=False)
+
+    def all_rows(array):
+        share = local_width // spread
+        own = lax.dynamic_slice_in_dim(array, spread_at * share, share, 0)
+        rows = jnp.stack([over_rows(own, turn) for turn in range(row_count)])
+        rows = jnp.stack([pick_from(rows, row_at ^ row) for row in range(row_count)])
+        shares = jnp.stack([over_dp(rows, turn) for turn in range(spread)])
+        ordered = jnp.stack([pick_from(shares, spread_at ^ at) for at in range(spread)], 1)
+        return ordered.reshape(width, array.shape[1])
+
+    qkv_cols = query_cols + 2 * key_cols
+    first_weights = all_rows(
+        jnp.concatenate(
+            [
+                query_weight,
+                key_weight,
+                value_weight,
+                jnp.pad(extras, ((0, 0), (0, LANES - extras.shape[1]))),
+            ],
+            1,
+        )
+    )
+    first_weights, grad_late = lax.optimization_barrier((first_weights, grad_out))
+    grad_stack = lax.all_gather(grad_late, ("row", "col"), axis=0, tiled=True).reshape(
         row_count, group, local_width
     )
 
-    def own_share(weight):
-        split = weight.reshape((copies, spread, per_dp) + weight.shape[1:])
-        return lax.dynamic_index_in_dim(split, spread_at, 1, keepdims=False).reshape(
-            (cells,) + weight.shape[1:]
-        )
-
-    shares = jnp.concatenate(
-        [own_share(gate_weight), own_share(up_weight), jnp.swapaxes(own_share(down_weight), 1, 2)],
-        2,
-    ).reshape(cells * local_width, 3 * hidden_part)
-    got = lax.all_to_all(shares, ("row", "col"), 0, 0, tiled=True).reshape(
-        row_count, col_count, local_width, 3, hidden_part
-    )
-    pair_weight = (
-        got[:, :, :, :2, :].transpose(0, 2, 3, 1, 4).reshape(width, 2 * hidden_cols)
-    )
-    down_full = got[:, :, :, 2, :].transpose(1, 3, 0, 2).reshape(hidden_cols, width)
+    qkv_weight = first_weights[:, :qkv_cols]
+    extras = first_weights[:, qkv_cols:]
+    out_weight = all_rows(output_weight.T)
+    router_pad = jnp.where(jnp.arange(LANES)[None, :] < experts, extras, jnp.zeros((), bf16))
+    router = extras[:, :experts]
+    terms = extras[:, experts : experts + 6].astype(f32)
+    gain_one = (terms[:, 0] + terms[:, 1] + terms[:, 2])[None, :]
+    gain_two = (terms[:, 3] + terms[:, 4] + terms[:, 5])[None, :]
+    def from_cells(array):
+        rows = [over_rows(array, turn) for turn in range(row_count)]
+        return [(block, lax.ppermute(block, "col", mirror)) for block in rows]
 
     member = jnp.any(
         expert_ids[:, :, None] == jnp.arange(experts, dtype=jnp.int32)[None, None, :], 1
@@ -531,9 +806,35 @@
     mine = lax.dynamic_index_in_dim(
         by_cell(member.astype(f32)), cell, 2, keepdims=False
     )
+    mine = jnp.concatenate(
+        [lax.dynamic_slice_in_dim(mine, spread_at ^ turn, 1, 1) for turn in range(spread)], 1
+    )
     places = jnp.where(mine > 0.5, running_count(mine) - 1, -1)
-    place_rows = places.T.reshape(spread, 1, group)
-    place_cols = jnp.pad(places, ((0, 0), (0, LANES - spread)), constant_values=-1)
+    first = running_count(mine) - mine.astype(jnp.int32)
+    token_blocks = places.reshape(cells, own_rows, spread)
+    first_blocks = first.reshape(cells, own_rows, spread)[:, ::LANES]
+    pad_cols = lambda array: jnp.pad(
+        array, ((0, 0), (0, LANES - spread)), constant_values=-1
+    )
+    arrival = [
+        block_of(row_at ^ turn, col_at ^ side)
+        for turn in range(row_count)
+        for side in range(2)
+    ]
+    away_first = [arrival[1::2], arrival[0::2]]
+    order = lambda array, cells_of: jnp.stack(
+        [lax.dynamic_index_in_dim(array, at, 0, keepdims=False) for at in cells_of]
+    )
+    rows_of = lambda array: array.reshape(group, spread).T.reshape(spread, 1, group)
+    places_two = rows_of(order(token_blocks, arrival))
+    starts_two = order(first_blocks, arrival)[:, 0].T.reshape(-1)
+    combined = away_first[0] + away_first[1]
+    places_back = pad_cols(order(token_blocks, combined).reshape(group, spread))
+    starts_back = order(first_blocks, combined).reshape(-1)
+    places_all = pad_cols(places)
+    starts_all = first_blocks.reshape(-1)
+    places_grad = rows_of(places)
+    starts_grad = first_blocks[:, 0].T.reshape(-1)
     member_pad = jnp.pad(member.astype(bf16), ((0, 0), (0, LANES - experts)))
     my_expert = ((cell // per_dp) * spread + spread_at) * per_dp + cell % per_dp
     lane = jnp.arange(LANES)[None, :]
@@ -545,14 +846,8 @@
         ],
         0,
     )
-    grad_slots = exchange(
-        dispatch(place_rows, [grad_stack, member_pad[None]], capacity).reshape(
-            spread * capacity, width + LANES
-        )
-    )
-
     tables = rope_tables(seq_len)
-    segments = lax.dynamic_index_in_dim(segment_ids, row_at, 0, keepdims=True)
+    segments = lax.dynamic_index_in_dim(segment_ids, sequence_of(row_at), 0, keepdims=True)
     seg_col = segments.reshape(seq_len, 1)
     residual = tokens_in.astype(f32)
     inv_one = inverse_rms(residual)
@@ -561,111 +856,150 @@
     query_low, key_low, value_low, heads, log_sums = attend_forward(
         raw, tables, seg_col, segments, kv_heads, block
     )
-    attended = lax.psum_scatter(
-        dot(heads, out_weight).astype(bf16), "col", scatter_dimension=0, tiled=True
-    )
-    own_start = col_at * own_rows
-    middle = lax.dynamic_slice_in_dim(residual, own_start, own_rows, 0) + attended.astype(f32)
+    attended = dot_nt(heads, out_weight)
+    middle = lax.dynamic_slice_in_dim(residual, own_start, own_rows, 0) + sum_halves(attended)
     inv_two = inverse_rms(middle)
     normed_two = (middle * inv_two * gain_two).astype(bf16)
-
-    tokens_two = lax.all_gather(normed_two, ("row", "col"), axis=0, tiled=True)
-    slots = exchange(
-        dispatch(place_rows, [tokens_two[None]], capacity).reshape(spread * capacity, width)
-    )
-    results, back, grad_pair_w, grad_down_w = run_expert(
-        slots, grad_slots, pair_weight, down_full, router_pad, pick, 256
-    )
-    back_rows = combine(place_cols, exchange(back), capacity, own_rows)
-    grad_own = lax.psum_scatter(back_rows, ("row", "col"), scatter_dimension=0, tiled=True).astype(
-        f32
-    )
+    half = width // 2
+    pieces_two = from_cells(normed_two)
+    blocks = [block for pair in pieces_two for block in pair]
+    grad_sent = dispatch_grads(
+        starts_grad, places_grad, grad_stack, member_pad, capacity, own_rows
+    )
+    grad_slots = exchange(grad_sent)
+    grad_slots[0], grad_slots[1], blocks[0] = lax.optimization_barrier(
+        (grad_slots[0], grad_slots[1], blocks[0])
+    )
+
+    def own_share(weight):
+        split = weight.reshape((copies, spread, per_dp) + weight.shape[1:])
+        return lax.dynamic_index_in_dim(split, spread_at, 1, keepdims=False).reshape(
+            (cells,) + weight.shape[1:]
+        )
+
+    shares = jnp.concatenate(
+        [own_share(gate_weight), own_share(up_weight), own_share(down_weight)], 1
+    )
+    *blocks, shares = lax.optimization_barrier((*blocks, shares))
+    expert_weights = lax.all_to_all(shares, ("row", "col"), 0, 0, tiled=True)
+
+    slots = exchange(dispatch_two(starts_two, places_two, blocks, capacity))
+    results, back_a, back_b, grad_blocks = run_expert(
+        slots, grad_slots, expert_weights, router_pad, pick, 2, row_count, col_count
+    )
+
+    def to_cells(back):
+        return combine(starts_back, places_back, back, own_rows)
+
+    def half_sums(own, away):
+        return [own[turn].astype(f32) + away[turn].astype(f32) for turn in range(row_count)]
+
+    def row_parts(sums):
+        return [over_rows(sums[turn].astype(bf16), turn) for turn in range(1, row_count)]
+
+    grad_got = lax.all_to_all(grad_blocks, ("row", "col"), 0, 0, tiled=True)
+    kept_a, away_a = to_cells(exchange(back_a))
+    away_a = lax.ppermute(away_a, "col", mirror)
+    back_b = exchange(back_b)
+    kept_b, away_b = to_cells(back_b)
+    away_a, kept_b, away_b = lax.optimization_barrier((away_a, kept_b, away_b))
+    away_b = lax.ppermute(away_b, "col", mirror)
+    sums_a = half_sums(kept_a, away_a)
+    parts_a = row_parts(sums_a)
+    away_b, *parts_a = lax.optimization_barrier((away_b, *parts_a))
+    sums_b = half_sums(kept_b, away_b)
+    parts_b = row_parts(sums_b)
+    own_a = sums_a[0] + sum(part.astype(f32) for part in parts_a)
+    own_b = sums_b[0] + sum(part.astype(f32) for part in parts_b)
+    own_a, grad_got = lax.optimization_barrier((own_a, grad_got))
+
+    if copies > 1:
+        grad_got = lax.psum_scatter(
+            grad_got, "dp", scatter_dimension=0, axis_index_groups=far, tiled=True
+        )
+    grad_gate, grad_up, grad_down = spread_blocks(grad_got, 3)
+
+    back_b, results = lax.optimization_barrier((back_b, results))
+    results = exchange(results)
     mixed_rows = combine_add(
-        cell.reshape(1), place_cols, exchange(results), middle, capacity, row_count
-    )
+        own_block.reshape(1), starts_all, places_all, results, middle, row_count
+    )
+    own_member = lax.dynamic_slice_in_dim(member, own_block * own_rows, own_rows, 0)
+    logits = jnp.where(own_member, dot(normed_two, router), masked_score)
+    powers = jnp.where(own_member, jnp.exp(logits - jnp.max(logits, -1, keepdims=True)), 0.0)
+    gates = powers / jnp.sum(powers, -1, keepdims=True)
+    extra = own_a[:, :LANES]
+    grad_gates = extra[:, :experts] + extra[:, experts : 2 * experts]
+    grad_logits = (
+        gates * (grad_gates - jnp.sum(gates * grad_gates, -1, keepdims=True))
+    ).astype(bf16)
+    grad_router = dot_tn(normed_two, grad_logits)
+    grad_two = jnp.concatenate([own_a[:, LANES:], own_b], 1) + dot_nt(grad_logits, router)
+    grad_norm, grad_gain_two = norm_back(grad_two, middle, inv_two, gain_two)
+    own_grad = (
+        lax.dynamic_slice_in_dim(grad_stack, own_block * own_rows, own_rows, 1)
+        .transpose(1, 0, 2)
+        .reshape(own_rows, width)
+    )
+    grad_middle = own_grad.astype(f32) + grad_norm
+
+    def dp_sums(*columns):
+        stacked = jnp.concatenate([column.astype(bf16) for column in columns], 1)
+        stacked = jnp.pad(stacked, ((0, 0), (0, -stacked.shape[1] % LANES)))
+        cols = stacked.shape[1]
+        share = local_width // dp_count
+        parts = stacked.reshape(row_count, dp_count, share, cols).swapaxes(0, 1)
+        parts = lax.all_to_all(
+            parts.reshape(dp_count, row_count * share, cols), "dp", 0, 0, tiled=True
+        )
+        return jnp.sum(parts.astype(f32), 0).astype(bf16).reshape(row_count, share, cols)
+
+    def row_sums(parts):
+        parts = lax.all_to_all(parts, "row", 0, 0, tiled=True)
+        return jnp.sum(parts.astype(f32), 0).astype(bf16)
+
+    grad_mid = join_halves(grad_middle.astype(bf16))
+    out_sums = dp_sums(dot_tn(grad_mid, heads))
+    grad_heads = dot(grad_mid, out_weight).astype(bf16)
+    grad_heads, mixed_rows = lax.optimization_barrier((grad_heads, mixed_rows))
     mixed_out = lax.psum_scatter(
         mixed_rows.reshape(cells * local_rows, local_width),
         ("row", "col"),
         scatter_dimension=0,
         tiled=True,
     )
-
-    pair_split = grad_pair_w.reshape(row_count, local_width, 2, col_count, hidden_part)
-    down_split = grad_down_w.reshape(col_count, hidden_part, row_count, local_width)
-    grad_shares = jnp.concatenate(
-        [
-            pair_split.transpose(0, 3, 1, 2, 4).reshape(cells, local_width, 2 * hidden_part),
-            down_split.transpose(2, 0, 3, 1).reshape(cells, local_width, hidden_part),
-        ],
-        2,
-    ).astype(bf16)
-    grad_got = lax.all_to_all(
-        grad_shares.reshape(cells * local_width, 3 * hidden_part), ("row", "col"), 0, 0, tiled=True
-    )
-    if copies > 1:
-        grad_got = lax.psum_scatter(
-            grad_got, "dp", scatter_dimension=0, axis_index_groups=far, tiled=True
-        )
-    grad_got = grad_got.reshape(per_dp, local_width, 3, hidden_part).astype(f32)
-    grad_gate, grad_up = grad_got[:, :, 0], grad_got[:, :, 1]
-    grad_down = jnp.swapaxes(grad_got[:, :, 2], 1, 2)
-
-    own_member = lax.dynamic_slice_in_dim(member, cell * own_rows, own_rows, 0)
-    logits = jnp.where(own_member, dot(normed_two, router), masked_score)
-    powers = jnp.where(own_member, jnp.exp(logits - jnp.max(logits, -1, keepdims=True)), 0.0)
-    gates = powers / jnp.sum(powers, -1, keepdims=True)
-    extra = grad_own[:, width:]
-    grad_gates = extra[:, :experts] + extra[:, experts : 2 * experts]
-    grad_logits = (
-        gates * (grad_gates - jnp.sum(gates * grad_gates, -1, keepdims=True))
-    ).astype(bf16)
-    grad_router = dot_tn(normed_two, grad_logits)
-    grad_two = grad_own[:, :width] + dot_nt(grad_logits, router)
-    grad_norm, grad_gain_two = norm_back(grad_two, middle, inv_two, gain_two)
-    own_grad = (
-        lax.dynamic_slice_in_dim(grad_stack, cell * own_rows, own_rows, 1)
-        .transpose(1, 0, 2)
-        .reshape(own_rows, width)
-    )
-    grad_middle = own_grad.astype(f32) + grad_norm
-
-    grad_mid = lax.all_gather(grad_middle.astype(bf16), "col", axis=0, tiled=True)
-    grad_out_w = dot_tn(heads, grad_mid).astype(bf16)
-    grad_heads = dot_nt(grad_mid, out_weight).astype(bf16)
     grad_qkv = jnp.concatenate(
         attend_backward(
             query_low, key_low, value_low, log_sums, grad_heads, tables, seg_col, segments, block
         ),
         1,
     )
-    grad_qkv_w = dot_tn(normed_one, grad_qkv).astype(bf16)
     grad_one = dot_nt(grad_qkv, qkv_weight)
     grad_part, grad_gain_one = norm_back(grad_one, residual, inv_one, gain_one)
     at_own = lax.dynamic_slice_in_dim(grad_part, own_start, own_rows, 0) + grad_middle
     grad_part = lax.dynamic_update_slice_in_dim(grad_part, at_own, own_start, 0)
-    grad_cols = lax.all_to_all(grad_part.astype(bf16), "row", 1, 0, tiled=True)
-    grad_in = lax.psum_scatter(grad_cols, "col", scatter_dimension=0, tiled=True).astype(f32)
-
-    qkv_sum = lax.psum(
-        lax.psum_scatter(grad_qkv_w, "row", scatter_dimension=0, tiled=True), "dp"
-    ).astype(f32)
-    out_sum = lax.psum(
-        lax.psum_scatter(grad_out_w, "row", scatter_dimension=1, tiled=True), "dp"
-    ).astype(f32)
-    small = lax.psum(
-        (grad_gain_one, grad_gain_two, grad_router), ("dp", "row", "col")
-    )
-    mine_of = lambda array: lax.dynamic_slice_in_dim(array, row_at * local_width, local_width, 0)
+    grad_in = from_sequences(grad_part.astype(bf16))
+    qkv_sums = dp_sums(
+        dot_tn(normed_one, grad_qkv), grad_router, grad_gain_two[:, None], grad_gain_one[:, None]
+    )
+    qkv_sums, grad_in = lax.optimization_barrier((qkv_sums, grad_in))
+    summed = row_sums(jnp.concatenate([out_sums, qkv_sums], 2))
+    summed, mixed_out = lax.optimization_barrier((summed, mixed_out))
+    summed = lax.all_gather(summed, "dp", axis=0, tiled=True)
+    also = summed[:, -LANES:]
+    also = also.astype(f32) + lax.ppermute(also, "col", mirror).astype(f32)
+    out_sum = summed[:, :query_cols].astype(f32)
+    qkv_sum = summed[:, query_cols:-LANES].astype(f32)
     return (
         mixed_out,
         grad_in,
-        mine_of(small[0]),
+        also[:, experts + 1],
         qkv_sum[:, :query_cols],
         qkv_sum[:, query_cols : query_cols + key_cols],
         qkv_sum[:, query_cols + key_cols :],
-        out_sum,
-        mine_of(small[1]),
-        mine_of(small[2]),
+        out_sum.T,
+        also[:, experts],
+        also[:, :experts],
         grad_gate,
         grad_up,
         grad_down,

time: 1090 us -> 765 us (0.70)
  waiting for transfers between devices: 623 us -> 365 us
  blocking collectives: 155 us -> 8.84 us
  starting transfers between devices: 34.7 us -> 126 us
  local copies, waits for them, and re-layouts: 68.7 us -> 56.1 us
    ppermute x0 -> x53, waiting for transfers between devices: none -> 343 us  [the longest x21 191 us: over_dp(): return lax.ppermute(array, 'dp', pairs) if turn else array]
    all_gather x6 -> x1, waiting for transfers between devices: 210 us -> 7.84 us  [per_device(): lax.all_gather(grad_late, ('row', 'col'), axis=0, tiled=True)]
    all_to_all x7 -> x5, waiting for transfers between devices: 215 us -> 14.4 us  [the longest x1 14.4 us: row_sums(): parts = lax.all_to_all(parts, 'row', 0, 0, tiled=True)]
    reduce_scatter x5 -> x0, waiting for transfers between devices: 102 us -> none  [the longest x1 86.2 us: per_device(): lax.psum_scatter(back_rows, ('row', 'col'), scatter_dimension=0, tiled=True)]
    ppermute x0 -> x53, starting transfers between devices: none -> 89.2 us  [the longest x15 31.4 us: over_rows(): return lax.ppermute(array, 'row', pairs) if turn else array]
    reduce_scatter x1, waiting for transfers between devices: 88 us -> 0.02 us  [per_device(): lax.psum_scatter(mixed_rows.reshape(cells * local_rows, local_width), ('r...]
    all_gather x2 -> x1, blocking collectives: 63.7 us -> 8.84 us  [per_device(): summed = lax.all_gather(summed, 'dp', axis=0, tiled=True)]
    all_to_all x1 -> x0, blocking collectives: 53.8 us -> none  [per_device(): grad_cols = lax.all_to_all(grad_part.astype(bf16), 'row', 1, 0, tiled=True)]
  transfers between devices with their start and end apart: 21 -> 60, of which waited for: 16 -> 27; matrix products, arithmetic and copies ran while one was open for 10% -> 12% of each run, Pallas kernels for 6% -> 9%
where the time goes in v2:
time: 765 us; the launch traced here: 758 us
  waiting for transfers between devices  365 us (48%)
  Pallas kernels  131 us (17%)
  starting transfers between devices  126 us (16%)
  local copies, waits for them, and re-layouts  56.1 us (7%)
  other arithmetic  40.7 us (5%)
  between operations  15.7 us (2%)
  matrix products  14 us (2%)
  blocking collectives  8.84 us (1%)
    ppermute x21, waiting for transfers between devices, over_dp(): return lax.ppermute(array, 'dp', pairs) if turn else array  191 us
    ppermute x15, waiting for transfers between devices, over_rows(): return lax.ppermute(array, 'row', pairs) if turn else array  75.9 us
    pallas_call x1, Pallas kernels, run_expert(): pl.pallas_call(functools.partial(expert_kernel, groups=groups, row_count=...  48.6 us
    ppermute x4, waiting for transfers between devices, to_sequences(): got.append(lax.ppermute(own, ('row', 'col'), there))  31.9 us
    ppermute x15, starting transfers between devices, over_rows(): return lax.ppermute(array, 'row', pairs) if turn else array  31.4 us
    pallas_call x2, Pallas kernels, dispatch(): pl.pallas_call(kernel, grid=(count,), in_specs=[pl.BlockSpec(memory_space...  24.6 us
    pallas_call x2, Pallas kernels, combine(): pl.pallas_call(functools.partial(combine_kernel, capacity=capacity), grid...  19.9 us
    ppermute x4, starting transfers between devices, from_sequences(): got.append(lax.ppermute(own, ('row', 'col'), back).astype(f32))  19 us
  transfers between devices with their start and end apart: 60, of which 27 were waited for; matrix products, arithmetic and copies ran while one was open for 12% of the time, Pallas kernels for 9%

profile of v2, /device:TPU:0, one launch (start us, length us, event | category | flops | bytes accessed | tf_op | source)
XLA Modules:
  0.0 758.4 jit_solution(16384124694840547716)
XLA Ops:
  10.6 5.1 collective-permute-start.2
  16.3 4.1 collective-permute-done.2
  20.5 7.7 %collective-permute-done.1 = bf16[64,1152]{1,0:T(8,128)(2,1)S(1)} collective-permute-done((bf16[64,1152]{1,0:T(8,128)(2,1)S(1)}, bf16[64,1152]{1,0:T(8,128)(2,1)S(1)}, u32[]{:S(2)}, u32[]{:S(2)}) %collective-permute-start.1) | collective-permute-done | bytes 147488 | tf_op jit(solution)/shard_map/ppermute | solution.py:753
  34.9 10.2 %collective-permute-done.5 = bf16[4,64,1152]{2,1,0:T(8,128)(2,1)S(1)} collective-permute-done((bf16[4,64,1152]{2,1,0:T(8,128)(2,1)}, bf16[4,64,1152]{2,1,0:T(8,128)(2,1)S(1)}, u32[]{:S(2)}, u32[]{:S(2)}) %collective-permute-start.5) | collective-permute-done | bytes 589856 | tf_op jit(solution)/shard_map/ppermute | solution.py:757
  45.1 12.7 %collective-permute-done.4 = bf16[4,64,1152]{2,1,0:T(8,128)(2,1)S(1)} collective-permute-done((bf16[4,64,1152]{2,1,0:T(8,128)(2,1)}, bf16[4,64,1152]{2,1,0:T(8,128)(2,1)S(1)}, u32[]{:S(2)}, u32[]{:S(2)}) %collective-permute-start.4) | collective-permute-done | bytes 589856 | tf_op jit(solution)/shard_map/ppermute | solution.py:757
  72.7 14.3 %collective-permute-done.8 = bf16[512,256]{1,0:T(8,128)(2,1)} collective-permute-done((bf16[512,256]{1,0:T(8,128)(2,1)}, bf16[512,256]{1,0:T(8,128)(2,1)}, u32[]{:S(2)}, u32[]{:S(2)}) %collective-permute-start.8) | collective-permute-done | bytes 262176 | tf_op jit(solution)/shard_map/ppermute | solution.py:696
  87.1 17.5 %collective-permute-done.7 = bf16[512,256]{1,0:T(8,128)(2,1)S(1)} collective-permute-done((bf16[512,256]{1,0:T(8,128)(2,1)S(1)}, bf16[512,256]{1,0:T(8,128)(2,1)S(1)}, u32[]{:S(2)}, u32[]{:S(2)}) %collective-permute-start.7) | collective-permute-done | bytes 262176 | tf_op jit(solution)/shard_map/ppermute | solution.py:696
  112.4 10.1 %attend_forward.1 = (bf16[512,512]{1,0:T(8,128)(2,1)}, bf16[512,256]{1,0:T(8,128)(2,1)}, bf16[512,256]{1,0:T(8,128)(2,1)}, bf16[512,512]{1,0:T(8,128)(2,1)}, f32[512,256]{1,0:T(8,128)}) custom-call(f32[512,1024]{1,0:T(8,128)} %fusion.3.query_in.key_in.value_in, f32[512,1024]{1,0:T(8,128)} %fusion.3.query_in.key_in.value_in, ...), custom_call_target="tpu_custom_call" | custom-call | tf_op jit(solution)/shard_map/attend_forward/pallas_call | solution.py:129
  125.7 10.0 %collective-permute-start.16 = (bf16[256,1024]{1,0:T(8,128)(2,1)S(1)}, bf16[256,1024]{1,0:T(8,128)(2,1)S(1)}, u32[]{:S(2)}, u32[]{:S(2)}) collective-permute-start(bf16[256,1024]{1,0:T(8,128)(2,1)S(1)} %fusion.13), channel_id=1, source_target_pairs={{0,1},{1,0},{2,3},{3,2},{4,5},{5,4},{6,7},{7,6},{8,9},{9,8},{10,11... | collective-permute-start | bytes 1572872 | tf_op jit(solution)/shard_map/ppermute | solution.py:731
  140.5 9.7 %collective-permute-done.16 = bf16[256,1024]{1,0:T(8,128)(2,1)S(1)} collective-permute-done((bf16[256,1024]{1,0:T(8,128)(2,1)S(1)}, bf16[256,1024]{1,0:T(8,128)(2,1)S(1)}, u32[]{:S(2)}, u32[]{:S(2)}) %collective-permute-start.16) | collective-permute-done | bytes 524320 | tf_op jit(solution)/shard_map/ppermute | solution.py:731
  151.7 7.8 %all-gather.2.cloned.1.call-done = bf16[8192,256]{1,0:T(8,128)(2,1)} async-done(((bf16[1024,256]{1,0:T(8,128)(2,1)}), bf16[8192,256]{1,0:T(8,128)(2,1)}) %all-gather.2.cloned.1.call-update) | async-done | bytes 4194320 | tf_op jit(solution)/shard_map/all_gather | solution.py:787
  159.5 13.6 %dispatch_grads.1 = (bf16[640,1152]{1,0:T(8,128)(2,1)}, bf16[640,1152]{1,0:T(8,128)(2,1)}, bf16[640,1152]{1,0:T(8,128)(2,1)}, bf16[640,1152]{1,0:T(8,128)(2,1)}) custom-call(s32[32]{0:T(128)} %reshape.370.starts_ref, s32[4,1,2048]{2,1,0:T(1,128)} %copy.275.place_ref, bf16[4,2048,256]{2,1,0:T(8,128)(2,1)} %bitcast.202, ...), custom_call_target="tpu_custom_call" | custom-call | tf_op jit(solution)/shard_map/dispatch_grads/pallas_call | solution.py:300
  177.9 19.5 %collective-permute-done.19.refs_2_ = bf16[256,1024]{1,0:T(8,128)(2,1)S(1)} collective-permute-done((bf16[256,1024]{1,0:T(8,128)(2,1)S(1)}, bf16[256,1024]{1,0:T(8,128)(2,1)S(1)}, u32[]{:S(2)}, u32[]{:S(2)}) %collective-permute-start.19) | collective-permute-done | bytes 524320 | tf_op jit(solution)/shard_map/ppermute | solution.py:753
  198.3 13.3 %collective-permute-done.21.refs_4_ = bf16[256,1024]{1,0:T(8,128)(2,1)S(1)} collective-permute-done((bf16[256,1024]{1,0:T(8,128)(2,1)S(1)}, bf16[256,1024]{1,0:T(8,128)(2,1)S(1)}, u32[]{:S(2)}, u32[]{:S(2)}) %collective-permute-start.21) | collective-permute-done | bytes 524320 | tf_op jit(solution)/shard_map/ppermute | solution.py:753
  219.5 6.9 collective-permute-done.22.refs_5_
  227.2 8.8 %collective-permute-done.24.refs_7_ = bf16[256,1024]{1,0:T(8,128)(2,1)} collective-permute-done((bf16[256,1024]{1,0:T(8,128)(2,1)S(1)}, bf16[256,1024]{1,0:T(8,128)(2,1)}, u32[]{:S(2)}, u32[]{:S(2)}) %collective-permute-start.24) | collective-permute-done | bytes 524320 | tf_op jit(solution)/shard_map/ppermute | solution.py:801
  236.0 4.7 all-to-all-start
  245.5 11.0 %dispatch_tokens.1 = (bf16[640,1024]{1,0:T(8,128)(2,1)}, bf16[640,1024]{1,0:T(8,128)(2,1)}, bf16[640,1024]{1,0:T(8,128)(2,1)}, bf16[640,1024]{1,0:T(8,128)(2,1)}) custom-call(s32[32]{0:T(128)} %reshape.378.starts_ref, s32[4,1,2048]{2,1,0:T(1,128)} %reshape.380.place_ref, bf16[256,1024]{1,0:T(8,128)(2,1)} %copy-done.4, bf16[256,1024]{1,0:T(8,128)(2,1)} %copy-done.33, ...), custom_call_target="tpu_custom_call" | custom-call | tf_op jit(solution)/shard_map/dispatch_tokens/pallas_call | solution.py:300
  261.1 16.6 %collective-permute-done.28.refs_6_ = bf16[640,1152]{1,0:T(8,128)(2,1)} collective-permute-done((bf16[640,1152]{1,0:T(8,128)(2,1)}, bf16[640,1152]{1,0:T(8,128)(2,1)}, u32[]{:S(2)}, u32[]{:S(2)}) %collective-permute-start.28) | collective-permute-done | bytes 1474592 | tf_op jit(solution)/shard_map/ppermute | solution.py:757
  277.7 31.1 %collective-permute-done.29.refs_7_ = bf16[640,1152]{1,0:T(8,128)(2,1)} collective-permute-done((bf16[640,1152]{1,0:T(8,128)(2,1)}, bf16[640,1152]{1,0:T(8,128)(2,1)}, u32[]{:S(2)}, u32[]{:S(2)}) %collective-permute-start.29) | collective-permute-done | bytes 1474592 | tf_op jit(solution)/shard_map/ppermute | solution.py:757
  308.8 28.5 %collective-permute-done.26.refs_2_ = bf16[640,1024]{1,0:T(8,128)(2,1)} collective-permute-done((bf16[640,1024]{1,0:T(8,128)(2,1)}, bf16[640,1024]{1,0:T(8,128)(2,1)}, u32[]{:S(2)}, u32[]{:S(2)}) %collective-permute-start.26) | collective-permute-done | bytes 1310752 | tf_op jit(solution)/shard_map/ppermute | solution.py:757
  337.3 25.0 %collective-permute-done.27.refs_3_ = bf16[640,1024]{1,0:T(8,128)(2,1)} collective-permute-done((bf16[640,1024]{1,0:T(8,128)(2,1)}, bf16[640,1024]{1,0:T(8,128)(2,1)}, u32[]{:S(2)}, u32[]{:S(2)}) %collective-permute-start.27) | collective-permute-done | bytes 1310752 | tf_op jit(solution)/shard_map/ppermute | solution.py:757
  362.3 48.6 %expert_pass.1 = (bf16[640,1024]{1,0:T(8,128)(2,1)}, bf16[640,1024]{1,0:T(8,128)(2,1)}, bf16[640,1024]{1,0:T(8,128)(2,1)}, bf16[640,1024]{1,0:T(8,128)(2,1)}, bf...) custom-call(bf16[8,768,256]{2,1,0:T(8,128)(2,1)} %all-to-all-done.we, ...), custom_call_target="tpu_custom_call" | custom-call | tf_op jit(solution)/shard_map/expert_pass/pallas_call | solution.py:539
  410.9 5.7 all-to-all-start.1
  421.5 17.4 %collective-permute-done.31.refs_2_ = bf16[640,640]{1,0:T(8,128)(2,1)} collective-permute-done((bf16[640,640]{1,0:T(8,128)(2,1)}, bf16[640,640]{1,0:T(8,128)(2,1)}, u32[]{:S(2)}, u32[]{:S(2)}) %collective-permute-start.31) | collective-permute-done | bytes 819232 | tf_op jit(solution)/shard_map/ppermute | solution.py:757
  438.8 16.2 %collective-permute-done.32.refs_3_ = bf16[640,640]{1,0:T(8,128)(2,1)} collective-permute-done((bf16[640,640]{1,0:T(8,128)(2,1)}, bf16[640,640]{1,0:T(8,128)(2,1)}, u32[]{:S(2)}, u32[]{:S(2)}) %collective-permute-start.32) | collective-permute-done | bytes 819232 | tf_op jit(solution)/shard_map/ppermute | solution.py:757
  455.0 10.5 %combine_rows.2 = (bf16[4,256,640]{2,1,0:T(8,128)(2,1)}, bf16[4,256,640]{2,1,0:T(8,128)(2,1)}) custom-call(s32[64]{0:T(128)} %reshape.368.starts_ref, s32[2048,128]{1,0:T(8,128)} %pad.22.place_ref, bf16[640,640]{1,0:T(8,128)(2,1)} %get-tuple-element.104.refs_0_, bf16[640,640]{1,0:T(8,128)(2,1)} %collective-permute-done.30.refs_1_, ...), custom_call_target="tpu_custom_call" | custom-call | tf_op jit(solution)/shard_map/combine_rows/pallas_call | solution.py:371
  469.9 15.8 %collective-permute-done.35.refs_2_ = bf16[640,512]{1,0:T(8,128)(2,1)S(1)} collective-permute-done((bf16[640,512]{1,0:T(8,128)(2,1)S(1)}, bf16[640,512]{1,0:T(8,128)(2,1)S(1)}, u32[]{:S(2)}, u32[]{:S(2)}) %collective-permute-start.35) | collective-permute-done | bytes 655392 | tf_op jit(solution)/shard_map/ppermute | solution.py:757
  485.7 12.6 %collective-permute-done.36.refs_3_ = bf16[640,512]{1,0:T(8,128)(2,1)S(1)} collective-permute-done((bf16[640,512]{1,0:T(8,128)(2,1)S(1)}, bf16[640,512]{1,0:T(8,128)(2,1)S(1)}, u32[]{:S(2)}, u32[]{:S(2)}) %collective-permute-start.36) | collective-permute-done | bytes 655392 | tf_op jit(solution)/shard_map/ppermute | solution.py:757
  499.1 9.3 %combine_rows.3 = (bf16[4,256,512]{2,1,0:T(8,128)(2,1)}, bf16[4,256,512]{2,1,0:T(8,128)(2,1)}) custom-call(s32[64]{0:T(128)} %reshape.368.starts_ref, s32[2048,128]{1,0:T(8,128)} %pad.22.place_ref, bf16[640,512]{1,0:T(8,128)(2,1)} %get-tuple-element.110.refs_0_, bf16[640,512]{1,0:T(8,128)(2,1)} %copy-done.24, bf16[640,512]{1,0:T(8,128)(2,1)} %copy-done.25, ...), custom_call_target="tpu_custom_call" | custom-call | tf_op jit(solution)/shard_map/combine_rows/pallas_call | solution.py:371
  520.7 6.6 collective-permute-done.38
  528.7 9.2 %collective-permute-done.39 = bf16[256,640]{1,0:T(8,128)(2,1)S(1)} collective-permute-done((bf16[256,640]{1,0:T(8,128)(2,1)S(1)}, bf16[256,640]{1,0:T(8,128)(2,1)S(1)}, u32[]{:S(2)}, u32[]{:S(2)}) %collective-permute-start.39) | collective-permute-done | bytes 327712 | tf_op jit(solution)/shard_map/ppermute | solution.py:753
  541.9 11.3 %collective-permute-start.42 = (bf16[256,512]{1,0:T(8,128)(2,1)S(1)}, bf16[256,512]{1,0:T(8,128)(2,1)S(1)}, u32[]{:S(2)}, u32[]{:S(2)}) collective-permute-start(bf16[256,512]{1,0:T(8,128)(2,1)S(1)} %get-tuple-element.267), channel_id=1, source_target_pairs={{0,4},{2,6},{4,0},{6,2},{1,5},{3,7},{5,1},{7,3},{8,12},{10,14},{12... | collective-permute-start | bytes 786440 | tf_op jit(solution)/shard_map/ppermute | solution.py:753
  554.6 15.5 %collective-permute-done.42 = bf16[256,512]{1,0:T(8,128)(2,1)S(1)} collective-permute-done((bf16[256,512]{1,0:T(8,128)(2,1)S(1)}, bf16[256,512]{1,0:T(8,128)(2,1)S(1)}, u32[]{:S(2)}, u32[]{:S(2)}) %collective-permute-start.42) | collective-permute-done | bytes 262176 | tf_op jit(solution)/shard_map/ppermute | solution.py:753
  581.1 4.9 collective-permute-done.47.refs_3_
  586.0 11.0 %combine_rows_add.1 = bf16[4,2048,256]{2,1,0:T(8,128)(2,1)} custom-call(s32[1]{0:T(128)} %bitcast.87.own_ref, s32[64]{0:T(128)} %reshape.385.starts_ref, s32[2048,128]{1,0:T(8,128)} %pad.25.place_ref, f32[256,1024]{1,0:T(8,128)} %copy-done.2, bf16[640,1024]{1,0:T(8,128)(2,1)} %get-tuple-element.133.refs_0_, ...), custom_call_target="tpu_custom_call" | custom-call | tf_op jit(solution)/shard_map/combine_rows_add/pallas_call | solution.py:409
  602.9 4.4 all-to-all-start.2
  607.4 10.8 %attend_backward.1 = (bf16[512,512]{1,0:T(8,128)(2,1)}, bf16[512,256]{1,0:T(8,128)(2,1)}, bf16[512,256]{1,0:T(8,128)(2,1)}) custom-call(bf16[512,512]{1,0:T(8,128)(2,1)} %get-tuple-element.125.query_in, bf16[512,256]{1,0:T(8,128)(2,1)} %get-tuple-element.126.key_in, bf16[512,256]{1,0:T(8,128)(2,1)} %get-tuple-element.127.value_in, ...), custom_call_target="tpu_custom_call" | custom-call | tf_op jit(solution)/shard_map/attend_backward/pallas_call | solution.py:216
  625.5 6.7 concatenate.82
  636.9 3.6 all-to-all-start.3
  647.0 4.7 constant_dynamic-slice_fusion.33
  653.1 12.3 %collective-permute-start.49 = (bf16[512,256]{1,0:T(8,128)(2,1)S(1)}, bf16[512,256]{1,0:T(8,128)(2,1)}, u32[]{:S(2)}, u32[]{:S(2)}) collective-permute-start(bf16[512,256]{1,0:T(8,128)(2,1)S(1)} %bitcast.229), channel_id=1, source_target_pairs={{5,0},{7,1},{0,2},{2,3},{1,4},{3,5},{4,6},{6,7},{13,8},{15,9},{8,1... | collective-permute-start | bytes 786440 | tf_op jit(solution)/shard_map/ppermute | solution.py:713
  665.5 4.0 collective-permute-start.50
  670.9 18.8 %collective-permute-done.49 = bf16[512,256]{1,0:T(8,128)(2,1)} collective-permute-done((bf16[512,256]{1,0:T(8,128)(2,1)S(1)}, bf16[512,256]{1,0:T(8,128)(2,1)}, u32[]{:S(2)}, u32[]{:S(2)}) %collective-permute-start.49) | collective-permute-done | bytes 262176 | tf_op jit(solution)/shard_map/ppermute | solution.py:713
  695.3 18.1 %all-to-all-start.4 = ((bf16[4,64,1664]{2,1,0:T(8,128)(2,1)}), bf16[4,64,1664]{2,1,0:T(8,128)(2,1)S(1)}, u32[]{:S(2)}, u32[]{:S(2)}) async-start(bf16[4,64,1664]{2,1,0:T(8,128)(2,1)} %pad_maximum_fusion.9), calls=%async_computation.4 | async-start | bytes 1703936 | tf_op jit(solution)/shard_map/all_to_all | solution.py:958
  713.4 6.6 spread_blocks.1
  719.9 14.4 %all-to-all-done.4 = bf16[4,64,1664]{2,1,0:T(8,128)(2,1)S(1)} async-done(((bf16[4,64,1664]{2,1,0:T(8,128)(2,1)}), bf16[4,64,1664]{2,1,0:T(8,128)(2,1)S(1)}, u32[]{:S(2)}, u32[]{:S(2)}) %all-to-all-start.4) | async-done | bytes 852000 | tf_op jit(solution)/shard_map/all_to_all | solution.py:958
  734.5 8.8 %all_gather.7 = bf16[256,1664]{1,0:T(8,128)(2,1)S(1)} all-gather(bf16[64,1664]{1,0:T(8,128)(2,1)S(1)} %reduce_sum.146), channel_id=1, replica_groups=mesh['dp'=4,'row'=4,'col'=2] {'dp'}, dimensions={0}, use_global_device_ids=true | all-gather | bytes 1064960 | tf_op jit(solution)/shard_map/all_gather | solution.py:988
  (353 shorter events, 146.7 us)
Async XLA Ops:
  7.2 152.3 %all-gather.2.cloned.1.call-start = ((), (), s32[]{:S(2)}) async-start(), calls=%async_computation.6 | async-start | bytes 4718592 | tf_op jit(solution)/shard_map/all_gather | solution.py:787
  29.5 28.2 %collective-permute-start.4 = (bf16[4,64,1152]{2,1,0:T(8,128)(2,1)}, bf16[4,64,1152]{2,1,0:T(8,128)(2,1)S(1)}, u32[]{:S(2)}, u32[]{:S(2)}) collective-permute-start(bf16[4,64,1152]{2,1,0:T(8,128)(2,1)} %get-tuple-element.287), channel_id=1, source_target_pairs={{0,16},{8,24},{16,0},{24,8},{1,17},{9,25},{17,1},{25,9},{2,18},{10... | collective-permute-start | bytes 1769480 | tf_op jit(solution)/shard_map/ppermute | solution.py:757
  30.8 28.5 %collective-permute-start.3 = (bf16[4,64,1152]{2,1,0:T(8,128)(2,1)}, bf16[4,64,1152]{2,1,0:T(8,128)(2,1)S(1)}, u32[]{:S(2)}, u32[]{:S(2)}) collective-permute-start(bf16[4,64,1152]{2,1,0:T(8,128)(2,1)} %get-tuple-element.287), channel_id=1, source_target_pairs={{0,8},{8,0},{16,24},{24,16},{1,9},{9,1},{17,25},{25,17},{2,10},{10... | collective-permute-start | bytes 1769480 | tf_op jit(solution)/shard_map/ppermute | solution.py:757
  31.3 35.7 %collective-permute-start.12 = (bf16[64,512]{1,0:T(8,128)(2,1)S(1)}, bf16[64,512]{1,0:T(8,128)(2,1)}, u32[]{:S(2)}, u32[]{:S(2)}) collective-permute-start(bf16[64,512]{1,0:T(8,128)(2,1)S(1)} %bitcast.233), channel_id=1, source_target_pairs={{0,6},{2,4},{4,2},{6,0},{1,7},{3,5},{5,3},{7,1},{8,14},{10,12},{12... | collective-permute-start | bytes 196616 | tf_op jit(solution)/shard_map/ppermute | solution.py:753
  33.9 35.6 %collective-permute-start.11 = (bf16[64,512]{1,0:T(8,128)(2,1)S(1)}, bf16[64,512]{1,0:T(8,128)(2,1)}, u32[]{:S(2)}, u32[]{:S(2)}) collective-permute-start(bf16[64,512]{1,0:T(8,128)(2,1)S(1)} %bitcast.234), channel_id=1, source_target_pairs={{0,4},{2,6},{4,0},{6,2},{1,5},{3,7},{5,1},{7,3},{8,12},{10,14},{12... | collective-permute-start | bytes 196616 | tf_op jit(solution)/shard_map/ppermute | solution.py:753
  45.1 25.4 %collective-permute-start.10 = (bf16[64,512]{1,0:T(8,128)(2,1)S(1)}, bf16[64,512]{1,0:T(8,128)(2,1)}, u32[]{:S(2)}, u32[]{:S(2)}) collective-permute-start(bf16[64,512]{1,0:T(8,128)(2,1)S(1)} %bitcast.235), channel_id=1, source_target_pairs={{0,2},{2,0},{4,6},{6,4},{1,3},{3,1},{5,7},{7,5},{8,10},{10,8},{12,... | collective-permute-start | bytes 196616 | tf_op jit(solution)/shard_map/ppermute | solution.py:753
  59.3 27.8 %collective-permute-start.8 = (bf16[512,256]{1,0:T(8,128)(2,1)}, bf16[512,256]{1,0:T(8,128)(2,1)}, u32[]{:S(2)}, u32[]{:S(2)}) collective-permute-start(bf16[512,256]{1,0:T(8,128)(2,1)} %get-tuple-element.294), channel_id=1, source_target_pairs={{0,4},{1,6},{2,5},{3,7},{4,0},{5,2},{6,1},{7,3},{8,12},{9,14},{10,... | collective-permute-start | bytes 786440 | tf_op jit(solution)/shard_map/ppermute | solution.py:696
  67.0 37.6 %collective-permute-start.7 = (bf16[512,256]{1,0:T(8,128)(2,1)S(1)}, bf16[512,256]{1,0:T(8,128)(2,1)S(1)}, u32[]{:S(2)}, u32[]{:S(2)}) collective-permute-start(bf16[512,256]{1,0:T(8,128)(2,1)S(1)} %copy-done.38), channel_id=1, source_target_pairs={{0,5},{1,7},{2,0},{3,2},{4,1},{5,3},{6,4},{7,6},{8,13},{9,15},{10,... | collective-permute-start | bytes 786440 | tf_op jit(solution)/shard_map/ppermute | solution.py:696
  69.6 35.1 %collective-permute-start.6 = (bf16[512,256]{1,0:T(8,128)(2,1)S(1)}, bf16[512,256]{1,0:T(8,128)(2,1)S(1)}, u32[]{:S(2)}, u32[]{:S(2)}) collective-permute-start(bf16[512,256]{1,0:T(8,128)(2,1)S(1)} %get-tuple-element.292), channel_id=1, source_target_pairs={{0,0},{1,2},{2,1},{3,3},{4,4},{5,6},{6,5},{7,7},{8,8},{9,10},{10,9... | collective-permute-start | bytes 786440 | tf_op jit(solution)/shard_map/ppermute | solution.py:696
  71.5 34.7 %collective-permute-start.15 = (bf16[4,64,512]{2,1,0:T(8,128)(2,1)S(1)}, bf16[4,64,512]{2,1,0:T(8,128)(2,1)S(1)}, u32[]{:S(2)}, u32[]{:S(2)}) collective-permute-start(bf16[4,64,512]{2,1,0:T(8,128)(2,1)S(1)} %get-tuple-element.301), channel_id=1, source_target_pairs={{0,24},{8,16},{16,8},{24,0},{1,25},{9,17},{17,9},{25,1},{2,26},{10... | collective-permute-start | bytes 786440 | tf_op jit(solution)/shard_map/ppermute | solution.py:757
  71.6 34.6 %collective-permute-start.14 = (bf16[4,64,512]{2,1,0:T(8,128)(2,1)S(1)}, bf16[4,64,512]{2,1,0:T(8,128)(2,1)S(1)}, u32[]{:S(2)}, u32[]{:S(2)}) collective-permute-start(bf16[4,64,512]{2,1,0:T(8,128)(2,1)S(1)} %get-tuple-element.301), channel_id=1, source_target_pairs={{0,16},{8,24},{16,0},{24,8},{1,17},{9,25},{17,1},{25,9},{2,18},{10... | collective-permute-start | bytes 786440 | tf_op jit(solution)/shard_map/ppermute | solution.py:757
  87.1 19.2 %collective-permute-start.13 = (bf16[4,64,512]{2,1,0:T(8,128)(2,1)S(1)}, bf16[4,64,512]{2,1,0:T(8,128)(2,1)S(1)}, u32[]{:S(2)}, u32[]{:S(2)}) collective-permute-start(bf16[4,64,512]{2,1,0:T(8,128)(2,1)S(1)} %get-tuple-element.301), channel_id=1, source_target_pairs={{0,8},{8,0},{16,24},{24,16},{1,9},{9,1},{17,25},{25,17},{2,10},{10... | collective-permute-start | bytes 786440 | tf_op jit(solution)/shard_map/ppermute | solution.py:757
  125.7 24.4 %collective-permute-start.16 = (bf16[256,1024]{1,0:T(8,128)(2,1)S(1)}, bf16[256,1024]{1,0:T(8,128)(2,1)S(1)}, u32[]{:S(2)}, u32[]{:S(2)}) collective-permute-start(bf16[256,1024]{1,0:T(8,128)(2,1)S(1)} %fusion.13), channel_id=1, source_target_pairs={{0,1},{1,0},{2,3},{3,2},{4,5},{5,4},{6,7},{7,6},{8,9},{9,8},{10,11... | collective-permute-start | bytes 1572872 | tf_op jit(solution)/shard_map/ppermute | solution.py:731
  173.1 45.3 %collective-permute-start.17 = (bf16[640,1152]{1,0:T(8,128)(2,1)}, bf16[640,1152]{1,0:T(8,128)(2,1)S(1)}, u32[]{:S(2)}, u32[]{:S(2)}) collective-permute-start(bf16[640,1152]{1,0:T(8,128)(2,1)} %get-tuple-element.85), channel_id=1, source_target_pairs={{0,8},{8,0},{16,24},{24,16},{1,9},{9,1},{17,25},{25,17},{2,10},{10... | collective-permute-start | bytes 4423688 | tf_op jit(solution)/shard_map/ppermute | solution.py:757
  173.3 24.1 %collective-permute-start.19 = (bf16[256,1024]{1,0:T(8,128)(2,1)S(1)}, bf16[256,1024]{1,0:T(8,128)(2,1)S(1)}, u32[]{:S(2)}, u32[]{:S(2)}) collective-permute-start(bf16[256,1024]{1,0:T(8,128)(2,1)S(1)} %multiply_convert_fusion.1.refs_0_), channel_id=1, source_target_pairs={{0,2},{2,0},{4,6},{6,4},{1,3},{3,1},{5,7},{7,5},{8,10},{10,8},{12,... | collective-permute-start | bytes 1572872 | tf_op jit(solution)/shard_map/ppermute | solution.py:753
  173.4 38.2 %collective-permute-start.21 = (bf16[256,1024]{1,0:T(8,128)(2,1)S(1)}, bf16[256,1024]{1,0:T(8,128)(2,1)S(1)}, u32[]{:S(2)}, u32[]{:S(2)}) collective-permute-start(bf16[256,1024]{1,0:T(8,128)(2,1)S(1)} %multiply_convert_fusion.1.refs_0_), channel_id=1, source_target_pairs={{0,4},{2,6},{4,0},{6,2},{1,5},{3,7},{5,1},{7,3},{8,12},{10,14},{12... | collective-permute-start | bytes 1572872 | tf_op jit(solution)/shard_map/ppermute | solution.py:753
  174.7 37.0 %collective-permute-start.23 = (bf16[256,1024]{1,0:T(8,128)(2,1)S(1)}, bf16[256,1024]{1,0:T(8,128)(2,1)S(1)}, u32[]{:S(2)}, u32[]{:S(2)}) collective-permute-start(bf16[256,1024]{1,0:T(8,128)(2,1)S(1)} %multiply_convert_fusion.1.refs_0_), channel_id=1, source_target_pairs={{0,6},{2,4},{4,2},{6,0},{1,7},{3,5},{5,3},{7,1},{8,14},{10,12},{12... | collective-permute-start | bytes 1572872 | tf_op jit(solution)/shard_map/ppermute | solution.py:753
  177.7 40.7 %collective-permute-start.18 = (bf16[256,1024]{1,0:T(8,128)(2,1)S(1)}, bf16[256,1024]{1,0:T(8,128)(2,1)S(1)}, u32[]{:S(2)}, u32[]{:S(2)}) collective-permute-start(bf16[256,1024]{1,0:T(8,128)(2,1)S(1)} %multiply_convert_fusion.1.refs_0_), channel_id=1, source_target_pairs={{0,1},{1,0},{2,3},{3,2},{4,5},{5,4},{6,7},{7,6},{8,9},{9,8},{10,11... | collective-permute-start | bytes 1572872 | tf_op jit(solution)/shard_map/ppermute | solution.py:801
  197.4 22.1 %collective-permute-start.20 = (bf16[256,1024]{1,0:T(8,128)(2,1)S(1)}, bf16[256,1024]{1,0:T(8,128)(2,1)S(1)}, u32[]{:S(2)}, u32[]{:S(2)}) collective-permute-start(bf16[256,1024]{1,0:T(8,128)(2,1)S(1)} %collective-permute-done.19.refs_2_), channel_id=1, source_target_pairs={{0,1},{1,0},{2,3},{3,2},{4,5},{5,4},{6,7},{7,6},{8,9},{9,8},{10,11... | collective-permute-start | bytes 1572872 | tf_op jit(solution)/shard_map/ppermute | solution.py:801
  211.7 24.3 %collective-permute-start.24 = (bf16[256,1024]{1,0:T(8,128)(2,1)S(1)}, bf16[256,1024]{1,0:T(8,128)(2,1)}, u32[]{:S(2)}, u32[]{:S(2)}) collective-permute-start(bf16[256,1024]{1,0:T(8,128)(2,1)S(1)} %collective-permute-done.23.refs_6_), channel_id=1, source_target_pairs={{0,1},{1,0},{2,3},{3,2},{4,5},{5,4},{6,7},{7,6},{8,9},{9,8},{10,11... | collective-permute-start | bytes 1572872 | tf_op jit(solution)/shard_map/ppermute | solution.py:801
  236.0 126.3 %all-to-all-start = ((bf16[8,768,256]{2,1,0:T(8,128)(2,1)}), bf16[8,768,256]{2,1,0:T(8,128)(2,1)}, u32[]{:S(2)}, u32[]{:S(2)}) async-start(bf16[8,768,256]{2,1,0:T(8,128)(2,1)} %pad_maximum_fusion), calls=%async_computation | async-start | bytes 6291456 | tf_op jit(solution)/shard_map/all_to_all | solution.py:884
  241.9 35.7 %collective-permute-start.28 = (bf16[640,1152]{1,0:T(8,128)(2,1)}, bf16[640,1152]{1,0:T(8,128)(2,1)}, u32[]{:S(2)}, u32[]{:S(2)}) collective-permute-start(bf16[640,1152]{1,0:T(8,128)(2,1)} %get-tuple-element.102), channel_id=1, source_target_pairs={{0,16},{8,24},{16,0},{24,8},{1,17},{9,25},{17,1},{25,9},{2,18},{10... | collective-permute-start | bytes 4423688 | tf_op jit(solution)/shard_map/ppermute | solution.py:757
  244.1 64.7 %collective-permute-start.29 = (bf16[640,1152]{1,0:T(8,128)(2,1)}, bf16[640,1152]{1,0:T(8,128)(2,1)}, u32[]{:S(2)}, u32[]{:S(2)}) collective-permute-start(bf16[640,1152]{1,0:T(8,128)(2,1)} %get-tuple-element.103), channel_id=1, source_target_pairs={{0,24},{8,16},{16,8},{24,0},{1,25},{9,17},{17,9},{25,1},{2,26},{10... | collective-permute-start | bytes 4423688 | tf_op jit(solution)/shard_map/ppermute | solution.py:757
  256.5 52.3 %collective-permute-start.25 = (bf16[640,1024]{1,0:T(8,128)(2,1)}, bf16[640,1024]{1,0:T(8,128)(2,1)}, u32[]{:S(2)}, u32[]{:S(2)}) collective-permute-start(bf16[640,1024]{1,0:T(8,128)(2,1)} %get-tuple-element.97), channel_id=1, source_target_pairs={{0,8},{8,0},{16,24},{24,16},{1,9},{9,1},{17,25},{25,17},{2,10},{10... | collective-permute-start | bytes 3932168 | tf_op jit(solution)/shard_map/ppermute | solution.py:757
  256.7 80.6 %collective-permute-start.26 = (bf16[640,1024]{1,0:T(8,128)(2,1)}, bf16[640,1024]{1,0:T(8,128)(2,1)}, u32[]{:S(2)}, u32[]{:S(2)}) collective-permute-start(bf16[640,1024]{1,0:T(8,128)(2,1)} %get-tuple-element.98), channel_id=1, source_target_pairs={{0,16},{8,24},{16,0},{24,8},{1,17},{9,25},{17,1},{25,9},{2,18},{10... | collective-permute-start | bytes 3932168 | tf_op jit(solution)/shard_map/ppermute | solution.py:757
  258.7 103.7 %collective-permute-start.27 = (bf16[640,1024]{1,0:T(8,128)(2,1)}, bf16[640,1024]{1,0:T(8,128)(2,1)}, u32[]{:S(2)}, u32[]{:S(2)}) collective-permute-start(bf16[640,1024]{1,0:T(8,128)(2,1)} %get-tuple-element.99), channel_id=1, source_target_pairs={{0,24},{8,16},{16,8},{24,0},{1,25},{9,17},{17,9},{25,1},{2,26},{10... | collective-permute-start | bytes 3932168 | tf_op jit(solution)/shard_map/ppermute | solution.py:757
  410.9 161.1 %all-to-all-start.1 = ((bf16[8,768,256]{2,1,0:T(8,128)(2,1)}), bf16[8,768,256]{2,1,0:T(8,128)(2,1)}, u32[]{:S(2)}, u32[]{:S(2)}) async-start(bf16[8,768,256]{2,1,0:T(8,128)(2,1)} %get-tuple-element.121), calls=%async_computation.1 | async-start | bytes 6291456 | tf_op jit(solution)/shard_map/all_to_all | solution.py:900
  416.6 317.9 %reduce-scatter.2.cloned.1.call-start = ((), (), s32[]{:S(2)}) async-start(), calls=%async_computation.7 | async-start | bytes 4718592 | tf_op jit(solution)/shard_map/reduce_scatter | solution.py:965
  417.4 21.4 %collective-permute-start.31 = (bf16[640,640]{1,0:T(8,128)(2,1)}, bf16[640,640]{1,0:T(8,128)(2,1)}, u32[]{:S(2)}, u32[]{:S(2)}) collective-permute-start(bf16[640,640]{1,0:T(8,128)(2,1)} %get-tuple-element.106), channel_id=1, source_target_pairs={{0,16},{8,24},{16,0},{24,8},{1,17},{9,25},{17,1},{25,9},{2,18},{10... | collective-permute-start | bytes 2457608 | tf_op jit(solution)/shard_map/ppermute | solution.py:757
  419.2 35.8 %collective-permute-start.32 = (bf16[640,640]{1,0:T(8,128)(2,1)}, bf16[640,640]{1,0:T(8,128)(2,1)}, u32[]{:S(2)}, u32[]{:S(2)}) collective-permute-start(bf16[640,640]{1,0:T(8,128)(2,1)} %get-tuple-element.107), channel_id=1, source_target_pairs={{0,24},{8,16},{16,8},{24,0},{1,25},{9,17},{17,9},{25,1},{2,26},{10... | collective-permute-start | bytes 2457608 | tf_op jit(solution)/shard_map/ppermute | solution.py:757
  465.5 42.9 %collective-permute-start.33 = (bf16[4,256,640]{2,1,0:T(8,128)(2,1)}, bf16[4,256,640]{2,1,0:T(8,128)(2,1)}, u32[]{:S(2)}, u32[]{:S(2)}) collective-permute-start(bf16[4,256,640]{2,1,0:T(8,128)(2,1)} %get-tuple-element.109), channel_id=1, source_target_pairs={{0,1},{1,0},{2,3},{3,2},{4,5},{5,4},{6,7},{7,6},{8,9},{9,8},{10,11... | collective-permute-start | bytes 3932168 | tf_op jit(solution)/shard_map/ppermute | solution.py:902
  468.1 17.6 %collective-permute-start.35 = (bf16[640,512]{1,0:T(8,128)(2,1)S(1)}, bf16[640,512]{1,0:T(8,128)(2,1)S(1)}, u32[]{:S(2)}, u32[]{:S(2)}) collective-permute-start(bf16[640,512]{1,0:T(8,128)(2,1)S(1)} %copy-done.51), channel_id=1, source_target_pairs={{0,16},{8,24},{16,0},{24,8},{1,17},{9,25},{17,1},{25,9},{2,18},{10... | collective-permute-start | bytes 1966088 | tf_op jit(solution)/shard_map/ppermute | solution.py:757
  469.4 28.9 %collective-permute-start.36 = (bf16[640,512]{1,0:T(8,128)(2,1)S(1)}, bf16[640,512]{1,0:T(8,128)(2,1)S(1)}, u32[]{:S(2)}, u32[]{:S(2)}) collective-permute-start(bf16[640,512]{1,0:T(8,128)(2,1)S(1)} %copy-done.50), channel_id=1, source_target_pairs={{0,24},{8,16},{16,8},{24,0},{1,25},{9,17},{17,9},{25,1},{2,26},{10... | collective-permute-start | bytes 1966088 | tf_op jit(solution)/shard_map/ppermute | solution.py:757
  508.4 29.4 %collective-permute-start.37 = (bf16[4,256,512]{2,1,0:T(8,128)(2,1)}, bf16[4,256,512]{2,1,0:T(8,128)(2,1)}, u32[]{:S(2)}, u32[]{:S(2)}) collective-permute-start(bf16[4,256,512]{2,1,0:T(8,128)(2,1)} %get-tuple-element.117), channel_id=1, source_target_pairs={{0,1},{1,0},{2,3},{3,2},{4,5},{5,4},{6,7},{7,6},{8,9},{9,8},{10,11... | collective-permute-start | bytes 3145736 | tf_op jit(solution)/shard_map/ppermute | solution.py:906
  512.3 25.5 %collective-permute-start.39 = (bf16[256,640]{1,0:T(8,128)(2,1)S(1)}, bf16[256,640]{1,0:T(8,128)(2,1)S(1)}, u32[]{:S(2)}, u32[]{:S(2)}) collective-permute-start(bf16[256,640]{1,0:T(8,128)(2,1)S(1)} %get-tuple-element.259), channel_id=1, source_target_pairs={{0,4},{2,6},{4,0},{6,2},{1,5},{3,7},{5,1},{7,3},{8,12},{10,14},{12... | collective-permute-start | bytes 983048 | tf_op jit(solution)/shard_map/ppermute | solution.py:753
  514.7 23.2 %collective-permute-start.40 = (bf16[256,640]{1,0:T(8,128)(2,1)S(1)}, bf16[256,640]{1,0:T(8,128)(2,1)S(1)}, u32[]{:S(2)}, u32[]{:S(2)}) collective-permute-start(bf16[256,640]{1,0:T(8,128)(2,1)S(1)} %get-tuple-element.258), channel_id=1, source_target_pairs={{0,6},{2,4},{4,2},{6,0},{1,7},{3,5},{5,3},{7,1},{8,14},{10,12},{12... | collective-permute-start | bytes 983048 | tf_op jit(solution)/shard_map/ppermute | solution.py:753
  520.7 60.4 %collective-permute-start.45 = (bf16[640,1024]{1,0:T(8,128)(2,1)}, bf16[640,1024]{1,0:T(8,128)(2,1)}, u32[]{:S(2)}, u32[]{:S(2)}) collective-permute-start(bf16[640,1024]{1,0:T(8,128)(2,1)} %get-tuple-element.134), channel_id=1, source_target_pairs={{0,8},{8,0},{16,24},{24,16},{1,9},{9,1},{17,25},{25,17},{2,10},{10... | collective-permute-start | bytes 3932168 | tf_op jit(solution)/shard_map/ppermute | solution.py:757
  527.3 53.8 %collective-permute-start.46 = (bf16[640,1024]{1,0:T(8,128)(2,1)}, bf16[640,1024]{1,0:T(8,128)(2,1)}, u32[]{:S(2)}, u32[]{:S(2)}) collective-permute-start(bf16[640,1024]{1,0:T(8,128)(2,1)} %get-tuple-element.135), channel_id=1, source_target_pairs={{0,16},{8,24},{16,0},{24,8},{1,17},{9,25},{17,1},{25,9},{2,18},{10... | collective-permute-start | bytes 3932168 | tf_op jit(solution)/shard_map/ppermute | solution.py:757
  541.9 28.2 %collective-permute-start.42 = (bf16[256,512]{1,0:T(8,128)(2,1)S(1)}, bf16[256,512]{1,0:T(8,128)(2,1)S(1)}, u32[]{:S(2)}, u32[]{:S(2)}) collective-permute-start(bf16[256,512]{1,0:T(8,128)(2,1)S(1)} %get-tuple-element.267), channel_id=1, source_target_pairs={{0,4},{2,6},{4,0},{6,2},{1,5},{3,7},{5,1},{7,3},{8,12},{10,14},{12... | collective-permute-start | bytes 786440 | tf_op jit(solution)/shard_map/ppermute | solution.py:753
  554.4 31.5 %collective-permute-start.47 = (bf16[640,1024]{1,0:T(8,128)(2,1)}, bf16[640,1024]{1,0:T(8,128)(2,1)}, u32[]{:S(2)}, u32[]{:S(2)}) collective-permute-start(bf16[640,1024]{1,0:T(8,128)(2,1)} %get-tuple-element.136), channel_id=1, source_target_pairs={{0,24},{8,16},{16,8},{24,0},{1,25},{9,17},{17,9},{25,1},{2,26},{10... | collective-permute-start | bytes 3932168 | tf_op jit(solution)/shard_map/ppermute | solution.py:757
  577.4 19.6 %collective-permute-start.44 = (bf16[256,1024]{1,0:T(8,128)(2,1)S(1)}, bf16[256,1024]{1,0:T(8,128)(2,1)S(1)}, u32[]{:S(2)}, u32[]{:S(2)}) collective-permute-start(bf16[256,1024]{1,0:T(8,128)(2,1)S(1)} %get-tuple-element.254), channel_id=1, source_target_pairs={{0,1},{1,0},{2,3},{3,2},{4,5},{5,4},{6,7},{7,6},{8,9},{9,8},{10,11... | collective-permute-start | bytes 1572872 | tf_op jit(solution)/shard_map/ppermute | solution.py:734
  602.9 34.0 %all-to-all-start.2 = ((bf16[4,256,512]{2,1,0:T(8,128)(2,1)}), bf16[4,256,512]{2,1,0:T(8,128)(2,1)}, u32[]{:S(2)}, u32[]{:S(2)}) async-start(bf16[4,256,512]{2,1,0:T(8,128)(2,1)} %bitcast.85), calls=%async_computation.2 | async-start | bytes 2097152 | tf_op jit(solution)/shard_map/all_to_all | solution.py:952
  636.9 56.7 %all-to-all-start.3 = ((bf16[4,256,1152]{2,1,0:T(8,128)(2,1)}), bf16[4,256,1152]{2,1,0:T(8,128)(2,1)S(1)}, u32[]{:S(2)}, u32[]{:S(2)}) async-start(bf16[4,256,1152]{2,1,0:T(8,128)(2,1)} %bitcast.90), calls=%async_computation.3 | async-start | bytes 4718592 | tf_op jit(solution)/shard_map/all_to_all | solution.py:952
  651.7 19.2 %collective-permute-start.48 = (bf16[512,256]{1,0:T(8,128)(2,1)S(1)}, bf16[512,256]{1,0:T(8,128)(2,1)}, u32[]{:S(2)}, u32[]{:S(2)}) collective-permute-start(bf16[512,256]{1,0:T(8,128)(2,1)S(1)} %bitcast.228), channel_id=1, source_target_pairs={{0,0},{2,1},{1,2},{3,3},{4,4},{6,5},{5,6},{7,7},{8,8},{10,9},{9,10... | collective-permute-start | bytes 786440 | tf_op jit(solution)/shard_map/ppermute | solution.py:713
  653.1 36.5 %collective-permute-start.49 = (bf16[512,256]{1,0:T(8,128)(2,1)S(1)}, bf16[512,256]{1,0:T(8,128)(2,1)}, u32[]{:S(2)}, u32[]{:S(2)}) collective-permute-start(bf16[512,256]{1,0:T(8,128)(2,1)S(1)} %bitcast.229), channel_id=1, source_target_pairs={{5,0},{7,1},{0,2},{2,3},{1,4},{3,5},{4,6},{6,7},{13,8},{15,9},{8,1... | collective-permute-start | bytes 786440 | tf_op jit(solution)/shard_map/ppermute | solution.py:713
  665.5 24.1 %collective-permute-start.50 = (bf16[512,256]{1,0:T(8,128)(2,1)S(1)}, bf16[512,256]{1,0:T(8,128)(2,1)}, u32[]{:S(2)}, u32[]{:S(2)}) collective-permute-start(bf16[512,256]{1,0:T(8,128)(2,1)S(1)} %bitcast.230), channel_id=1, source_target_pairs={{4,0},{6,1},{5,2},{7,3},{0,4},{2,5},{1,6},{3,7},{12,8},{14,9},{13,... | collective-permute-start | bytes 786440 | tf_op jit(solution)/shard_map/ppermute | solution.py:713
  669.5 20.1 %collective-permute-start.51 = (bf16[512,256]{1,0:T(8,128)(2,1)S(1)}, bf16[512,256]{1,0:T(8,128)(2,1)}, u32[]{:S(2)}, u32[]{:S(2)}) collective-permute-start(bf16[512,256]{1,0:T(8,128)(2,1)S(1)} %bitcast.231), channel_id=1, source_target_pairs={{1,0},{3,1},{4,2},{6,3},{5,4},{7,5},{0,6},{2,7},{9,8},{11,9},{12,1... | collective-permute-start | bytes 786440 | tf_op jit(solution)/shard_map/ppermute | solution.py:713
  695.3 39.0 %all-to-all-start.4 = ((bf16[4,64,1664]{2,1,0:T(8,128)(2,1)}), bf16[4,64,1664]{2,1,0:T(8,128)(2,1)S(1)}, u32[]{:S(2)}, u32[]{:S(2)}) async-start(bf16[4,64,1664]{2,1,0:T(8,128)(2,1)} %pad_maximum_fusion.9), calls=%async_computation.4 | async-start | bytes 1703936 | tf_op jit(solution)/shard_map/all_to_all | solution.py:958
  (65 other events, 1125.0 us)
Sparse Core Ops, SparseCore 0:
  61.8 97.6 all-gather.1
  600.0 111.3 reduce-scatter.1

commit v3 on v2

--- a/solution.py
+++ b/solution.py
@@ -206,6 +206,34 @@
     value_out[...] = grad_value.astype(bf16)
 
 
+def in_vmem(count):
+    return [pl.BlockSpec(memory_space=pltpu.VMEM) for _ in range(count)]
+
+
+def weight_products_kernel(mid_ref, heads_ref, small_ref, left_ref, *refs):
+    *right_refs, out_ref = refs
+    start = heads_ref.shape[1]
+    out_ref[:, :start] = dot_tn(mid_ref[...], heads_ref[...]).astype(bf16)
+    out_ref[:, start : start + LANES] = small_ref[...]
+    start += LANES
+    for right in right_refs:
+        stop = start + right.shape[1]
+        out_ref[:, start:stop] = dot_tn(left_ref[...], right[...]).astype(bf16)
+        start = stop
+
+
+def weight_products(mid, heads, small, left, rights):
+    cols = heads.shape[1] + LANES + sum(right.shape[1] for right in rights)
+    return pl.pallas_call(
+        weight_products_kernel,
+        in_specs=in_vmem(4 + len(rights)),
+        out_specs=in_vmem(1)[0],
+        out_shape=jax.ShapeDtypeStruct((left.shape[1], cols), bf16),
+        compiler_params=BIG,
+        name="weight_products",
+    )(mid, heads, small, left, *rights)
+
+
 def attend_backward(query, key, value, sums, grad, tables, seg_col, seg_row, block):
     seq_len = query.shape[0]
     width = key.shape[1]
@@ -423,6 +451,15 @@
     )(own, starts, places, addition, *values)
 
 
+def weight_blocks(row_count, col_count, part, hidden_cols):
+    for row in range(row_count):
+        for col in range(col_count):
+            rows = slice(row * part, (row + 1) * part)
+            cols = slice(col * part, (col + 1) * part)
+            above = slice(hidden_cols + col * part, hidden_cols + (col + 1) * part)
+            yield row * col_count + col, rows, cols, above
+
+
 def expert_kernel(
     weight_ref, router_ref, pick_ref, *refs, groups, row_count, col_count
 ):
@@ -430,11 +467,9 @@
     out_refs, back_a_refs, back_b_refs = (
         refs[at * groups : (at + 1) * groups] for at in (2, 3, 4)
     )
-    grad_weight_ref, up_ref, down_ref, grad_up_ref, grad_down_ref, slot_ref, grad_ref = refs[
-        5 * groups :
-    ]
+    save_refs = refs[5 * groups : 6 * groups]
+    up_ref, down_ref, slot_ref, grad_ref = refs[6 * groups :]
     step = pl.program_id(0) * pl.num_programs(1) + pl.program_id(1)
-    last = pl.num_programs(0) * pl.num_programs(1) - 1
     width = slot_ref.shape[1]
     split = back_b_refs[0].shape[1]
     for group in range(groups):
@@ -447,22 +482,12 @@
     hidden_cols = down_ref.shape[0]
     part = weight_ref.shape[2]
 
-    def blocks():
-        for row in range(row_count):
-            for col in range(col_count):
-                rows = slice(row * part, (row + 1) * part)
-                cols = slice(col * part, (col + 1) * part)
-                above = slice(hidden_cols + col * part, hidden_cols + (col + 1) * part)
-                yield row * col_count + col, rows, cols, above
-
     @pl.when(step == 0)
     def _():
-        for cell, rows, cols, above in blocks():
+        for cell, rows, cols, above in weight_blocks(row_count, col_count, part, hidden_cols):
             up_ref[rows, cols] = weight_ref[cell, :part, :]
             up_ref[rows, above] = weight_ref[cell, part : 2 * part, :]
             down_ref[cols, rows] = weight_ref[cell, 2 * part :, :]
-        grad_up_ref[...] = jnp.zeros_like(grad_up_ref)
-        grad_down_ref[...] = jnp.zeros_like(grad_down_ref)
 
     slots = slot_ref[...]
     grads = grad_ref[:, :width].astype(f32)
@@ -502,16 +527,46 @@
             back_a_refs[group][:, :LANES] = split_dots
             back_a_refs[group][:, LANES:] = back[:, : width - split]
             back_b_refs[group][...] = back[:, width - split :]
-
-    grad_up_ref[...] += dot_tn(slots, grad_pair)
-    grad_down_ref[...] += dot_tn(hidden, grad_expert)
-
-    @pl.when(step == last)
-    def _():
-        for cell, rows, cols, above in blocks():
-            grad_weight_ref[cell, :part, :] = grad_up_ref[rows, cols].astype(bf16)
-            grad_weight_ref[cell, part : 2 * part, :] = grad_up_ref[rows, above].astype(bf16)
-            grad_weight_ref[cell, 2 * part :, :] = grad_down_ref[cols, rows].astype(bf16)
+            save_refs[group][:, :hidden_cols] = hidden
+            save_refs[group][:, hidden_cols : hidden_cols + width] = grad_expert
+            save_refs[group][:, hidden_cols + width :] = grad_pair
+
+
+def expert_grads_kernel(*refs, groups, row_count, col_count):
+    slot_refs, save_refs, out_ref = refs[:groups], refs[groups : 2 * groups], refs[2 * groups]
+    part = out_ref.shape[2]
+    width = slot_refs[0].shape[1]
+    hidden_cols = col_count * part
+    first_pair = hidden_cols + width
+
+    def product(lefts, left_cols, rights, right_cols):
+        terms = [
+            dot_tn(left[:, left_cols], right[:, right_cols]) for left, right in zip(lefts, rights)
+        ]
+        return sum(terms).astype(bf16)
+
+    for cell, rows, cols, above in weight_blocks(row_count, col_count, part, hidden_cols):
+        for place, pair in enumerate((cols, above)):
+            pair = slice(first_pair + pair.start, first_pair + pair.stop)
+            out_ref[cell, place * part : (place + 1) * part, :] = product(
+                slot_refs, rows, save_refs, pair
+            )
+        out = slice(hidden_cols + rows.start, hidden_cols + rows.stop)
+        out_ref[cell, 2 * part :, :] = product(save_refs, cols, save_refs, out)
+
+
+def expert_grads(slots, saved, shape, row_count, col_count):
+    groups = len(slots)
+    return pl.pallas_call(
+        functools.partial(
+            expert_grads_kernel, groups=groups, row_count=row_count, col_count=col_count
+        ),
+        in_specs=in_vmem(2 * groups),
+        out_specs=in_vmem(1)[0],
+        out_shape=jax.ShapeDtypeStruct(shape, bf16),
+        compiler_params=BIG,
+        name="expert_grads",
+    )(*slots, *saved)
 
 
 def run_expert(slots, grads, weights, router, pick, steps, row_count, col_count):
@@ -521,6 +576,7 @@
     half = width // 2
     block = capacity // steps
     hidden_cols = weights.shape[2] * col_count
+    kept = 3 * hidden_cols + width
     whole = lambda shape: pl.BlockSpec(shape, lambda i, j: (0,) * len(shape))
 
     def some(cols):
@@ -544,16 +600,14 @@
         in_specs=[whole(weights.shape), whole(router.shape), whole(pick.shape)]
         + some(width)
         + some(rest),
-        out_specs=some(width) + some(half + LANES) + some(half) + [whole(weights.shape)],
+        out_specs=some(width) + some(half + LANES) + some(half) + some(kept),
         out_shape=shapes(width)
         + shapes(half + LANES)
         + shapes(half)
-        + [jax.ShapeDtypeStruct(weights.shape, bf16)],
+        + shapes(kept),
         scratch_shapes=[
             pltpu.VMEM((width, 2 * hidden_cols), bf16),
             pltpu.VMEM((hidden_cols, width), bf16),
-            pltpu.VMEM((width, 2 * hidden_cols), f32),
-            pltpu.VMEM((hidden_cols, width), f32),
             pltpu.VMEM((block, width), bf16),
             pltpu.VMEM((block, rest), bf16),
         ],
@@ -564,7 +618,7 @@
         outs[:groups],
         outs[groups : 2 * groups],
         outs[2 * groups : 3 * groups],
-        outs[3 * groups],
+        outs[3 * groups :],
     )
 
 
@@ -783,22 +837,24 @@
             1,
         )
     )
-    first_weights, grad_late = lax.optimization_barrier((first_weights, grad_out))
-    grad_stack = lax.all_gather(grad_late, ("row", "col"), axis=0, tiled=True).reshape(
+    first_weights, out_late = lax.optimization_barrier((first_weights, output_weight))
+    out_weight = all_rows(out_late.T)
+    grad_stack = lax.all_gather(grad_out, ("row", "col"), axis=0, tiled=True).reshape(
         row_count, group, local_width
     )
 
     qkv_weight = first_weights[:, :qkv_cols]
     extras = first_weights[:, qkv_cols:]
-    out_weight = all_rows(output_weight.T)
     router_pad = jnp.where(jnp.arange(LANES)[None, :] < experts, extras, jnp.zeros((), bf16))
     router = extras[:, :experts]
     terms = extras[:, experts : experts + 6].astype(f32)
     gain_one = (terms[:, 0] + terms[:, 1] + terms[:, 2])[None, :]
     gain_two = (terms[:, 3] + terms[:, 4] + terms[:, 5])[None, :]
-    def from_cells(array):
-        rows = [over_rows(array, turn) for turn in range(row_count)]
-        return [(block, lax.ppermute(block, "col", mirror)) for block in rows]
+    def from_rows(array):
+        return [over_rows(array, turn) for turn in range(row_count)]
+
+    def from_columns(rows):
+        return [block for row in rows for block in (row, lax.ppermute(row, "col", mirror))]
 
     member = jnp.any(
         expert_ids[:, :, None] == jnp.arange(experts, dtype=jnp.int32)[None, None, :], 1
@@ -861,15 +917,13 @@
     inv_two = inverse_rms(middle)
     normed_two = (middle * inv_two * gain_two).astype(bf16)
     half = width // 2
-    pieces_two = from_cells(normed_two)
-    blocks = [block for pair in pieces_two for block in pair]
-    grad_sent = dispatch_grads(
-        starts_grad, places_grad, grad_stack, member_pad, capacity, own_rows
-    )
-    grad_slots = exchange(grad_sent)
-    grad_slots[0], grad_slots[1], blocks[0] = lax.optimization_barrier(
-        (grad_slots[0], grad_slots[1], blocks[0])
-    )
+    early = spread - 1
+    grad_slots = exchange(
+        dispatch_grads(starts_grad, places_grad, grad_stack, member_pad, capacity, own_rows)
+    )
+    normed_sent, *grad_slots[:2] = lax.optimization_barrier((normed_two, *grad_slots[:2]))
+    blocks = from_columns(from_rows(normed_sent))
+    blocks[0], *grad_slots = lax.optimization_barrier((blocks[0], *grad_slots))
 
     def own_share(weight):
         split = weight.reshape((copies, spread, per_dp) + weight.shape[1:])
@@ -884,7 +938,7 @@
     expert_weights = lax.all_to_all(shares, ("row", "col"), 0, 0, tiled=True)
 
     slots = exchange(dispatch_two(starts_two, places_two, blocks, capacity))
-    results, back_a, back_b, grad_blocks = run_expert(
+    results, back_a, back_b, saved = run_expert(
         slots, grad_slots, expert_weights, router_pad, pick, 2, row_count, col_count
     )
 
@@ -897,33 +951,38 @@
     def row_parts(sums):
         return [over_rows(sums[turn].astype(bf16), turn) for turn in range(1, row_count)]
 
+    back_a, saved = exchange(back_a), list(saved)
+    back_b = exchange(back_b)
+    *back_a[:2], saved[0] = lax.optimization_barrier((*back_a[:2], saved[0]))
+    back_a[0], *back_b[:early] = lax.optimization_barrier((back_a[0], *back_b[:early]))
+    kept_a, away_a = to_cells(back_a)
+    grad_blocks = expert_grads(slots, saved, shares.shape, row_count, col_count)
     grad_got = lax.all_to_all(grad_blocks, ("row", "col"), 0, 0, tiled=True)
-    kept_a, away_a = to_cells(exchange(back_a))
     away_a = lax.ppermute(away_a, "col", mirror)
-    back_b = exchange(back_b)
     kept_b, away_b = to_cells(back_b)
     away_a, kept_b, away_b = lax.optimization_barrier((away_a, kept_b, away_b))
     away_b = lax.ppermute(away_b, "col", mirror)
     sums_a = half_sums(kept_a, away_a)
     parts_a = row_parts(sums_a)
-    away_b, *parts_a = lax.optimization_barrier((away_b, *parts_a))
+    back_b[0], *results = lax.optimization_barrier((back_b[0], *results))
+    results = exchange(results)
+    away_b, parts_a, results[:early] = lax.optimization_barrier(
+        (away_b, parts_a, results[:early])
+    )
     sums_b = half_sums(kept_b, away_b)
     parts_b = row_parts(sums_b)
+    mixed_rows = combine_add(
+        own_block.reshape(1), starts_all, places_all, results, middle, row_count
+    )
+    parts_b, mixed_rows = lax.optimization_barrier((parts_b, mixed_rows))
     own_a = sums_a[0] + sum(part.astype(f32) for part in parts_a)
     own_b = sums_b[0] + sum(part.astype(f32) for part in parts_b)
-    own_a, grad_got = lax.optimization_barrier((own_a, grad_got))
 
     if copies > 1:
         grad_got = lax.psum_scatter(
             grad_got, "dp", scatter_dimension=0, axis_index_groups=far, tiled=True
         )
-    grad_gate, grad_up, grad_down = spread_blocks(grad_got, 3)
-
-    back_b, results = lax.optimization_barrier((back_b, results))
-    results = exchange(results)
-    mixed_rows = combine_add(
-        own_block.reshape(1), starts_all, places_all, results, middle, row_count
-    )
+
     own_member = lax.dynamic_slice_in_dim(member, own_block * own_rows, own_rows, 0)
     logits = jnp.where(own_member, dot(normed_two, router), masked_score)
     powers = jnp.where(own_member, jnp.exp(logits - jnp.max(logits, -1, keepdims=True)), 0.0)
@@ -943,23 +1002,34 @@
     )
     grad_middle = own_grad.astype(f32) + grad_norm
 
-    def dp_sums(*columns):
-        stacked = jnp.concatenate([column.astype(bf16) for column in columns], 1)
-        stacked = jnp.pad(stacked, ((0, 0), (0, -stacked.shape[1] % LANES)))
-        cols = stacked.shape[1]
-        share = local_width // dp_count
-        parts = stacked.reshape(row_count, dp_count, share, cols).swapaxes(0, 1)
-        parts = lax.all_to_all(
-            parts.reshape(dp_count, row_count * share, cols), "dp", 0, 0, tiled=True
-        )
-        return jnp.sum(parts.astype(f32), 0).astype(bf16).reshape(row_count, share, cols)
+    share_rows = local_width // dp_count
+    by_share = lambda array: array.reshape(
+        array.shape[0], row_count, dp_count, share_rows
+    ).swapaxes(1, 2).reshape(array.shape)
+
+    def dp_sums(stacked):
+        parts = stacked.reshape(dp_count, row_count * share_rows, stacked.shape[1])
+        parts = lax.all_to_all(parts, "dp", 0, 0, tiled=True)
+        summed = jnp.sum(parts.astype(f32), 0)
+        return summed.reshape(row_count, share_rows, stacked.shape[1])
 
     def row_sums(parts):
         parts = lax.all_to_all(parts, "row", 0, 0, tiled=True)
-        return jnp.sum(parts.astype(f32), 0).astype(bf16)
+        return jnp.sum(parts.astype(f32), 0)
+
+    def in_two(array):
+        high = array.astype(bf16)
+        low = (array - high.astype(f32)).astype(bf16)
+        pad = ((0, 0),) * (array.ndim - 1) + ((0, LANES - 2 * array.shape[-1]),)
+        return jnp.pad(jnp.concatenate([high, low], -1), pad)
+
+    smalls = experts + 1
+    of_two = lambda array: array[..., :smalls] + array[..., smalls : 2 * smalls]
 
     grad_mid = join_halves(grad_middle.astype(bf16))
-    out_sums = dp_sums(dot_tn(grad_mid, heads))
+    grad_mid, grad_got = lax.optimization_barrier((grad_mid, grad_got))
+    grad_gate, grad_up, grad_down = spread_blocks(grad_got, 3)
+    small = jnp.concatenate([grad_router, grad_gain_two[:, None]], 1)
     grad_heads = dot(grad_mid, out_weight).astype(bf16)
     grad_heads, mixed_rows = lax.optimization_barrier((grad_heads, mixed_rows))
     mixed_out = lax.psum_scatter(
@@ -968,28 +1038,41 @@
         scatter_dimension=0,
         tiled=True,
     )
-    grad_qkv = jnp.concatenate(
-        attend_backward(
-            query_low, key_low, value_low, log_sums, grad_heads, tables, seg_col, segments, block
-        ),
-        1,
-    )
+    grad_qkv = attend_backward(
+        query_low, key_low, value_low, log_sums, grad_heads, tables, seg_col, segments, block
+    )
+    small = in_two(by_share(small.T).T)
+    sums = dp_sums(
+        weight_products(by_share(grad_mid), heads, small, by_share(normed_one), grad_qkv)
+    )
+    grad_qkv = jnp.concatenate(grad_qkv, 1)
     grad_one = dot_nt(grad_qkv, qkv_weight)
-    grad_part, grad_gain_one = norm_back(grad_one, residual, inv_one, gain_one)
+    grad_part, _ = norm_back(grad_one, residual, inv_one, gain_one)
     at_own = lax.dynamic_slice_in_dim(grad_part, own_start, own_rows, 0) + grad_middle
     grad_part = lax.dynamic_update_slice_in_dim(grad_part, at_own, own_start, 0)
     grad_in = from_sequences(grad_part.astype(bf16))
-    qkv_sums = dp_sums(
-        dot_tn(normed_one, grad_qkv), grad_router, grad_gain_two[:, None], grad_gain_one[:, None]
-    )
-    qkv_sums, grad_in = lax.optimization_barrier((qkv_sums, grad_in))
-    summed = row_sums(jnp.concatenate([out_sums, qkv_sums], 2))
+    main = query_cols + LANES
+
+    def rounded(sums):
+        return jnp.concatenate(
+            [
+                sums[..., :query_cols].astype(bf16),
+                in_two(of_two(sums[..., query_cols:main])),
+                sums[..., main:].astype(bf16),
+            ],
+            -1,
+        )
+
+    sums, grad_in = lax.optimization_barrier((rounded(sums), grad_in))
+    summed = rounded(row_sums(sums))
     summed, mixed_out = lax.optimization_barrier((summed, mixed_out))
-    summed = lax.all_gather(summed, "dp", axis=0, tiled=True)
-    also = summed[:, -LANES:]
-    also = also.astype(f32) + lax.ppermute(also, "col", mirror).astype(f32)
-    out_sum = summed[:, :query_cols].astype(f32)
-    qkv_sum = summed[:, query_cols:-LANES].astype(f32)
+    summed = lax.all_gather(summed, "dp", axis=0, tiled=True).astype(f32)
+    out_sum = summed[:, :query_cols]
+    qkv_sum = summed[:, main:]
+    weights = jnp.concatenate([query_weight, key_weight, value_weight], 1).astype(f32)
+    small_gain = jnp.sum(weights * qkv_sum, 1) / norm1_gain
+    also = jnp.concatenate([of_two(summed[:, query_cols:main]), small_gain[:, None]], 1)
+    also = also + lax.ppermute(also, "col", mirror)
     return (
         mixed_out,
         grad_in,

time: 765 us -> 694 us (0.907)
  waiting for transfers between devices: 365 us -> 314 us
  starting transfers between devices: 126 us -> 97.2 us
  Pallas kernels: 131 us -> 144 us
    ppermute x21, waiting for transfers between devices: 191 us -> 146 us  [over_dp(): return lax.ppermute(array, 'dp', pairs) if turn else array]
    pallas_call x0 -> x2, Pallas kernels: none -> 23.6 us  [the longest x1 17.9 us: expert_grads(): pl.pallas_call(functools.partial(expert_grads_kernel, groups=groups, row_...]
    ppermute x4, waiting for transfers between devices: 31.9 us -> 18.9 us  [to_sequences(): got.append(lax.ppermute(own, ('row', 'col'), there))]
    all_to_all x1, waiting for transfers between devices: 14.4 us -> 26.9 us  [row_sums(): parts = lax.all_to_all(parts, 'row', 0, 0, tiled=True)]
    pallas_call x1, Pallas kernels: 48.6 us -> 36 us  [run_expert(): pl.pallas_call(functools.partial(expert_kernel, groups=groups, row_count=...]
    all_to_all x1, starting transfers between devices: 18.1 us -> 6.58 us  [row_sums(): parts = lax.all_to_all(parts, 'row', 0, 0, tiled=True)]
    ppermute x1, waiting for transfers between devices: 0.01 us -> 8.79 us  [join_halves(): other = lax.ppermute(array, 'col', mirror)]
    ppermute x1, starting transfers between devices: 10 us -> 1.52 us  [sum_halves(): return own + lax.ppermute(away, 'col', mirror).astype(f32)]
  transfers between devices with their start and end apart: 60 -> 59, of which waited for: 27 -> 25; matrix products, arithmetic and copies ran while one was open for 12% -> 13% of each run, Pallas kernels for 9% -> 14%
where the time goes in v3:
time: 694 us; the launch traced here: 685 us
  waiting for transfers between devices  314 us (45%)
  Pallas kernels  144 us (21%)
  starting transfers between devices  97.2 us (14%)
  local copies, waits for them, and re-layouts  52.3 us (8%)
  other arithmetic  38.7 us (6%)
  between operations  16.1 us (2%)
  matrix products  14.4 us (2%)
  blocking collectives  8.93 us (1%)
    ppermute x21, waiting for transfers between devices, over_dp(): return lax.ppermute(array, 'dp', pairs) if turn else array  146 us
    ppermute x15, waiting for transfers between devices, over_rows(): return lax.ppermute(array, 'row', pairs) if turn else array  68.1 us
    pallas_call x1, Pallas kernels, run_expert(): pl.pallas_call(functools.partial(expert_kernel, groups=groups, row_count=...  36 us
    ppermute x15, starting transfers between devices, over_rows(): return lax.ppermute(array, 'row', pairs) if turn else array  29.8 us
    all_to_all x1, waiting for transfers between devices, row_sums(): parts = lax.all_to_all(parts, 'row', 0, 0, tiled=True)  26.9 us
    pallas_call x2, Pallas kernels, dispatch(): pl.pallas_call(kernel, grid=(count,), in_specs=[pl.BlockSpec(memory_space...  24.9 us
    pallas_call x2, Pallas kernels, combine(): pl.pallas_call(functools.partial(combine_kernel, capacity=capacity), grid...  20.1 us
    ppermute x4, waiting for transfers between devices, to_sequences(): got.append(lax.ppermute(own, ('row', 'col'), there))  18.9 us
  transfers between devices with their start and end apart: 59, of which 25 were waited for; matrix products, arithmetic and copies ran while one was open for 13% of the time, Pallas kernels for 14%

profile of v3, /device:TPU:0, one launch (start us, length us, event | category | flops | bytes accessed | tf_op | source)
XLA Modules:
  0.0 685.2 jit_solution(10977936126356169821)
XLA Ops:
  10.6 5.1 collective-permute-start.6
  31.9 15.9 %collective-permute-done.5 = bf16[64,1152]{1,0:T(8,128)(2,1)} collective-permute-done((bf16[64,1152]{1,0:T(8,128)(2,1)S(1)}, bf16[64,1152]{1,0:T(8,128)(2,1)}, u32[]{:S(2)}, u32[]{:S(2)}) %collective-permute-start.5) | collective-permute-done | bytes 147488 | tf_op jit(solution)/shard_map/ppermute | solution.py:807
  52.1 10.1 %collective-permute-done.2 = bf16[512,256]{0,1:T(8,128)(2,1)} collective-permute-done((bf16[512,256]{0,1:T(8,128)(2,1)S(1)}, bf16[512,256]{0,1:T(8,128)(2,1)}, u32[]{:S(2)}, u32[]{:S(2)}) %collective-permute-start.2) | collective-permute-done | bytes 262176 | tf_op jit(solution)/shard_map/ppermute | solution.py:750
  62.2 8.8 %collective-permute-done.1 = bf16[512,256]{0,1:T(8,128)(2,1)S(1)} collective-permute-done((bf16[512,256]{0,1:T(8,128)(2,1)S(1)}, bf16[512,256]{0,1:T(8,128)(2,1)S(1)}, u32[]{:S(2)}, u32[]{:S(2)}) %collective-permute-start.1) | collective-permute-done | bytes 262176 | tf_op jit(solution)/shard_map/ppermute | solution.py:750
  73.6 5.5 collective-permute-done.8
  84.0 4.6 collective-permute-start.12
  92.9 10.0 %collective-permute-done.11 = bf16[64,512]{1,0:T(8,128)(2,1)S(1)} collective-permute-done((bf16[64,512]{1,0:T(8,128)(2,1)S(1)}, bf16[64,512]{1,0:T(8,128)(2,1)S(1)}, u32[]{:S(2)}, u32[]{:S(2)}) %collective-permute-start.11) | collective-permute-done | bytes 65568 | tf_op jit(solution)/shard_map/ppermute | solution.py:807
  107.6 10.6 %attend_forward.1 = (bf16[512,512]{1,0:T(8,128)(2,1)}, bf16[512,256]{1,0:T(8,128)(2,1)}, bf16[512,256]{1,0:T(8,128)(2,1)}, bf16[512,512]{1,0:T(8,128)(2,1)}, f32[512,256]{1,0:T(8,128)}) custom-call(f32[512,1024]{1,0:T(8,128)} %fusion.3.query_in.key_in.value_in, f32[512,1024]{1,0:T(8,128)} %fusion.3.query_in.key_in.value_in, ...), custom_call_target="tpu_custom_call" | custom-call | tf_op jit(solution)/shard_map/attend_forward/pallas_call | solution.py:129
  118.8 6.3 all-gather.2.cloned.1.call-done
  125.1 13.5 %dispatch_grads.1 = (bf16[640,1152]{1,0:T(8,128)(2,1)}, bf16[640,1152]{1,0:T(8,128)(2,1)}, bf16[640,1152]{1,0:T(8,128)(2,1)}, bf16[640,1152]{1,0:T(8,128)(2,1)}) custom-call(s32[32]{0:T(128)} %reshape.379.starts_ref, s32[4,1,2048]{2,1,0:T(1,128)} %copy.422.place_ref, bf16[4,2048,256]{2,1,0:T(8,128)(2,1)} %bitcast.214, ...), custom_call_target="tpu_custom_call" | custom-call | tf_op jit(solution)/shard_map/dispatch_grads/pallas_call | solution.py:328
  143.9 9.9 %collective-permute-done.16 = bf16[256,1024]{1,0:T(8,128)(2,1)S(1)} collective-permute-done((bf16[256,1024]{1,0:T(8,128)(2,1)S(1)}, bf16[256,1024]{1,0:T(8,128)(2,1)S(1)}, u32[]{:S(2)}, u32[]{:S(2)}) %collective-permute-start.16) | collective-permute-done | bytes 524320 | tf_op jit(solution)/shard_map/ppermute | solution.py:785
  159.8 16.6 %collective-permute-done.18.refs_6_ = bf16[640,1152]{1,0:T(8,128)(2,1)} collective-permute-done((bf16[640,1152]{1,0:T(8,128)(2,1)}, bf16[640,1152]{1,0:T(8,128)(2,1)}, u32[]{:S(2)}, u32[]{:S(2)}) %collective-permute-start.18) | collective-permute-done | bytes 1474592 | tf_op jit(solution)/shard_map/ppermute | solution.py:811
  181.4 12.3 %collective-permute-done.23.refs_4_ = bf16[256,1024]{1,0:T(8,128)(2,1)S(1)} collective-permute-done((bf16[256,1024]{1,0:T(8,128)(2,1)S(1)}, bf16[256,1024]{1,0:T(8,128)(2,1)S(1)}, u32[]{:S(2)}, u32[]{:S(2)}) %collective-permute-start.23) | collective-permute-done | bytes 524320 | tf_op jit(solution)/shard_map/ppermute | solution.py:807
  200.6 5.9 collective-permute-done.19.refs_7_
  207.6 6.2 collective-permute-done.24.refs_5_
  214.5 8.2 %collective-permute-done.26.refs_7_ = bf16[256,1024]{1,0:T(8,128)(2,1)} collective-permute-done((bf16[256,1024]{1,0:T(8,128)(2,1)S(1)}, bf16[256,1024]{1,0:T(8,128)(2,1)}, u32[]{:S(2)}, u32[]{:S(2)}) %collective-permute-start.26) | collective-permute-done | bytes 524320 | tf_op jit(solution)/shard_map/ppermute | solution.py:857
  222.7 3.8 all-to-all-start
  229.1 11.4 %dispatch_tokens.1 = (bf16[640,1024]{1,0:T(8,128)(2,1)}, bf16[640,1024]{1,0:T(8,128)(2,1)}, bf16[640,1024]{1,0:T(8,128)(2,1)}, bf16[640,1024]{1,0:T(8,128)(2,1)}) custom-call(s32[32]{0:T(128)} %reshape.387.starts_ref, s32[4,1,2048]{2,1,0:T(1,128)} %reshape.389.place_ref, bf16[256,1024]{1,0:T(8,128)(2,1)} %copy-done.7, bf16[256,1024]{1,0:T(8,128)(2,1)} %copy-done.40, ...), custom_call_target="tpu_custom_call" | custom-call | tf_op jit(solution)/shard_map/dispatch_tokens/pallas_call | solution.py:328
  244.8 27.7 %collective-permute-done.28.refs_2_ = bf16[640,1024]{1,0:T(8,128)(2,1)} collective-permute-done((bf16[640,1024]{1,0:T(8,128)(2,1)}, bf16[640,1024]{1,0:T(8,128)(2,1)}, u32[]{:S(2)}, u32[]{:S(2)}) %collective-permute-start.28) | collective-permute-done | bytes 1310752 | tf_op jit(solution)/shard_map/ppermute | solution.py:811
  272.5 27.2 %collective-permute-done.29.refs_3_ = bf16[640,1024]{1,0:T(8,128)(2,1)} collective-permute-done((bf16[640,1024]{1,0:T(8,128)(2,1)}, bf16[640,1024]{1,0:T(8,128)(2,1)}, u32[]{:S(2)}, u32[]{:S(2)}) %collective-permute-start.29) | collective-permute-done | bytes 1310752 | tf_op jit(solution)/shard_map/ppermute | solution.py:811
  301.3 36.0 %expert_pass.1 = (bf16[640,1024]{1,0:T(8,128)(2,1)}, bf16[640,1024]{1,0:T(8,128)(2,1)}, bf16[640,1024]{1,0:T(8,128)(2,1)}, bf16[640,1024]{1,0:T(8,128)(2,1)}, bf...) custom-call(bf16[8,768,256]{2,1,0:T(8,128)(2,1)} %copy-done.5, ...), custom_call_target="tpu_custom_call" | custom-call | tf_op jit(solution)/shard_map/expert_pass/pallas_call | solution.py:595
  341.4 17.9 %expert_grads.1 = bf16[8,768,256]{2,1,0:T(8,128)(2,1)} custom-call(bf16[640,1024]{1,0:T(8,128)(2,1)} %get-tuple-element.123.refs_0_, bf16[640,1024]{1,0:T(8,128)(2,1)} %collective-permute-done.27.refs_1_, bf16[640,1024]{1,0:T(8,128)(2,1)} %collective-permute-done.28.refs_2_, bf16[640,1024]{1,0:T(8,128)(2,1)} %collective-permute-done.29.refs_3_, ...), custom_call_target="tpu_custom_call" | custom-call | tf_op jit(solution)/shard_map/expert_grads/pallas_call | solution.py:560
  359.3 6.0 all-to-all-start.1
  369.9 20.1 %collective-permute-done.32.refs_2_ = bf16[640,512]{1,0:T(8,128)(2,1)} collective-permute-done((bf16[640,512]{1,0:T(8,128)(2,1)}, bf16[640,512]{1,0:T(8,128)(2,1)}, u32[]{:S(2)}, u32[]{:S(2)}) %collective-permute-start.32) | collective-permute-done | bytes 655392 | tf_op jit(solution)/shard_map/ppermute | solution.py:811
  390.0 10.8 %combine_rows.2 = (bf16[4,256,640]{2,1,0:T(8,128)(2,1)}, bf16[4,256,640]{2,1,0:T(8,128)(2,1)}) custom-call(s32[64]{0:T(128)} %reshape.377.starts_ref, s32[2048,128]{1,0:T(8,128)} %pad.30.place_ref, bf16[640,640]{1,0:T(8,128)(2,1)} %get-tuple-element.138.refs_0_, bf16[640,640]{1,0:T(8,128)(2,1)} %collective-permute-done.30.refs_1_, ...), custom_call_target="tpu_custom_call" | custom-call | tf_op jit(solution)/shard_map/combine_rows/pallas_call | solution.py:399
  404.7 43.2 %collective-permute-done.36.refs_3_ = bf16[640,512]{1,0:T(8,128)(2,1)S(1)} collective-permute-done((bf16[640,512]{1,0:T(8,128)(2,1)S(1)}, bf16[640,512]{1,0:T(8,128)(2,1)S(1)}, u32[]{:S(2)}, u32[]{:S(2)}) %collective-permute-start.36) | collective-permute-done | bytes 655392 | tf_op jit(solution)/shard_map/ppermute | solution.py:811
  448.7 9.3 %combine_rows.3 = (bf16[4,256,512]{2,1,0:T(8,128)(2,1)}, bf16[4,256,512]{2,1,0:T(8,128)(2,1)}) custom-call(s32[64]{0:T(128)} %reshape.377.starts_ref, s32[2048,128]{1,0:T(8,128)} %pad.30.place_ref, bf16[640,512]{1,0:T(8,128)(2,1)} %get-tuple-element.144.refs_0_, bf16[640,512]{1,0:T(8,128)(2,1)} %collective-permute-done.31.refs_1_, ...), custom_call_target="tpu_custom_call" | custom-call | tf_op jit(solution)/shard_map/combine_rows/pallas_call | solution.py:399
  471.6 9.5 %collective-permute-done.38 = bf16[256,640]{1,0:T(8,128)(2,1)S(1)} collective-permute-done((bf16[256,640]{1,0:T(8,128)(2,1)S(1)}, bf16[256,640]{1,0:T(8,128)(2,1)S(1)}, u32[]{:S(2)}, u32[]{:S(2)}) %collective-permute-start.38) | collective-permute-done | bytes 327712 | tf_op jit(solution)/shard_map/ppermute | solution.py:807
  481.1 10.5 %collective-permute-done.39 = bf16[256,640]{1,0:T(8,128)(2,1)S(1)} collective-permute-done((bf16[256,640]{1,0:T(8,128)(2,1)S(1)}, bf16[256,640]{1,0:T(8,128)(2,1)S(1)}, u32[]{:S(2)}, u32[]{:S(2)}) %collective-permute-start.39) | collective-permute-done | bytes 327712 | tf_op jit(solution)/shard_map/ppermute | solution.py:807
  493.6 7.0 %collective-permute-start.43 = (bf16[256,512]{1,0:T(8,128)(2,1)}, bf16[256,512]{1,0:T(8,128)(2,1)S(1)}, u32[]{:S(2)}, u32[]{:S(2)}) collective-permute-start(bf16[256,512]{1,0:T(8,128)(2,1)} %get-tuple-element.325), channel_id=1, source_target_pairs={{0,2},{2,0},{4,6},{6,4},{1,3},{3,1},{5,7},{7,5},{8,10},{10,8},{12,... | collective-permute-start | bytes 786440 | tf_op jit(solution)/shard_map/ppermute | solution.py:807
  505.5 11.0 %combine_rows_add.1 = bf16[4,2048,256]{2,1,0:T(8,128)(2,1)} custom-call(s32[1]{0:T(128)} %bitcast.83.own_ref, s32[64]{0:T(128)} %reshape.391.starts_ref, s32[2048,128]{1,0:T(8,128)} %pad.33.place_ref, f32[256,1024]{1,0:T(8,128)} %copy-done.2, bf16[640,1024]{1,0:T(8,128)(2,1)} %get-tuple-element.164.refs_0_, ...), custom_call_target="tpu_custom_call" | custom-call | tf_op jit(solution)/shard_map/combine_rows_add/pallas_call | solution.py:437
  516.8 5.1 collective-permute-done.44
  528.5 8.8 %collective-permute-done.47 = bf16[256,1024]{1,0:T(8,128)(2,1)} collective-permute-done((bf16[256,1024]{1,0:T(8,128)(2,1)}, bf16[256,1024]{1,0:T(8,128)(2,1)}, u32[]{:S(2)}, u32[]{:S(2)}) %collective-permute-start.47) | collective-permute-done | bytes 524320 | tf_op jit(solution)/shard_map/ppermute | solution.py:788
  539.6 4.2 convolution_convert_fusion.grad_in
  551.2 10.8 %attend_backward.1 = (bf16[512,512]{1,0:T(8,128)(2,1)}, bf16[512,256]{1,0:T(8,128)(2,1)}, bf16[512,256]{1,0:T(8,128)(2,1)}) custom-call(bf16[512,512]{1,0:T(8,128)(2,1)} %get-tuple-element.176.query_in, bf16[512,256]{1,0:T(8,128)(2,1)} %get-tuple-element.177.key_in, bf16[512,256]{1,0:T(8,128)(2,1)} %get-tuple-element.178.value_in, ...), custom_call_target="tpu_custom_call" | custom-call | tf_op jit(solution)/shard_map/attend_backward/pallas_call | solution.py:244
  562.0 5.7 weight_products.1
  567.7 3.7 all-to-all-start.2
  571.6 3.7 multiply_reduce_fusion
  580.6 4.7 constant_dynamic-slice_fusion.32
  586.0 3.6 collective-permute-start.48
  590.4 4.2 collective-permute-start.49
  595.3 3.8 collective-permute-start.50
  599.9 3.6 collective-permute-start.51
  603.6 11.6 %collective-permute-done.49 = bf16[512,256]{1,0:T(8,128)(2,1)} collective-permute-done((bf16[512,256]{1,0:T(8,128)(2,1)}, bf16[512,256]{1,0:T(8,128)(2,1)}, u32[]{:S(2)}, u32[]{:S(2)}) %collective-permute-start.49) | collective-permute-done | bytes 262176 | tf_op jit(solution)/shard_map/ppermute | solution.py:767
  622.4 6.6 all-to-all-start.3
  628.9 6.6 spread_blocks.1
  635.5 26.9 %all-to-all-done.3 = bf16[4,64,1664]{2,1,0:T(8,128)(2,1)S(1)} async-done(((bf16[4,64,1664]{2,1,0:T(8,128)(2,1)}), bf16[4,64,1664]{2,1,0:T(8,128)(2,1)S(1)}, u32[]{:S(2)}, u32[]{:S(2)}) %all-to-all-start.3) | async-done | bytes 852000 | tf_op jit(solution)/shard_map/all_to_all | solution.py:1017
  662.9 8.9 %all_gather.7 = bf16[256,1664]{1,0:T(8,128)(2,1)S(1)} all-gather(bf16[64,1664]{1,0:T(8,128)(2,1)S(1)} %pad_maximum_fusion.14), channel_id=1, replica_groups=mesh['dp'=4,'row'=4,'col'=2] {'dp'}, dimensions={0}, use_global_device_ids=true | all-gather | bytes 1064960 | tf_op jit(solution)/shard_map/all_gather | solution.py:1069
  (371 shorter events, 145.5 us)
Async XLA Ops:
  7.2 117.9 %all-gather.2.cloned.1.call-start = ((), (), s32[]{:S(2)}) async-start(), calls=%async_computation.5 | async-start | bytes 4718592 | tf_op jit(solution)/shard_map/all_gather | solution.py:842
  10.6 19.8 %collective-permute-start.6 = (bf16[64,1152]{1,0:T(8,128)(2,1)S(1)}, bf16[64,1152]{1,0:T(8,128)(2,1)}, u32[]{:S(2)}, u32[]{:S(2)}) collective-permute-start(bf16[64,1152]{1,0:T(8,128)(2,1)S(1)} %fusion.38), channel_id=1, source_target_pairs={{0,6},{2,4},{4,2},{6,0},{1,7},{3,5},{5,3},{7,1},{8,14},{10,12},{12... | collective-permute-start | bytes 442376 | tf_op jit(solution)/shard_map/ppermute | solution.py:807
  15.7 32.1 %collective-permute-start.5 = (bf16[64,1152]{1,0:T(8,128)(2,1)S(1)}, bf16[64,1152]{1,0:T(8,128)(2,1)}, u32[]{:S(2)}, u32[]{:S(2)}) collective-permute-start(bf16[64,1152]{1,0:T(8,128)(2,1)S(1)} %fusion.38), channel_id=1, source_target_pairs={{0,4},{2,6},{4,0},{6,2},{1,5},{3,7},{5,1},{7,3},{8,12},{10,14},{12... | collective-permute-start | bytes 442376 | tf_op jit(solution)/shard_map/ppermute | solution.py:807
  15.7 32.8 %collective-permute-start.4 = (bf16[64,1152]{1,0:T(8,128)(2,1)S(1)}, bf16[64,1152]{1,0:T(8,128)(2,1)}, u32[]{:S(2)}, u32[]{:S(2)}) collective-permute-start(bf16[64,1152]{1,0:T(8,128)(2,1)S(1)} %fusion.38), channel_id=1, source_target_pairs={{0,2},{2,0},{4,6},{6,4},{1,3},{3,1},{5,7},{7,5},{8,10},{10,8},{12,... | collective-permute-start | bytes 442376 | tf_op jit(solution)/shard_map/ppermute | solution.py:807
  17.5 33.1 %collective-permute-start.3 = (bf16[512,256]{0,1:T(8,128)(2,1)}, bf16[512,256]{0,1:T(8,128)(2,1)}, u32[]{:S(2)}, u32[]{:S(2)}) collective-permute-start(bf16[512,256]{0,1:T(8,128)(2,1)} %bitcast.9), channel_id=1, source_target_pairs={{0,1},{1,3},{2,4},{3,6},{4,5},{5,7},{6,0},{7,2},{8,9},{9,11},{10,1... | collective-permute-start | bytes 786440 | tf_op jit(solution)/shard_map/ppermute | solution.py:750
  19.3 42.9 %collective-permute-start.2 = (bf16[512,256]{0,1:T(8,128)(2,1)S(1)}, bf16[512,256]{0,1:T(8,128)(2,1)}, u32[]{:S(2)}, u32[]{:S(2)}) collective-permute-start(bf16[512,256]{0,1:T(8,128)(2,1)S(1)} %bitcast.263), channel_id=1, source_target_pairs={{0,4},{1,6},{2,5},{3,7},{4,0},{5,2},{6,1},{7,3},{8,12},{9,14},{10,... | collective-permute-start | bytes 786440 | tf_op jit(solution)/shard_map/ppermute | solution.py:750
  30.4 40.7 %collective-permute-start.1 = (bf16[512,256]{0,1:T(8,128)(2,1)S(1)}, bf16[512,256]{0,1:T(8,128)(2,1)S(1)}, u32[]{:S(2)}, u32[]{:S(2)}) collective-permute-start(bf16[512,256]{0,1:T(8,128)(2,1)S(1)} %bitcast.265), channel_id=1, source_target_pairs={{0,5},{1,7},{2,0},{3,2},{4,1},{5,3},{6,4},{7,6},{8,13},{9,15},{10,... | collective-permute-start | bytes 786440 | tf_op jit(solution)/shard_map/ppermute | solution.py:750
  47.8 23.3 %collective-permute-start = (bf16[512,256]{0,1:T(8,128)(2,1)S(1)}, bf16[512,256]{0,1:T(8,128)(2,1)S(1)}, u32[]{:S(2)}, u32[]{:S(2)}) collective-permute-start(bf16[512,256]{0,1:T(8,128)(2,1)S(1)} %bitcast.264), channel_id=1, source_target_pairs={{0,0},{1,2},{2,1},{3,3},{4,4},{5,6},{6,5},{7,7},{8,8},{9,10},{10,9... | collective-permute-start | bytes 786440 | tf_op jit(solution)/shard_map/ppermute | solution.py:750
  50.6 23.0 %collective-permute-start.9 = (bf16[4,64,1152]{2,1,0:T(8,128)(2,1)}, bf16[4,64,1152]{2,1,0:T(8,128)(2,1)S(1)}, u32[]{:S(2)}, u32[]{:S(2)}) collective-permute-start(bf16[4,64,1152]{2,1,0:T(8,128)(2,1)} %get-tuple-element.345), channel_id=1, source_target_pairs={{0,24},{8,16},{16,8},{24,0},{1,25},{9,17},{17,9},{25,1},{2,26},{10... | collective-permute-start | bytes 1769480 | tf_op jit(solution)/shard_map/ppermute | solution.py:811
  50.6 28.5 %collective-permute-start.8 = (bf16[4,64,1152]{2,1,0:T(8,128)(2,1)}, bf16[4,64,1152]{2,1,0:T(8,128)(2,1)S(1)}, u32[]{:S(2)}, u32[]{:S(2)}) collective-permute-start(bf16[4,64,1152]{2,1,0:T(8,128)(2,1)} %get-tuple-element.345), channel_id=1, source_target_pairs={{0,16},{8,24},{16,0},{24,8},{1,17},{9,25},{17,1},{25,9},{2,18},{10... | collective-permute-start | bytes 1769480 | tf_op jit(solution)/shard_map/ppermute | solution.py:811
  62.2 16.9 %collective-permute-start.7 = (bf16[4,64,1152]{2,1,0:T(8,128)(2,1)}, bf16[4,64,1152]{2,1,0:T(8,128)(2,1)}, u32[]{:S(2)}, u32[]{:S(2)}) collective-permute-start(bf16[4,64,1152]{2,1,0:T(8,128)(2,1)} %get-tuple-element.345), channel_id=1, source_target_pairs={{0,8},{8,0},{16,24},{24,16},{1,9},{9,1},{17,25},{25,17},{2,10},{10... | collective-permute-start | bytes 1769480 | tf_op jit(solution)/shard_map/ppermute | solution.py:811
  138.6 16.7 %collective-permute-start.17 = (bf16[640,1152]{1,0:T(8,128)(2,1)}, bf16[640,1152]{1,0:T(8,128)(2,1)}, u32[]{:S(2)}, u32[]{:S(2)}) collective-permute-start(bf16[640,1152]{1,0:T(8,128)(2,1)} %get-tuple-element.107), channel_id=1, source_target_pairs={{0,8},{8,0},{16,24},{24,16},{1,9},{9,1},{17,25},{25,17},{2,10},{10... | collective-permute-start | bytes 4423688 | tf_op jit(solution)/shard_map/ppermute | solution.py:811
  141.0 35.4 %collective-permute-start.18 = (bf16[640,1152]{1,0:T(8,128)(2,1)}, bf16[640,1152]{1,0:T(8,128)(2,1)}, u32[]{:S(2)}, u32[]{:S(2)}) collective-permute-start(bf16[640,1152]{1,0:T(8,128)(2,1)} %get-tuple-element.111), channel_id=1, source_target_pairs={{0,16},{8,24},{16,0},{24,8},{1,17},{9,25},{17,1},{25,9},{2,18},{10... | collective-permute-start | bytes 4423688 | tf_op jit(solution)/shard_map/ppermute | solution.py:811
  154.1 52.3 %collective-permute-start.19 = (bf16[640,1152]{1,0:T(8,128)(2,1)S(1)}, bf16[640,1152]{1,0:T(8,128)(2,1)S(1)}, u32[]{:S(2)}, u32[]{:S(2)}) collective-permute-start(bf16[640,1152]{1,0:T(8,128)(2,1)S(1)} %copy-done.48), channel_id=1, source_target_pairs={{0,24},{8,16},{16,8},{24,0},{1,25},{9,17},{17,9},{25,1},{2,26},{10... | collective-permute-start | bytes 4423688 | tf_op jit(solution)/shard_map/ppermute | solution.py:811
  155.3 24.6 %collective-permute-start.21 = (bf16[256,1024]{1,0:T(8,128)(2,1)S(1)}, bf16[256,1024]{1,0:T(8,128)(2,1)S(1)}, u32[]{:S(2)}, u32[]{:S(2)}) collective-permute-start(bf16[256,1024]{1,0:T(8,128)(2,1)S(1)} %multiply_convert_fusion.3.refs_0_), channel_id=1, source_target_pairs={{0,2},{2,0},{4,6},{6,4},{1,3},{3,1},{5,7},{7,5},{8,10},{10,8},{12,... | collective-permute-start | bytes 1572872 | tf_op jit(solution)/shard_map/ppermute | solution.py:807
  155.4 38.3 %collective-permute-start.23 = (bf16[256,1024]{1,0:T(8,128)(2,1)S(1)}, bf16[256,1024]{1,0:T(8,128)(2,1)S(1)}, u32[]{:S(2)}, u32[]{:S(2)}) collective-permute-start(bf16[256,1024]{1,0:T(8,128)(2,1)S(1)} %multiply_convert_fusion.3.refs_0_), channel_id=1, source_target_pairs={{0,4},{2,6},{4,0},{6,2},{1,5},{3,7},{5,1},{7,3},{8,12},{10,14},{12... | collective-permute-start | bytes 1572872 | tf_op jit(solution)/shard_map/ppermute | solution.py:807
  157.3 37.9 %collective-permute-start.25 = (bf16[256,1024]{1,0:T(8,128)(2,1)S(1)}, bf16[256,1024]{1,0:T(8,128)(2,1)S(1)}, u32[]{:S(2)}, u32[]{:S(2)}) collective-permute-start(bf16[256,1024]{1,0:T(8,128)(2,1)S(1)} %multiply_convert_fusion.3.refs_0_), channel_id=1, source_target_pairs={{0,6},{2,4},{4,2},{6,0},{1,7},{3,5},{5,3},{7,1},{8,14},{10,12},{12... | collective-permute-start | bytes 1572872 | tf_op jit(solution)/shard_map/ppermute | solution.py:807
  176.4 30.1 %collective-permute-start.20 = (bf16[256,1024]{1,0:T(8,128)(2,1)S(1)}, bf16[256,1024]{1,0:T(8,128)(2,1)S(1)}, u32[]{:S(2)}, u32[]{:S(2)}) collective-permute-start(bf16[256,1024]{1,0:T(8,128)(2,1)S(1)} %multiply_convert_fusion.3.refs_0_), channel_id=1, source_target_pairs={{0,1},{1,0},{2,3},{3,2},{4,5},{5,4},{6,7},{7,6},{8,9},{9,8},{10,11... | collective-permute-start | bytes 1572872 | tf_op jit(solution)/shard_map/ppermute | solution.py:857
  179.9 27.7 %collective-permute-start.22 = (bf16[256,1024]{1,0:T(8,128)(2,1)S(1)}, bf16[256,1024]{1,0:T(8,128)(2,1)S(1)}, u32[]{:S(2)}, u32[]{:S(2)}) collective-permute-start(bf16[256,1024]{1,0:T(8,128)(2,1)S(1)} %collective-permute-done.21.refs_2_), channel_id=1, source_target_pairs={{0,1},{1,0},{2,3},{3,2},{4,5},{5,4},{6,7},{7,6},{8,9},{9,8},{10,11... | collective-permute-start | bytes 1572872 | tf_op jit(solution)/shard_map/ppermute | solution.py:857
  193.7 20.1 %collective-permute-start.24 = (bf16[256,1024]{1,0:T(8,128)(2,1)S(1)}, bf16[256,1024]{1,0:T(8,128)(2,1)S(1)}, u32[]{:S(2)}, u32[]{:S(2)}) collective-permute-start(bf16[256,1024]{1,0:T(8,128)(2,1)S(1)} %collective-permute-done.23.refs_4_), channel_id=1, source_target_pairs={{0,1},{1,0},{2,3},{3,2},{4,5},{5,4},{6,7},{7,6},{8,9},{9,8},{10,11... | collective-permute-start | bytes 1572872 | tf_op jit(solution)/shard_map/ppermute | solution.py:857
  195.2 27.5 %collective-permute-start.26 = (bf16[256,1024]{1,0:T(8,128)(2,1)S(1)}, bf16[256,1024]{1,0:T(8,128)(2,1)}, u32[]{:S(2)}, u32[]{:S(2)}) collective-permute-start(bf16[256,1024]{1,0:T(8,128)(2,1)S(1)} %collective-permute-done.25.refs_6_), channel_id=1, source_target_pairs={{0,1},{1,0},{2,3},{3,2},{4,5},{5,4},{6,7},{7,6},{8,9},{9,8},{10,11... | collective-permute-start | bytes 1572872 | tf_op jit(solution)/shard_map/ppermute | solution.py:857
  222.7 76.9 %all-to-all-start = ((bf16[8,768,256]{2,1,0:T(8,128)(2,1)}), bf16[8,768,256]{2,1,0:T(8,128)(2,1)S(1)}, u32[]{:S(2)}, u32[]{:S(2)}) async-start(bf16[8,768,256]{2,1,0:T(8,128)(2,1)} %pad_maximum_fusion), calls=%async_computation | async-start | bytes 6291456 | tf_op jit(solution)/shard_map/all_to_all | solution.py:938
  240.5 32.0 %collective-permute-start.28 = (bf16[640,1024]{1,0:T(8,128)(2,1)}, bf16[640,1024]{1,0:T(8,128)(2,1)}, u32[]{:S(2)}, u32[]{:S(2)}) collective-permute-start(bf16[640,1024]{1,0:T(8,128)(2,1)} %get-tuple-element.125), channel_id=1, source_target_pairs={{0,16},{8,24},{16,0},{24,8},{1,17},{9,25},{17,1},{25,9},{2,18},{10... | collective-permute-start | bytes 3932168 | tf_op jit(solution)/shard_map/ppermute | solution.py:811
  242.1 57.5 %collective-permute-start.29 = (bf16[640,1024]{1,0:T(8,128)(2,1)}, bf16[640,1024]{1,0:T(8,128)(2,1)}, u32[]{:S(2)}, u32[]{:S(2)}) collective-permute-start(bf16[640,1024]{1,0:T(8,128)(2,1)} %get-tuple-element.126), channel_id=1, source_target_pairs={{0,24},{8,16},{16,8},{24,0},{1,25},{9,17},{17,9},{25,1},{2,26},{10... | collective-permute-start | bytes 3932168 | tf_op jit(solution)/shard_map/ppermute | solution.py:811
  337.7 52.3 %collective-permute-start.33 = (bf16[640,640]{1,0:T(8,128)(2,1)}, bf16[640,640]{1,0:T(8,128)(2,1)}, u32[]{:S(2)}, u32[]{:S(2)}) collective-permute-start(bf16[640,640]{1,0:T(8,128)(2,1)} %get-tuple-element.140), channel_id=1, source_target_pairs={{0,16},{8,24},{16,0},{24,8},{1,17},{9,25},{17,1},{25,9},{2,18},{10... | collective-permute-start | bytes 2457608 | tf_op jit(solution)/shard_map/ppermute | solution.py:811
  339.3 50.8 %collective-permute-start.34 = (bf16[640,640]{1,0:T(8,128)(2,1)}, bf16[640,640]{1,0:T(8,128)(2,1)}, u32[]{:S(2)}, u32[]{:S(2)}) collective-permute-start(bf16[640,640]{1,0:T(8,128)(2,1)} %get-tuple-element.141), channel_id=1, source_target_pairs={{0,24},{8,16},{16,8},{24,0},{1,25},{9,17},{17,9},{25,1},{2,26},{10... | collective-permute-start | bytes 2457608 | tf_op jit(solution)/shard_map/ppermute | solution.py:811
  339.3 30.5 %collective-permute-start.31 = (bf16[640,512]{1,0:T(8,128)(2,1)}, bf16[640,512]{1,0:T(8,128)(2,1)}, u32[]{:S(2)}, u32[]{:S(2)}) collective-permute-start(bf16[640,512]{1,0:T(8,128)(2,1)} %get-tuple-element.136), channel_id=1, source_target_pairs={{0,8},{8,0},{16,24},{24,16},{1,9},{9,1},{17,25},{25,17},{2,10},{10... | collective-permute-start | bytes 1966088 | tf_op jit(solution)/shard_map/ppermute | solution.py:811
  339.9 50.1 %collective-permute-start.32 = (bf16[640,512]{1,0:T(8,128)(2,1)}, bf16[640,512]{1,0:T(8,128)(2,1)}, u32[]{:S(2)}, u32[]{:S(2)}) collective-permute-start(bf16[640,512]{1,0:T(8,128)(2,1)} %get-tuple-element.137), channel_id=1, source_target_pairs={{0,16},{8,24},{16,0},{24,8},{1,17},{9,25},{17,1},{25,9},{2,18},{10... | collective-permute-start | bytes 1966088 | tf_op jit(solution)/shard_map/ppermute | solution.py:811
  359.3 180.3 %all-to-all-start.1 = ((bf16[8,768,256]{2,1,0:T(8,128)(2,1)}), bf16[8,768,256]{2,1,0:T(8,128)(2,1)S(1)}, u32[]{:S(2)}, u32[]{:S(2)}) async-start(bf16[8,768,256]{2,1,0:T(8,128)(2,1)} %expert_grads.1), calls=%async_computation.1 | async-start | bytes 6291456 | tf_op jit(solution)/shard_map/all_to_all | solution.py:960
  365.3 297.5 %reduce-scatter.2.cloned.1.call-start = ((), (), s32[]{:S(2)}) async-start(), calls=%async_computation.6 | async-start | bytes 4718592 | tf_op jit(solution)/shard_map/reduce_scatter | solution.py:1035
  400.8 57.2 %collective-permute-start.35 = (bf16[4,256,640]{2,1,0:T(8,128)(2,1)}, bf16[4,256,640]{2,1,0:T(8,128)(2,1)}, u32[]{:S(2)}, u32[]{:S(2)}) collective-permute-start(bf16[4,256,640]{2,1,0:T(8,128)(2,1)} %get-tuple-element.143), channel_id=1, source_target_pairs={{0,1},{1,0},{2,3},{3,2},{4,5},{5,4},{6,7},{7,6},{8,9},{9,8},{10,11... | collective-permute-start | bytes 3932168 | tf_op jit(solution)/shard_map/ppermute | solution.py:961
  402.8 63.2 %collective-permute-start.41 = (bf16[640,1024]{1,0:T(8,128)(2,1)}, bf16[640,1024]{1,0:T(8,128)(2,1)}, u32[]{:S(2)}, u32[]{:S(2)}) collective-permute-start(bf16[640,1024]{1,0:T(8,128)(2,1)} %get-tuple-element.157), channel_id=1, source_target_pairs={{0,8},{8,0},{16,24},{24,16},{1,9},{9,1},{17,25},{25,17},{2,10},{10... | collective-permute-start | bytes 3932168 | tf_op jit(solution)/shard_map/ppermute | solution.py:811
  402.8 65.6 %collective-permute-start.42 = (bf16[640,1024]{1,0:T(8,128)(2,1)}, bf16[640,1024]{1,0:T(8,128)(2,1)}, u32[]{:S(2)}, u32[]{:S(2)}) collective-permute-start(bf16[640,1024]{1,0:T(8,128)(2,1)} %get-tuple-element.158), channel_id=1, source_target_pairs={{0,16},{8,24},{16,0},{24,8},{1,17},{9,25},{17,1},{25,9},{2,18},{10... | collective-permute-start | bytes 3932168 | tf_op jit(solution)/shard_map/ppermute | solution.py:811
  404.4 43.5 %collective-permute-start.36 = (bf16[640,512]{1,0:T(8,128)(2,1)S(1)}, bf16[640,512]{1,0:T(8,128)(2,1)S(1)}, u32[]{:S(2)}, u32[]{:S(2)}) collective-permute-start(bf16[640,512]{1,0:T(8,128)(2,1)S(1)} %copy-done.49), channel_id=1, source_target_pairs={{0,24},{8,16},{16,8},{24,0},{1,25},{9,17},{17,9},{25,1},{2,26},{10... | collective-permute-start | bytes 1966088 | tf_op jit(solution)/shard_map/ppermute | solution.py:811
  458.0 33.5 %collective-permute-start.37 = (bf16[4,256,512]{2,1,0:T(8,128)(2,1)}, bf16[4,256,512]{2,1,0:T(8,128)(2,1)}, u32[]{:S(2)}, u32[]{:S(2)}) collective-permute-start(bf16[4,256,512]{2,1,0:T(8,128)(2,1)} %get-tuple-element.151), channel_id=1, source_target_pairs={{0,1},{1,0},{2,3},{3,2},{4,5},{5,4},{6,7},{7,6},{8,9},{9,8},{10,11... | collective-permute-start | bytes 3145736 | tf_op jit(solution)/shard_map/ppermute | solution.py:964
  461.1 43.3 %collective-permute-start.46 = (bf16[640,1024]{1,0:T(8,128)(2,1)}, bf16[640,1024]{1,0:T(8,128)(2,1)S(1)}, u32[]{:S(2)}, u32[]{:S(2)}) collective-permute-start(bf16[640,1024]{1,0:T(8,128)(2,1)} %get-tuple-element.167), channel_id=1, source_target_pairs={{0,24},{8,16},{16,8},{24,0},{1,25},{9,17},{17,9},{25,1},{2,26},{10... | collective-permute-start | bytes 3932168 | tf_op jit(solution)/shard_map/ppermute | solution.py:811
  464.2 16.8 %collective-permute-start.38 = (bf16[256,640]{1,0:T(8,128)(2,1)S(1)}, bf16[256,640]{1,0:T(8,128)(2,1)S(1)}, u32[]{:S(2)}, u32[]{:S(2)}) collective-permute-start(bf16[256,640]{1,0:T(8,128)(2,1)S(1)} %get-tuple-element.318), channel_id=1, source_target_pairs={{0,2},{2,0},{4,6},{6,4},{1,3},{3,1},{5,7},{7,5},{8,10},{10,8},{12,... | collective-permute-start | bytes 983048 | tf_op jit(solution)/shard_map/ppermute | solution.py:807
  466.0 25.5 %collective-permute-start.39 = (bf16[256,640]{1,0:T(8,128)(2,1)S(1)}, bf16[256,640]{1,0:T(8,128)(2,1)S(1)}, u32[]{:S(2)}, u32[]{:S(2)}) collective-permute-start(bf16[256,640]{1,0:T(8,128)(2,1)S(1)} %get-tuple-element.317), channel_id=1, source_target_pairs={{0,4},{2,6},{4,0},{6,2},{1,5},{3,7},{5,1},{7,3},{8,12},{10,14},{12... | collective-permute-start | bytes 983048 | tf_op jit(solution)/shard_map/ppermute | solution.py:807
  468.4 23.1 %collective-permute-start.40 = (bf16[256,640]{1,0:T(8,128)(2,1)S(1)}, bf16[256,640]{1,0:T(8,128)(2,1)S(1)}, u32[]{:S(2)}, u32[]{:S(2)}) collective-permute-start(bf16[256,640]{1,0:T(8,128)(2,1)S(1)} %get-tuple-element.316), channel_id=1, source_target_pairs={{0,6},{2,4},{4,2},{6,0},{1,7},{3,5},{5,3},{7,1},{8,14},{10,12},{12... | collective-permute-start | bytes 983048 | tf_op jit(solution)/shard_map/ppermute | solution.py:807
  493.6 23.2 %collective-permute-start.43 = (bf16[256,512]{1,0:T(8,128)(2,1)}, bf16[256,512]{1,0:T(8,128)(2,1)S(1)}, u32[]{:S(2)}, u32[]{:S(2)}) collective-permute-start(bf16[256,512]{1,0:T(8,128)(2,1)} %get-tuple-element.325), channel_id=1, source_target_pairs={{0,2},{2,0},{4,6},{6,4},{1,3},{3,1},{5,7},{7,5},{8,10},{10,8},{12,... | collective-permute-start | bytes 786440 | tf_op jit(solution)/shard_map/ppermute | solution.py:807
  500.5 21.4 %collective-permute-start.44 = (bf16[256,512]{1,0:T(8,128)(2,1)S(1)}, bf16[256,512]{1,0:T(8,128)(2,1)S(1)}, u32[]{:S(2)}, u32[]{:S(2)}) collective-permute-start(bf16[256,512]{1,0:T(8,128)(2,1)S(1)} %get-tuple-element.324), channel_id=1, source_target_pairs={{0,4},{2,6},{4,0},{6,2},{1,5},{3,7},{5,1},{7,3},{8,12},{10,14},{12... | collective-permute-start | bytes 786440 | tf_op jit(solution)/shard_map/ppermute | solution.py:807
  501.4 21.2 %collective-permute-start.45 = (bf16[256,512]{1,0:T(8,128)(2,1)S(1)}, bf16[256,512]{1,0:T(8,128)(2,1)}, u32[]{:S(2)}, u32[]{:S(2)}) collective-permute-start(bf16[256,512]{1,0:T(8,128)(2,1)S(1)} %get-tuple-element.323), channel_id=1, source_target_pairs={{0,6},{2,4},{4,2},{6,0},{1,7},{3,5},{5,3},{7,1},{8,14},{10,12},{12... | collective-permute-start | bytes 786440 | tf_op jit(solution)/shard_map/ppermute | solution.py:807
  567.7 52.8 %all-to-all-start.2 = ((bf16[4,256,1664]{2,1,0:T(8,128)(2,1)}), bf16[4,256,1664]{2,1,0:T(8,128)(2,1)S(1)}, u32[]{:S(2)}, u32[]{:S(2)}) async-start(bf16[4,256,1664]{2,1,0:T(8,128)(2,1)} %bitcast.210), calls=%async_computation.2 | async-start | bytes 6815744 | tf_op jit(solution)/shard_map/all_to_all | solution.py:1012
  586.0 17.6 %collective-permute-start.48 = (bf16[512,256]{1,0:T(8,128)(2,1)}, bf16[512,256]{1,0:T(8,128)(2,1)}, u32[]{:S(2)}, u32[]{:S(2)}) collective-permute-start(bf16[512,256]{1,0:T(8,128)(2,1)} %bitcast.208), channel_id=1, source_target_pairs={{0,0},{2,1},{1,2},{3,3},{4,4},{6,5},{5,6},{7,7},{8,8},{10,9},{9,10... | collective-permute-start | bytes 786440 | tf_op jit(solution)/shard_map/ppermute | solution.py:767
  590.4 24.8 %collective-permute-start.49 = (bf16[512,256]{1,0:T(8,128)(2,1)}, bf16[512,256]{1,0:T(8,128)(2,1)}, u32[]{:S(2)}, u32[]{:S(2)}) collective-permute-start(bf16[512,256]{1,0:T(8,128)(2,1)} %bitcast.207), channel_id=1, source_target_pairs={{5,0},{7,1},{0,2},{2,3},{1,4},{3,5},{4,6},{6,7},{13,8},{15,9},{8,1... | collective-permute-start | bytes 786440 | tf_op jit(solution)/shard_map/ppermute | solution.py:767
  595.3 22.6 %collective-permute-start.50 = (bf16[512,256]{1,0:T(8,128)(2,1)}, bf16[512,256]{1,0:T(8,128)(2,1)}, u32[]{:S(2)}, u32[]{:S(2)}) collective-permute-start(bf16[512,256]{1,0:T(8,128)(2,1)} %bitcast.206), channel_id=1, source_target_pairs={{4,0},{6,1},{5,2},{7,3},{0,4},{2,5},{1,6},{3,7},{12,8},{14,9},{13,... | collective-permute-start | bytes 786440 | tf_op jit(solution)/shard_map/ppermute | solution.py:767
  599.9 18.0 %collective-permute-start.51 = (bf16[512,256]{1,0:T(8,128)(2,1)}, bf16[512,256]{1,0:T(8,128)(2,1)}, u32[]{:S(2)}, u32[]{:S(2)}) collective-permute-start(bf16[512,256]{1,0:T(8,128)(2,1)} %bitcast.205), channel_id=1, source_target_pairs={{1,0},{3,1},{4,2},{6,3},{5,4},{7,5},{0,6},{2,7},{9,8},{11,9},{12,1... | collective-permute-start | bytes 786440 | tf_op jit(solution)/shard_map/ppermute | solution.py:767
  622.4 40.1 %all-to-all-start.3 = ((bf16[4,64,1664]{2,1,0:T(8,128)(2,1)}), bf16[4,64,1664]{2,1,0:T(8,128)(2,1)S(1)}, u32[]{:S(2)}, u32[]{:S(2)}) async-start(bf16[4,64,1664]{2,1,0:T(8,128)(2,1)} %pad_maximum_fusion.9), calls=%async_computation.3 | async-start | bytes 1703936 | tf_op jit(solution)/shard_map/all_to_all | solution.py:1017
  (62 other events, 688.1 us)
Sparse Core Ops, SparseCore 0:
  16.5 108.5 all-gather.1
  543.9 116.4 reduce-scatter.1

commit v4 on v3

--- a/solution.py
+++ b/solution.py
@@ -371,8 +371,9 @@
     return total
 
 
-def combine_kernel(starts_ref, place_ref, *refs, capacity):
-    *value_refs, own_ref, away_ref = refs
+def combine_kernel(starts_ref, place_ref, *refs, capacity, count):
+    value_refs = refs[:count]
+    own_ref, away_ref = refs[-2:]
     step = pl.program_id(0)
     half = pl.num_programs(0) // 2
     pieces = place_ref.shape[0] // LANES
@@ -391,19 +392,20 @@
             own_ref[0, rows, :] = total
 
 
-def combine(starts, places, values, block):
+def combine(starts, places, values, block, after):
     tokens = places.shape[0]
     capacity, width = values[0].shape
     half = tokens // block // 2
     out = jax.ShapeDtypeStruct((half, block, width), bf16)
     return pl.pallas_call(
-        functools.partial(combine_kernel, capacity=capacity),
+        functools.partial(combine_kernel, capacity=capacity, count=len(values)),
         grid=(2 * half,),
         in_specs=[
             pl.BlockSpec(memory_space=pltpu.SMEM),
             pl.BlockSpec((block, LANES), lambda i: (i, 0)),
         ]
-        + [pl.BlockSpec((capacity, width), lambda i: (0, 0)) for _ in values],
+        + [pl.BlockSpec((capacity, width), lambda i: (0, 0)) for _ in values]
+        + [pl.BlockSpec(memory_space=pl.ANY) for _ in after],
         out_specs=[
             pl.BlockSpec((1, block, width), lambda i: (jnp.maximum(i - half, 0), 0, 0)),
             pl.BlockSpec((1, block, width), lambda i: (jnp.minimum(i, half - 1), 0, 0)),
@@ -411,7 +413,7 @@
         out_shape=[out, out],
         compiler_params=BIG,
         name="combine_rows",
-    )(starts, places, *values)
+    )(starts, places, *values, *after)
 
 
 def combine_add_kernel(own_ref, starts_ref, place_ref, add_ref, *refs, capacity):
@@ -942,8 +944,8 @@
         slots, grad_slots, expert_weights, router_pad, pick, 2, row_count, col_count
     )
 
-    def to_cells(back):
-        return combine(starts_back, places_back, back, own_rows)
+    def to_cells(back, after):
+        return combine(starts_back, places_back, back, own_rows, after)
 
     def half_sums(own, away):
         return [own[turn].astype(f32) + away[turn].astype(f32) for turn in range(row_count)]
@@ -955,20 +957,18 @@
     back_b = exchange(back_b)
     *back_a[:2], saved[0] = lax.optimization_barrier((*back_a[:2], saved[0]))
     back_a[0], *back_b[:early] = lax.optimization_barrier((back_a[0], *back_b[:early]))
-    kept_a, away_a = to_cells(back_a)
     grad_blocks = expert_grads(slots, saved, shares.shape, row_count, col_count)
+    kept_a, away_a = to_cells(back_a, [grad_blocks])
     grad_got = lax.all_to_all(grad_blocks, ("row", "col"), 0, 0, tiled=True)
     away_a = lax.ppermute(away_a, "col", mirror)
-    kept_b, away_b = to_cells(back_b)
+    kept_b, away_b = to_cells(back_b, [])
     away_a, kept_b, away_b = lax.optimization_barrier((away_a, kept_b, away_b))
     away_b = lax.ppermute(away_b, "col", mirror)
     sums_a = half_sums(kept_a, away_a)
     parts_a = row_parts(sums_a)
-    back_b[0], *results = lax.optimization_barrier((back_b[0], *results))
+    back_b[-1], *results = lax.optimization_barrier((back_b[-1], *results))
     results = exchange(results)
-    away_b, parts_a, results[:early] = lax.optimization_barrier(
-        (away_b, parts_a, results[:early])
-    )
+    away_b, parts_a = lax.optimization_barrier((away_b, parts_a))
     sums_b = half_sums(kept_b, away_b)
     parts_b = row_parts(sums_b)
     mixed_rows = combine_add(

time: 694 us -> 681 us (0.981)
  waiting for transfers between devices: 314 us -> 299 us
    ppermute x21, waiting for transfers between devices: 146 us -> 107 us  [over_dp(): return lax.ppermute(array, 'dp', pairs) if turn else array]
    ppermute x1, waiting for transfers between devices: 0.01 us -> 24.8 us  [per_device(): away_a = lax.ppermute(away_a, 'col', mirror)]
    unnamed x114 -> x104, local copies, waits for them, and re-layouts: 13.9 us -> 11.3 us
  transfers between devices with their start and end apart: 59 -> 59, of which waited for: 25 -> 26; matrix products, arithmetic and copies ran while one was open for 13% -> 13% of each run, Pallas kernels for 14% -> 14%
where the time goes in v4:
time: 681 us; the launch traced here: 672 us
  waiting for transfers between devices  299 us (44%)
  Pallas kernels  144 us (21%)
  starting transfers between devices  101 us (15%)
  local copies, waits for them, and re-layouts  49.8 us (7%)
  other arithmetic  38.5 us (6%)
  between operations  16.1 us (2%)
  matrix products  14.4 us (2%)
  blocking collectives  8.93 us (1%)
    ppermute x21, waiting for transfers between devices, over_dp(): return lax.ppermute(array, 'dp', pairs) if turn else array  107 us
    ppermute x15, waiting for transfers between devices, over_rows(): return lax.ppermute(array, 'row', pairs) if turn else array  64.2 us
    pallas_call x1, Pallas kernels, run_expert(): pl.pallas_call(functools.partial(expert_kernel, groups=groups, row_count=...  36 us
    ppermute x15, starting transfers between devices, over_rows(): return lax.ppermute(array, 'row', pairs) if turn else array  35.4 us
    all_to_all x1, waiting for transfers between devices, row_sums(): parts = lax.all_to_all(parts, 'row', 0, 0, tiled=True)  27.7 us
    pallas_call x2, Pallas kernels, dispatch(): pl.pallas_call(kernel, grid=(count,), in_specs=[pl.BlockSpec(memory_space...  25 us
    ppermute x1, waiting for transfers between devices, per_device(): away_a = lax.ppermute(away_a, 'col', mirror)  24.8 us
    pallas_call x2, Pallas kernels, combine(): pl.pallas_call(functools.partial(combine_kernel, capacity=capacity, count...  20.1 us
  transfers between devices with their start and end apart: 59, of which 26 were waited for; matrix products, arithmetic and copies ran while one was open for 13% of the time, Pallas kernels for 14%

profile of v4, /device:TPU:0, one launch (start us, length us, event | category | flops | bytes accessed | tf_op | source)
XLA Modules:
  0.0 671.9 jit_solution(2804677203647074738)
XLA Ops:
  10.6 5.1 collective-permute-start.6
  31.9 15.9 %collective-permute-done.5 = bf16[64,1152]{1,0:T(8,128)(2,1)} collective-permute-done((bf16[64,1152]{1,0:T(8,128)(2,1)S(1)}, bf16[64,1152]{1,0:T(8,128)(2,1)}, u32[]{:S(2)}, u32[]{:S(2)}) %collective-permute-start.5) | collective-permute-done | bytes 147488 | tf_op jit(solution)/shard_map/ppermute | solution.py:809
  52.1 10.1 %collective-permute-done.2 = bf16[512,256]{0,1:T(8,128)(2,1)} collective-permute-done((bf16[512,256]{0,1:T(8,128)(2,1)S(1)}, bf16[512,256]{0,1:T(8,128)(2,1)}, u32[]{:S(2)}, u32[]{:S(2)}) %collective-permute-start.2) | collective-permute-done | bytes 262176 | tf_op jit(solution)/shard_map/ppermute | solution.py:752
  62.2 8.8 %collective-permute-done.1 = bf16[512,256]{0,1:T(8,128)(2,1)S(1)} collective-permute-done((bf16[512,256]{0,1:T(8,128)(2,1)S(1)}, bf16[512,256]{0,1:T(8,128)(2,1)S(1)}, u32[]{:S(2)}, u32[]{:S(2)}) %collective-permute-start.1) | collective-permute-done | bytes 262176 | tf_op jit(solution)/shard_map/ppermute | solution.py:752
  73.7 5.4 collective-permute-done.8
  84.0 4.7 collective-permute-start.12
  93.0 10.0 %collective-permute-done.11 = bf16[64,512]{1,0:T(8,128)(2,1)S(1)} collective-permute-done((bf16[64,512]{1,0:T(8,128)(2,1)S(1)}, bf16[64,512]{1,0:T(8,128)(2,1)S(1)}, u32[]{:S(2)}, u32[]{:S(2)}) %collective-permute-start.11) | collective-permute-done | bytes 65568 | tf_op jit(solution)/shard_map/ppermute | solution.py:809
  107.7 10.6 %attend_forward.1 = (bf16[512,512]{1,0:T(8,128)(2,1)}, bf16[512,256]{1,0:T(8,128)(2,1)}, bf16[512,256]{1,0:T(8,128)(2,1)}, bf16[512,512]{1,0:T(8,128)(2,1)}, f32[512,256]{1,0:T(8,128)}) custom-call(f32[512,1024]{1,0:T(8,128)} %fusion.3.query_in.key_in.value_in, f32[512,1024]{1,0:T(8,128)} %fusion.3.query_in.key_in.value_in, ...), custom_call_target="tpu_custom_call" | custom-call | tf_op jit(solution)/shard_map/attend_forward/pallas_call | solution.py:129
  118.8 6.3 all-gather.2.cloned.1.call-done
  125.1 13.6 %dispatch_grads.1 = (bf16[640,1152]{1,0:T(8,128)(2,1)}, bf16[640,1152]{1,0:T(8,128)(2,1)}, bf16[640,1152]{1,0:T(8,128)(2,1)}, bf16[640,1152]{1,0:T(8,128)(2,1)}) custom-call(s32[32]{0:T(128)} %reshape.379.starts_ref, s32[4,1,2048]{2,1,0:T(1,128)} %copy.422.place_ref, bf16[4,2048,256]{2,1,0:T(8,128)(2,1)} %bitcast.214, ...), custom_call_target="tpu_custom_call" | custom-call | tf_op jit(solution)/shard_map/dispatch_grads/pallas_call | solution.py:328
  143.8 10.1 %collective-permute-done.16 = bf16[256,1024]{1,0:T(8,128)(2,1)S(1)} collective-permute-done((bf16[256,1024]{1,0:T(8,128)(2,1)S(1)}, bf16[256,1024]{1,0:T(8,128)(2,1)S(1)}, u32[]{:S(2)}, u32[]{:S(2)}) %collective-permute-start.16) | collective-permute-done | bytes 524320 | tf_op jit(solution)/shard_map/ppermute | solution.py:787
  159.9 16.5 %collective-permute-done.18.refs_6_ = bf16[640,1152]{1,0:T(8,128)(2,1)} collective-permute-done((bf16[640,1152]{1,0:T(8,128)(2,1)}, bf16[640,1152]{1,0:T(8,128)(2,1)}, u32[]{:S(2)}, u32[]{:S(2)}) %collective-permute-start.18) | collective-permute-done | bytes 1474592 | tf_op jit(solution)/shard_map/ppermute | solution.py:813
  181.4 12.4 %collective-permute-done.23.refs_4_ = bf16[256,1024]{1,0:T(8,128)(2,1)S(1)} collective-permute-done((bf16[256,1024]{1,0:T(8,128)(2,1)S(1)}, bf16[256,1024]{1,0:T(8,128)(2,1)S(1)}, u32[]{:S(2)}, u32[]{:S(2)}) %collective-permute-start.23) | collective-permute-done | bytes 524320 | tf_op jit(solution)/shard_map/ppermute | solution.py:809
  200.7 5.8 collective-permute-done.19.refs_7_
  207.6 6.1 collective-permute-done.24.refs_5_
  214.5 8.2 %collective-permute-done.26.refs_7_ = bf16[256,1024]{1,0:T(8,128)(2,1)} collective-permute-done((bf16[256,1024]{1,0:T(8,128)(2,1)S(1)}, bf16[256,1024]{1,0:T(8,128)(2,1)}, u32[]{:S(2)}, u32[]{:S(2)}) %collective-permute-start.26) | collective-permute-done | bytes 524320 | tf_op jit(solution)/shard_map/ppermute | solution.py:859
  222.7 3.8 all-to-all-start
  229.1 11.4 %dispatch_tokens.1 = (bf16[640,1024]{1,0:T(8,128)(2,1)}, bf16[640,1024]{1,0:T(8,128)(2,1)}, bf16[640,1024]{1,0:T(8,128)(2,1)}, bf16[640,1024]{1,0:T(8,128)(2,1)}) custom-call(s32[32]{0:T(128)} %reshape.387.starts_ref, s32[4,1,2048]{2,1,0:T(1,128)} %reshape.389.place_ref, bf16[256,1024]{1,0:T(8,128)(2,1)} %copy-done.7, bf16[256,1024]{1,0:T(8,128)(2,1)} %copy-done.37, ...), custom_call_target="tpu_custom_call" | custom-call | tf_op jit(solution)/shard_map/dispatch_tokens/pallas_call | solution.py:328
  244.8 27.7 %collective-permute-done.28.refs_2_ = bf16[640,1024]{1,0:T(8,128)(2,1)} collective-permute-done((bf16[640,1024]{1,0:T(8,128)(2,1)}, bf16[640,1024]{1,0:T(8,128)(2,1)}, u32[]{:S(2)}, u32[]{:S(2)}) %collective-permute-start.28) | collective-permute-done | bytes 1310752 | tf_op jit(solution)/shard_map/ppermute | solution.py:813
  272.5 27.2 %collective-permute-done.29.refs_3_ = bf16[640,1024]{1,0:T(8,128)(2,1)} collective-permute-done((bf16[640,1024]{1,0:T(8,128)(2,1)}, bf16[640,1024]{1,0:T(8,128)(2,1)}, u32[]{:S(2)}, u32[]{:S(2)}) %collective-permute-start.29) | collective-permute-done | bytes 1310752 | tf_op jit(solution)/shard_map/ppermute | solution.py:813
  301.3 36.0 %expert_pass.1 = (bf16[640,1024]{1,0:T(8,128)(2,1)}, bf16[640,1024]{1,0:T(8,128)(2,1)}, bf16[640,1024]{1,0:T(8,128)(2,1)}, bf16[640,1024]{1,0:T(8,128)(2,1)}, bf...) custom-call(bf16[8,768,256]{2,1,0:T(8,128)(2,1)} %copy-done.5, ...), custom_call_target="tpu_custom_call" | custom-call | tf_op jit(solution)/shard_map/expert_pass/pallas_call | solution.py:597
  341.3 17.9 %expert_grads.1.refs_4_ = bf16[8,768,256]{2,1,0:T(8,128)(2,1)} custom-call(bf16[640,1024]{1,0:T(8,128)(2,1)} %get-tuple-element.120.refs_0_, bf16[640,1024]{1,0:T(8,128)(2,1)} %collective-permute-done.27.refs_1_, bf16[640,1024]{1,0:T(8,128)(2,1)} %collective-permute-done.28.refs_2_, bf16[640,1024]{1,0:T(8,128)(2,1)} %collective-permute-done.29.refs_3_, ...), custom_call_target="tpu_custom_call" | custom-call | tf_op jit(solution)/shard_map/expert_grads/pallas_call | solution.py:562
  359.2 6.0 all-to-all-start.1
  369.8 20.9 %collective-permute-done.32.refs_2_ = bf16[640,512]{1,0:T(8,128)(2,1)} collective-permute-done((bf16[640,512]{1,0:T(8,128)(2,1)}, bf16[640,512]{1,0:T(8,128)(2,1)}, u32[]{:S(2)}, u32[]{:S(2)}) %collective-permute-start.32) | collective-permute-done | bytes 655392 | tf_op jit(solution)/shard_map/ppermute | solution.py:813
  390.7 10.8 %combine_rows.2 = (bf16[4,256,640]{2,1,0:T(8,128)(2,1)}, bf16[4,256,640]{2,1,0:T(8,128)(2,1)}) custom-call(s32[64]{0:T(128)} %reshape.377.starts_ref, s32[2048,128]{1,0:T(8,128)} %pad.30.place_ref, bf16[640,640]{1,0:T(8,128)(2,1)} %get-tuple-element.135.refs_0_, bf16[640,640]{1,0:T(8,128)(2,1)} %collective-permute-done.30.refs_1_, ...), custom_call_target="tpu_custom_call" | custom-call | tf_op jit(solution)/shard_map/combine_rows/pallas_call | solution.py:400
  405.4 9.3 %combine_rows.3 = (bf16[4,256,512]{2,1,0:T(8,128)(2,1)}, bf16[4,256,512]{2,1,0:T(8,128)(2,1)}) custom-call(s32[64]{0:T(128)} %reshape.377.starts_ref, s32[2048,128]{1,0:T(8,128)} %pad.30.place_ref, bf16[640,512]{1,0:T(8,128)(2,1)} %get-tuple-element.145.refs_0_, bf16[640,512]{1,0:T(8,128)(2,1)} %collective-permute-done.31.refs_1_, ...), custom_call_target="tpu_custom_call" | custom-call | tf_op jit(solution)/shard_map/combine_rows/pallas_call | solution.py:400
  414.7 24.8 %collective-permute-done.35 = bf16[4,256,640]{2,1,0:T(8,128)(2,1)} collective-permute-done((bf16[4,256,640]{2,1,0:T(8,128)(2,1)}, bf16[4,256,640]{2,1,0:T(8,128)(2,1)}, u32[]{:S(2)}, u32[]{:S(2)}) %collective-permute-start.35) | collective-permute-done | bytes 1310752 | tf_op jit(solution)/shard_map/ppermute | solution.py:963
  445.9 6.9 %collective-permute-start.38 = (bf16[256,640]{1,0:T(8,128)(2,1)}, bf16[256,640]{1,0:T(8,128)(2,1)S(1)}, u32[]{:S(2)}, u32[]{:S(2)}) collective-permute-start(bf16[256,640]{1,0:T(8,128)(2,1)} %get-tuple-element.312), channel_id=1, source_target_pairs={{0,2},{2,0},{4,6},{6,4},{1,3},{3,1},{5,7},{7,5},{8,10},{10,8},{12,... | collective-permute-start | bytes 983048 | tf_op jit(solution)/shard_map/ppermute | solution.py:809
  458.1 4.0 collective-permute-done.46.refs_3_
  462.1 11.1 %combine_rows_add.1 = bf16[4,2048,256]{2,1,0:T(8,128)(2,1)} custom-call(s32[1]{0:T(128)} %bitcast.83.own_ref, s32[64]{0:T(128)} %reshape.391.starts_ref, s32[2048,128]{1,0:T(8,128)} %pad.33.place_ref, f32[256,1024]{1,0:T(8,128)} %copy-done.2, bf16[640,1024]{1,0:T(8,128)(2,1)} %get-tuple-element.162.refs_0_, ...), custom_call_target="tpu_custom_call" | custom-call | tf_op jit(solution)/shard_map/combine_rows_add/pallas_call | solution.py:439
  473.3 4.1 collective-permute-done.39
  478.7 7.5 %collective-permute-start.41 = (bf16[256,512]{1,0:T(8,128)(2,1)S(1)}, bf16[256,512]{1,0:T(8,128)(2,1)S(1)}, u32[]{:S(2)}, u32[]{:S(2)}) collective-permute-start(bf16[256,512]{1,0:T(8,128)(2,1)S(1)} %get-tuple-element.319), channel_id=1, source_target_pairs={{0,2},{2,0},{4,6},{6,4},{1,3},{3,1},{5,7},{7,5},{8,10},{10,8},{12,... | collective-permute-start | bytes 786440 | tf_op jit(solution)/shard_map/ppermute | solution.py:809
  490.5 5.7 collective-permute-done.41
  496.2 11.4 %collective-permute-done.42 = bf16[256,512]{1,0:T(8,128)(2,1)S(1)} collective-permute-done((bf16[256,512]{1,0:T(8,128)(2,1)S(1)}, bf16[256,512]{1,0:T(8,128)(2,1)S(1)}, u32[]{:S(2)}, u32[]{:S(2)}) %collective-permute-start.42) | collective-permute-done | bytes 262176 | tf_op jit(solution)/shard_map/ppermute | solution.py:809
  513.4 10.1 %collective-permute-done.47 = bf16[256,1024]{1,0:T(8,128)(2,1)} collective-permute-done((bf16[256,1024]{1,0:T(8,128)(2,1)}, bf16[256,1024]{1,0:T(8,128)(2,1)}, u32[]{:S(2)}, u32[]{:S(2)}) %collective-permute-start.47) | collective-permute-done | bytes 524320 | tf_op jit(solution)/shard_map/ppermute | solution.py:790
  525.9 4.2 convolution_convert_fusion.grad_in
  537.4 10.8 %attend_backward.1 = (bf16[512,512]{1,0:T(8,128)(2,1)}, bf16[512,256]{1,0:T(8,128)(2,1)}, bf16[512,256]{1,0:T(8,128)(2,1)}) custom-call(bf16[512,512]{1,0:T(8,128)(2,1)} %get-tuple-element.170.query_in, bf16[512,256]{1,0:T(8,128)(2,1)} %get-tuple-element.171.key_in, bf16[512,256]{1,0:T(8,128)(2,1)} %get-tuple-element.172.value_in, ...), custom_call_target="tpu_custom_call" | custom-call | tf_op jit(solution)/shard_map/attend_backward/pallas_call | solution.py:244
  548.2 5.7 weight_products.1
  554.0 3.7 all-to-all-start.2
  557.8 3.7 multiply_reduce_fusion
  566.8 4.7 constant_dynamic-slice_fusion.32
  572.2 3.6 collective-permute-start.48
  576.6 4.5 collective-permute-start.49
  588.4 11.7 %collective-permute-done.49 = bf16[512,256]{1,0:T(8,128)(2,1)} collective-permute-done((bf16[512,256]{1,0:T(8,128)(2,1)}, bf16[512,256]{1,0:T(8,128)(2,1)}, u32[]{:S(2)}, u32[]{:S(2)}) %collective-permute-start.49) | collective-permute-done | bytes 262176 | tf_op jit(solution)/shard_map/ppermute | solution.py:769
  607.9 7.0 %all-to-all-start.3 = ((bf16[4,64,1664]{2,1,0:T(8,128)(2,1)}), bf16[4,64,1664]{2,1,0:T(8,128)(2,1)S(1)}, u32[]{:S(2)}, u32[]{:S(2)}) async-start(bf16[4,64,1664]{2,1,0:T(8,128)(2,1)} %pad_maximum_fusion.9), calls=%async_computation.3 | async-start | bytes 1703936 | tf_op jit(solution)/shard_map/all_to_all | solution.py:1017
  614.9 6.6 spread_blocks.1
  621.4 27.7 %all-to-all-done.3 = bf16[4,64,1664]{2,1,0:T(8,128)(2,1)S(1)} async-done(((bf16[4,64,1664]{2,1,0:T(8,128)(2,1)}), bf16[4,64,1664]{2,1,0:T(8,128)(2,1)S(1)}, u32[]{:S(2)}, u32[]{:S(2)}) %all-to-all-start.3) | async-done | bytes 852000 | tf_op jit(solution)/shard_map/all_to_all | solution.py:1017
  649.6 8.9 %all_gather.7 = bf16[256,1664]{1,0:T(8,128)(2,1)S(1)} all-gather(bf16[64,1664]{1,0:T(8,128)(2,1)S(1)} %pad_maximum_fusion.14), channel_id=1, replica_groups=mesh['dp'=4,'row'=4,'col'=2] {'dp'}, dimensions={0}, use_global_device_ids=true | all-gather | bytes 1064960 | tf_op jit(solution)/shard_map/all_gather | solution.py:1069
  (360 shorter events, 146.9 us)
Async XLA Ops:
  7.2 117.9 %all-gather.2.cloned.1.call-start = ((), (), s32[]{:S(2)}) async-start(), calls=%async_computation.5 | async-start | bytes 4718592 | tf_op jit(solution)/shard_map/all_gather | solution.py:844
  10.6 19.8 %collective-permute-start.6 = (bf16[64,1152]{1,0:T(8,128)(2,1)S(1)}, bf16[64,1152]{1,0:T(8,128)(2,1)}, u32[]{:S(2)}, u32[]{:S(2)}) collective-permute-start(bf16[64,1152]{1,0:T(8,128)(2,1)S(1)} %fusion.38), channel_id=1, source_target_pairs={{0,6},{2,4},{4,2},{6,0},{1,7},{3,5},{5,3},{7,1},{8,14},{10,12},{12... | collective-permute-start | bytes 442376 | tf_op jit(solution)/shard_map/ppermute | solution.py:809
  15.7 32.1 %collective-permute-start.5 = (bf16[64,1152]{1,0:T(8,128)(2,1)S(1)}, bf16[64,1152]{1,0:T(8,128)(2,1)}, u32[]{:S(2)}, u32[]{:S(2)}) collective-permute-start(bf16[64,1152]{1,0:T(8,128)(2,1)S(1)} %fusion.38), channel_id=1, source_target_pairs={{0,4},{2,6},{4,0},{6,2},{1,5},{3,7},{5,1},{7,3},{8,12},{10,14},{12... | collective-permute-start | bytes 442376 | tf_op jit(solution)/shard_map/ppermute | solution.py:809
  15.7 32.8 %collective-permute-start.4 = (bf16[64,1152]{1,0:T(8,128)(2,1)S(1)}, bf16[64,1152]{1,0:T(8,128)(2,1)}, u32[]{:S(2)}, u32[]{:S(2)}) collective-permute-start(bf16[64,1152]{1,0:T(8,128)(2,1)S(1)} %fusion.38), channel_id=1, source_target_pairs={{0,2},{2,0},{4,6},{6,4},{1,3},{3,1},{5,7},{7,5},{8,10},{10,8},{12,... | collective-permute-start | bytes 442376 | tf_op jit(solution)/shard_map/ppermute | solution.py:809
  17.5 33.1 %collective-permute-start.3 = (bf16[512,256]{0,1:T(8,128)(2,1)}, bf16[512,256]{0,1:T(8,128)(2,1)}, u32[]{:S(2)}, u32[]{:S(2)}) collective-permute-start(bf16[512,256]{0,1:T(8,128)(2,1)} %bitcast.9), channel_id=1, source_target_pairs={{0,1},{1,3},{2,4},{3,6},{4,5},{5,7},{6,0},{7,2},{8,9},{9,11},{10,1... | collective-permute-start | bytes 786440 | tf_op jit(solution)/shard_map/ppermute | solution.py:752
  19.3 42.9 %collective-permute-start.2 = (bf16[512,256]{0,1:T(8,128)(2,1)S(1)}, bf16[512,256]{0,1:T(8,128)(2,1)}, u32[]{:S(2)}, u32[]{:S(2)}) collective-permute-start(bf16[512,256]{0,1:T(8,128)(2,1)S(1)} %bitcast.263), channel_id=1, source_target_pairs={{0,4},{1,6},{2,5},{3,7},{4,0},{5,2},{6,1},{7,3},{8,12},{9,14},{10,... | collective-permute-start | bytes 786440 | tf_op jit(solution)/shard_map/ppermute | solution.py:752
  30.4 40.7 %collective-permute-start.1 = (bf16[512,256]{0,1:T(8,128)(2,1)S(1)}, bf16[512,256]{0,1:T(8,128)(2,1)S(1)}, u32[]{:S(2)}, u32[]{:S(2)}) collective-permute-start(bf16[512,256]{0,1:T(8,128)(2,1)S(1)} %bitcast.265), channel_id=1, source_target_pairs={{0,5},{1,7},{2,0},{3,2},{4,1},{5,3},{6,4},{7,6},{8,13},{9,15},{10,... | collective-permute-start | bytes 786440 | tf_op jit(solution)/shard_map/ppermute | solution.py:752
  47.8 23.3 %collective-permute-start = (bf16[512,256]{0,1:T(8,128)(2,1)S(1)}, bf16[512,256]{0,1:T(8,128)(2,1)S(1)}, u32[]{:S(2)}, u32[]{:S(2)}) collective-permute-start(bf16[512,256]{0,1:T(8,128)(2,1)S(1)} %bitcast.264), channel_id=1, source_target_pairs={{0,0},{1,2},{2,1},{3,3},{4,4},{5,6},{6,5},{7,7},{8,8},{9,10},{10,9... | collective-permute-start | bytes 786440 | tf_op jit(solution)/shard_map/ppermute | solution.py:752
  50.6 23.1 %collective-permute-start.9 = (bf16[4,64,1152]{2,1,0:T(8,128)(2,1)}, bf16[4,64,1152]{2,1,0:T(8,128)(2,1)S(1)}, u32[]{:S(2)}, u32[]{:S(2)}) collective-permute-start(bf16[4,64,1152]{2,1,0:T(8,128)(2,1)} %get-tuple-element.339), channel_id=1, source_target_pairs={{0,24},{8,16},{16,8},{24,0},{1,25},{9,17},{17,9},{25,1},{2,26},{10... | collective-permute-start | bytes 1769480 | tf_op jit(solution)/shard_map/ppermute | solution.py:813
  50.6 28.5 %collective-permute-start.8 = (bf16[4,64,1152]{2,1,0:T(8,128)(2,1)}, bf16[4,64,1152]{2,1,0:T(8,128)(2,1)S(1)}, u32[]{:S(2)}, u32[]{:S(2)}) collective-permute-start(bf16[4,64,1152]{2,1,0:T(8,128)(2,1)} %get-tuple-element.339), channel_id=1, source_target_pairs={{0,16},{8,24},{16,0},{24,8},{1,17},{9,25},{17,1},{25,9},{2,18},{10... | collective-permute-start | bytes 1769480 | tf_op jit(solution)/shard_map/ppermute | solution.py:813
  62.2 16.9 %collective-permute-start.7 = (bf16[4,64,1152]{2,1,0:T(8,128)(2,1)}, bf16[4,64,1152]{2,1,0:T(8,128)(2,1)}, u32[]{:S(2)}, u32[]{:S(2)}) collective-permute-start(bf16[4,64,1152]{2,1,0:T(8,128)(2,1)} %get-tuple-element.339), channel_id=1, source_target_pairs={{0,8},{8,0},{16,24},{24,16},{1,9},{9,1},{17,25},{25,17},{2,10},{10... | collective-permute-start | bytes 1769480 | tf_op jit(solution)/shard_map/ppermute | solution.py:813
  138.7 16.7 %collective-permute-start.17 = (bf16[640,1152]{1,0:T(8,128)(2,1)}, bf16[640,1152]{1,0:T(8,128)(2,1)}, u32[]{:S(2)}, u32[]{:S(2)}) collective-permute-start(bf16[640,1152]{1,0:T(8,128)(2,1)} %get-tuple-element.104), channel_id=1, source_target_pairs={{0,8},{8,0},{16,24},{24,16},{1,9},{9,1},{17,25},{25,17},{2,10},{10... | collective-permute-start | bytes 4423688 | tf_op jit(solution)/shard_map/ppermute | solution.py:813
  141.0 35.4 %collective-permute-start.18 = (bf16[640,1152]{1,0:T(8,128)(2,1)}, bf16[640,1152]{1,0:T(8,128)(2,1)}, u32[]{:S(2)}, u32[]{:S(2)}) collective-permute-start(bf16[640,1152]{1,0:T(8,128)(2,1)} %get-tuple-element.108), channel_id=1, source_target_pairs={{0,16},{8,24},{16,0},{24,8},{1,17},{9,25},{17,1},{25,9},{2,18},{10... | collective-permute-start | bytes 4423688 | tf_op jit(solution)/shard_map/ppermute | solution.py:813
  154.3 52.2 %collective-permute-start.19 = (bf16[640,1152]{1,0:T(8,128)(2,1)S(1)}, bf16[640,1152]{1,0:T(8,128)(2,1)S(1)}, u32[]{:S(2)}, u32[]{:S(2)}) collective-permute-start(bf16[640,1152]{1,0:T(8,128)(2,1)S(1)} %copy-done.44), channel_id=1, source_target_pairs={{0,24},{8,16},{16,8},{24,0},{1,25},{9,17},{17,9},{25,1},{2,26},{10... | collective-permute-start | bytes 4423688 | tf_op jit(solution)/shard_map/ppermute | solution.py:813
  155.4 24.5 %collective-permute-start.21 = (bf16[256,1024]{1,0:T(8,128)(2,1)S(1)}, bf16[256,1024]{1,0:T(8,128)(2,1)S(1)}, u32[]{:S(2)}, u32[]{:S(2)}) collective-permute-start(bf16[256,1024]{1,0:T(8,128)(2,1)S(1)} %multiply_convert_fusion.3.refs_0_), channel_id=1, source_target_pairs={{0,2},{2,0},{4,6},{6,4},{1,3},{3,1},{5,7},{7,5},{8,10},{10,8},{12,... | collective-permute-start | bytes 1572872 | tf_op jit(solution)/shard_map/ppermute | solution.py:809
  155.5 38.3 %collective-permute-start.23 = (bf16[256,1024]{1,0:T(8,128)(2,1)S(1)}, bf16[256,1024]{1,0:T(8,128)(2,1)S(1)}, u32[]{:S(2)}, u32[]{:S(2)}) collective-permute-start(bf16[256,1024]{1,0:T(8,128)(2,1)S(1)} %multiply_convert_fusion.3.refs_0_), channel_id=1, source_target_pairs={{0,4},{2,6},{4,0},{6,2},{1,5},{3,7},{5,1},{7,3},{8,12},{10,14},{12... | collective-permute-start | bytes 1572872 | tf_op jit(solution)/shard_map/ppermute | solution.py:809
  157.2 38.0 %collective-permute-start.25 = (bf16[256,1024]{1,0:T(8,128)(2,1)S(1)}, bf16[256,1024]{1,0:T(8,128)(2,1)S(1)}, u32[]{:S(2)}, u32[]{:S(2)}) collective-permute-start(bf16[256,1024]{1,0:T(8,128)(2,1)S(1)} %multiply_convert_fusion.3.refs_0_), channel_id=1, source_target_pairs={{0,6},{2,4},{4,2},{6,0},{1,7},{3,5},{5,3},{7,1},{8,14},{10,12},{12... | collective-permute-start | bytes 1572872 | tf_op jit(solution)/shard_map/ppermute | solution.py:809
  176.4 30.1 %collective-permute-start.20 = (bf16[256,1024]{1,0:T(8,128)(2,1)S(1)}, bf16[256,1024]{1,0:T(8,128)(2,1)S(1)}, u32[]{:S(2)}, u32[]{:S(2)}) collective-permute-start(bf16[256,1024]{1,0:T(8,128)(2,1)S(1)} %multiply_convert_fusion.3.refs_0_), channel_id=1, source_target_pairs={{0,1},{1,0},{2,3},{3,2},{4,5},{5,4},{6,7},{7,6},{8,9},{9,8},{10,11... | collective-permute-start | bytes 1572872 | tf_op jit(solution)/shard_map/ppermute | solution.py:859
  179.9 27.7 %collective-permute-start.22 = (bf16[256,1024]{1,0:T(8,128)(2,1)S(1)}, bf16[256,1024]{1,0:T(8,128)(2,1)S(1)}, u32[]{:S(2)}, u32[]{:S(2)}) collective-permute-start(bf16[256,1024]{1,0:T(8,128)(2,1)S(1)} %collective-permute-done.21.refs_2_), channel_id=1, source_target_pairs={{0,1},{1,0},{2,3},{3,2},{4,5},{5,4},{6,7},{7,6},{8,9},{9,8},{10,11... | collective-permute-start | bytes 1572872 | tf_op jit(solution)/shard_map/ppermute | solution.py:859
  193.8 19.9 %collective-permute-start.24 = (bf16[256,1024]{1,0:T(8,128)(2,1)S(1)}, bf16[256,1024]{1,0:T(8,128)(2,1)S(1)}, u32[]{:S(2)}, u32[]{:S(2)}) collective-permute-start(bf16[256,1024]{1,0:T(8,128)(2,1)S(1)} %collective-permute-done.23.refs_4_), channel_id=1, source_target_pairs={{0,1},{1,0},{2,3},{3,2},{4,5},{5,4},{6,7},{7,6},{8,9},{9,8},{10,11... | collective-permute-start | bytes 1572872 | tf_op jit(solution)/shard_map/ppermute | solution.py:859
  195.1 27.6 %collective-permute-start.26 = (bf16[256,1024]{1,0:T(8,128)(2,1)S(1)}, bf16[256,1024]{1,0:T(8,128)(2,1)}, u32[]{:S(2)}, u32[]{:S(2)}) collective-permute-start(bf16[256,1024]{1,0:T(8,128)(2,1)S(1)} %collective-permute-done.25.refs_6_), channel_id=1, source_target_pairs={{0,1},{1,0},{2,3},{3,2},{4,5},{5,4},{6,7},{7,6},{8,9},{9,8},{10,11... | collective-permute-start | bytes 1572872 | tf_op jit(solution)/shard_map/ppermute | solution.py:859
  222.7 76.9 %all-to-all-start = ((bf16[8,768,256]{2,1,0:T(8,128)(2,1)}), bf16[8,768,256]{2,1,0:T(8,128)(2,1)S(1)}, u32[]{:S(2)}, u32[]{:S(2)}) async-start(bf16[8,768,256]{2,1,0:T(8,128)(2,1)} %pad_maximum_fusion), calls=%async_computation | async-start | bytes 6291456 | tf_op jit(solution)/shard_map/all_to_all | solution.py:940
  240.5 32.0 %collective-permute-start.28 = (bf16[640,1024]{1,0:T(8,128)(2,1)}, bf16[640,1024]{1,0:T(8,128)(2,1)}, u32[]{:S(2)}, u32[]{:S(2)}) collective-permute-start(bf16[640,1024]{1,0:T(8,128)(2,1)} %get-tuple-element.122), channel_id=1, source_target_pairs={{0,16},{8,24},{16,0},{24,8},{1,17},{9,25},{17,1},{25,9},{2,18},{10... | collective-permute-start | bytes 3932168 | tf_op jit(solution)/shard_map/ppermute | solution.py:813
  242.1 57.6 %collective-permute-start.29 = (bf16[640,1024]{1,0:T(8,128)(2,1)}, bf16[640,1024]{1,0:T(8,128)(2,1)}, u32[]{:S(2)}, u32[]{:S(2)}) collective-permute-start(bf16[640,1024]{1,0:T(8,128)(2,1)} %get-tuple-element.123), channel_id=1, source_target_pairs={{0,24},{8,16},{16,8},{24,0},{1,25},{9,17},{17,9},{25,1},{2,26},{10... | collective-permute-start | bytes 3932168 | tf_op jit(solution)/shard_map/ppermute | solution.py:813
  337.7 53.0 %collective-permute-start.33 = (bf16[640,640]{1,0:T(8,128)(2,1)}, bf16[640,640]{1,0:T(8,128)(2,1)}, u32[]{:S(2)}, u32[]{:S(2)}) collective-permute-start(bf16[640,640]{1,0:T(8,128)(2,1)} %get-tuple-element.137), channel_id=1, source_target_pairs={{0,16},{8,24},{16,0},{24,8},{1,17},{9,25},{17,1},{25,9},{2,18},{10... | collective-permute-start | bytes 2457608 | tf_op jit(solution)/shard_map/ppermute | solution.py:813
  339.2 51.5 %collective-permute-start.34 = (bf16[640,640]{1,0:T(8,128)(2,1)}, bf16[640,640]{1,0:T(8,128)(2,1)}, u32[]{:S(2)}, u32[]{:S(2)}) collective-permute-start(bf16[640,640]{1,0:T(8,128)(2,1)} %get-tuple-element.138), channel_id=1, source_target_pairs={{0,24},{8,16},{16,8},{24,0},{1,25},{9,17},{17,9},{25,1},{2,26},{10... | collective-permute-start | bytes 2457608 | tf_op jit(solution)/shard_map/ppermute | solution.py:813
  339.3 30.6 %collective-permute-start.31 = (bf16[640,512]{1,0:T(8,128)(2,1)}, bf16[640,512]{1,0:T(8,128)(2,1)}, u32[]{:S(2)}, u32[]{:S(2)}) collective-permute-start(bf16[640,512]{1,0:T(8,128)(2,1)} %get-tuple-element.133), channel_id=1, source_target_pairs={{0,8},{8,0},{16,24},{24,16},{1,9},{9,1},{17,25},{25,17},{2,10},{10... | collective-permute-start | bytes 1966088 | tf_op jit(solution)/shard_map/ppermute | solution.py:813
  339.8 50.8 %collective-permute-start.32 = (bf16[640,512]{1,0:T(8,128)(2,1)}, bf16[640,512]{1,0:T(8,128)(2,1)}, u32[]{:S(2)}, u32[]{:S(2)}) collective-permute-start(bf16[640,512]{1,0:T(8,128)(2,1)} %get-tuple-element.134), channel_id=1, source_target_pairs={{0,16},{8,24},{16,0},{24,8},{1,17},{9,25},{17,1},{25,9},{2,18},{10... | collective-permute-start | bytes 1966088 | tf_op jit(solution)/shard_map/ppermute | solution.py:813
  359.2 166.6 %all-to-all-start.1 = ((bf16[8,768,256]{2,1,0:T(8,128)(2,1)}), bf16[8,768,256]{2,1,0:T(8,128)(2,1)S(1)}, u32[]{:S(2)}, u32[]{:S(2)}) async-start(bf16[8,768,256]{2,1,0:T(8,128)(2,1)} %expert_grads.1.refs_4_), calls=%async_computation.1 | async-start | bytes 6291456 | tf_op jit(solution)/shard_map/all_to_all | solution.py:962
  365.2 284.3 %reduce-scatter.2.cloned.1.call-start = ((), (), s32[]{:S(2)}) async-start(), calls=%async_computation.6 | async-start | bytes 4718592 | tf_op jit(solution)/shard_map/reduce_scatter | solution.py:1035
  365.3 38.2 %collective-permute-start.36 = (bf16[640,512]{1,0:T(8,128)(2,1)}, bf16[640,512]{1,0:T(8,128)(2,1)}, u32[]{:S(2)}, u32[]{:S(2)}) collective-permute-start(bf16[640,512]{1,0:T(8,128)(2,1)} %get-tuple-element.148), channel_id=1, source_target_pairs={{0,24},{8,16},{16,8},{24,0},{1,25},{9,17},{17,9},{25,1},{2,26},{10... | collective-permute-start | bytes 1966088 | tf_op jit(solution)/shard_map/ppermute | solution.py:813
  401.5 38.0 %collective-permute-start.35 = (bf16[4,256,640]{2,1,0:T(8,128)(2,1)}, bf16[4,256,640]{2,1,0:T(8,128)(2,1)}, u32[]{:S(2)}, u32[]{:S(2)}) collective-permute-start(bf16[4,256,640]{2,1,0:T(8,128)(2,1)} %get-tuple-element.144), channel_id=1, source_target_pairs={{0,1},{1,0},{2,3},{3,2},{4,5},{5,4},{6,7},{7,6},{8,9},{9,8},{10,11... | collective-permute-start | bytes 3932168 | tf_op jit(solution)/shard_map/ppermute | solution.py:963
  403.5 49.4 %collective-permute-start.44 = (bf16[640,1024]{1,0:T(8,128)(2,1)}, bf16[640,1024]{1,0:T(8,128)(2,1)}, u32[]{:S(2)}, u32[]{:S(2)}) collective-permute-start(bf16[640,1024]{1,0:T(8,128)(2,1)} %get-tuple-element.163), channel_id=1, source_target_pairs={{0,8},{8,0},{16,24},{24,16},{1,9},{9,1},{17,25},{25,17},{2,10},{10... | collective-permute-start | bytes 3932168 | tf_op jit(solution)/shard_map/ppermute | solution.py:813
  404.0 48.9 %collective-permute-start.45 = (bf16[640,1024]{1,0:T(8,128)(2,1)}, bf16[640,1024]{1,0:T(8,128)(2,1)}, u32[]{:S(2)}, u32[]{:S(2)}) collective-permute-start(bf16[640,1024]{1,0:T(8,128)(2,1)} %get-tuple-element.164), channel_id=1, source_target_pairs={{0,16},{8,24},{16,0},{24,8},{1,17},{9,25},{17,1},{25,9},{2,18},{10... | collective-permute-start | bytes 3932168 | tf_op jit(solution)/shard_map/ppermute | solution.py:813
  405.3 56.8 %collective-permute-start.46 = (bf16[640,1024]{1,0:T(8,128)(2,1)}, bf16[640,1024]{1,0:T(8,128)(2,1)}, u32[]{:S(2)}, u32[]{:S(2)}) collective-permute-start(bf16[640,1024]{1,0:T(8,128)(2,1)} %get-tuple-element.165), channel_id=1, source_target_pairs={{0,24},{8,16},{16,8},{24,0},{1,25},{9,17},{17,9},{25,1},{2,26},{10... | collective-permute-start | bytes 3932168 | tf_op jit(solution)/shard_map/ppermute | solution.py:813
  439.4 37.9 %collective-permute-start.37 = (bf16[4,256,512]{2,1,0:T(8,128)(2,1)}, bf16[4,256,512]{2,1,0:T(8,128)(2,1)}, u32[]{:S(2)}, u32[]{:S(2)}) collective-permute-start(bf16[4,256,512]{2,1,0:T(8,128)(2,1)} %get-tuple-element.152), channel_id=1, source_target_pairs={{0,1},{1,0},{2,3},{3,2},{4,5},{5,4},{6,7},{7,6},{8,9},{9,8},{10,11... | collective-permute-start | bytes 3145736 | tf_op jit(solution)/shard_map/ppermute | solution.py:966
  445.9 27.3 %collective-permute-start.38 = (bf16[256,640]{1,0:T(8,128)(2,1)}, bf16[256,640]{1,0:T(8,128)(2,1)S(1)}, u32[]{:S(2)}, u32[]{:S(2)}) collective-permute-start(bf16[256,640]{1,0:T(8,128)(2,1)} %get-tuple-element.312), channel_id=1, source_target_pairs={{0,2},{2,0},{4,6},{6,4},{1,3},{3,1},{5,7},{7,5},{8,10},{10,8},{12,... | collective-permute-start | bytes 983048 | tf_op jit(solution)/shard_map/ppermute | solution.py:809
  452.9 24.5 %collective-permute-start.39 = (bf16[256,640]{1,0:T(8,128)(2,1)}, bf16[256,640]{1,0:T(8,128)(2,1)S(1)}, u32[]{:S(2)}, u32[]{:S(2)}) collective-permute-start(bf16[256,640]{1,0:T(8,128)(2,1)} %get-tuple-element.311), channel_id=1, source_target_pairs={{0,4},{2,6},{4,0},{6,2},{1,5},{3,7},{5,1},{7,3},{8,12},{10,14},{12... | collective-permute-start | bytes 983048 | tf_op jit(solution)/shard_map/ppermute | solution.py:809
  452.9 24.4 %collective-permute-start.40 = (bf16[256,640]{1,0:T(8,128)(2,1)S(1)}, bf16[256,640]{1,0:T(8,128)(2,1)S(1)}, u32[]{:S(2)}, u32[]{:S(2)}) collective-permute-start(bf16[256,640]{1,0:T(8,128)(2,1)S(1)} %get-tuple-element.310), channel_id=1, source_target_pairs={{0,6},{2,4},{4,2},{6,0},{1,7},{3,5},{5,3},{7,1},{8,14},{10,12},{12... | collective-permute-start | bytes 983048 | tf_op jit(solution)/shard_map/ppermute | solution.py:809
  478.7 17.5 %collective-permute-start.41 = (bf16[256,512]{1,0:T(8,128)(2,1)S(1)}, bf16[256,512]{1,0:T(8,128)(2,1)S(1)}, u32[]{:S(2)}, u32[]{:S(2)}) collective-permute-start(bf16[256,512]{1,0:T(8,128)(2,1)S(1)} %get-tuple-element.319), channel_id=1, source_target_pairs={{0,2},{2,0},{4,6},{6,4},{1,3},{3,1},{5,7},{7,5},{8,10},{10,8},{12,... | collective-permute-start | bytes 786440 | tf_op jit(solution)/shard_map/ppermute | solution.py:809
  486.2 21.3 %collective-permute-start.42 = (bf16[256,512]{1,0:T(8,128)(2,1)S(1)}, bf16[256,512]{1,0:T(8,128)(2,1)S(1)}, u32[]{:S(2)}, u32[]{:S(2)}) collective-permute-start(bf16[256,512]{1,0:T(8,128)(2,1)S(1)} %get-tuple-element.318), channel_id=1, source_target_pairs={{0,4},{2,6},{4,0},{6,2},{1,5},{3,7},{5,1},{7,3},{8,12},{10,14},{12... | collective-permute-start | bytes 786440 | tf_op jit(solution)/shard_map/ppermute | solution.py:809
  486.2 21.3 %collective-permute-start.43 = (bf16[256,512]{1,0:T(8,128)(2,1)S(1)}, bf16[256,512]{1,0:T(8,128)(2,1)S(1)}, u32[]{:S(2)}, u32[]{:S(2)}) collective-permute-start(bf16[256,512]{1,0:T(8,128)(2,1)S(1)} %get-tuple-element.317), channel_id=1, source_target_pairs={{0,6},{2,4},{4,2},{6,0},{1,7},{3,5},{5,3},{7,1},{8,14},{10,12},{12... | collective-permute-start | bytes 786440 | tf_op jit(solution)/shard_map/ppermute | solution.py:809
  554.0 52.1 %all-to-all-start.2 = ((bf16[4,256,1664]{2,1,0:T(8,128)(2,1)}), bf16[4,256,1664]{2,1,0:T(8,128)(2,1)S(1)}, u32[]{:S(2)}, u32[]{:S(2)}) async-start(bf16[4,256,1664]{2,1,0:T(8,128)(2,1)} %bitcast.210), calls=%async_computation.2 | async-start | bytes 6815744 | tf_op jit(solution)/shard_map/all_to_all | solution.py:1012
  572.2 16.1 %collective-permute-start.48 = (bf16[512,256]{1,0:T(8,128)(2,1)}, bf16[512,256]{1,0:T(8,128)(2,1)}, u32[]{:S(2)}, u32[]{:S(2)}) collective-permute-start(bf16[512,256]{1,0:T(8,128)(2,1)} %bitcast.208), channel_id=1, source_target_pairs={{0,0},{2,1},{1,2},{3,3},{4,4},{6,5},{5,6},{7,7},{8,8},{10,9},{9,10... | collective-permute-start | bytes 786440 | tf_op jit(solution)/shard_map/ppermute | solution.py:769
  576.6 23.4 %collective-permute-start.49 = (bf16[512,256]{1,0:T(8,128)(2,1)}, bf16[512,256]{1,0:T(8,128)(2,1)}, u32[]{:S(2)}, u32[]{:S(2)}) collective-permute-start(bf16[512,256]{1,0:T(8,128)(2,1)} %bitcast.207), channel_id=1, source_target_pairs={{5,0},{7,1},{0,2},{2,3},{1,4},{3,5},{4,6},{6,7},{13,8},{15,9},{8,1... | collective-permute-start | bytes 786440 | tf_op jit(solution)/shard_map/ppermute | solution.py:769
  581.8 21.7 %collective-permute-start.50 = (bf16[512,256]{1,0:T(8,128)(2,1)}, bf16[512,256]{1,0:T(8,128)(2,1)}, u32[]{:S(2)}, u32[]{:S(2)}) collective-permute-start(bf16[512,256]{1,0:T(8,128)(2,1)} %bitcast.206), channel_id=1, source_target_pairs={{4,0},{6,1},{5,2},{7,3},{0,4},{2,5},{1,6},{3,7},{12,8},{14,9},{13,... | collective-permute-start | bytes 786440 | tf_op jit(solution)/shard_map/ppermute | solution.py:769
  584.8 18.7 %collective-permute-start.51 = (bf16[512,256]{1,0:T(8,128)(2,1)}, bf16[512,256]{1,0:T(8,128)(2,1)}, u32[]{:S(2)}, u32[]{:S(2)}) collective-permute-start(bf16[512,256]{1,0:T(8,128)(2,1)} %bitcast.205), channel_id=1, source_target_pairs={{1,0},{3,1},{4,2},{6,3},{5,4},{7,5},{0,6},{2,7},{9,8},{11,9},{12,1... | collective-permute-start | bytes 786440 | tf_op jit(solution)/shard_map/ppermute | solution.py:769
  607.9 41.2 %all-to-all-start.3 = ((bf16[4,64,1664]{2,1,0:T(8,128)(2,1)}), bf16[4,64,1664]{2,1,0:T(8,128)(2,1)S(1)}, u32[]{:S(2)}, u32[]{:S(2)}) async-start(bf16[4,64,1664]{2,1,0:T(8,128)(2,1)} %pad_maximum_fusion.9), calls=%async_computation.3 | async-start | bytes 1703936 | tf_op jit(solution)/shard_map/all_to_all | solution.py:1017
  (56 other events, 667.5 us)
Sparse Core Ops, SparseCore 0:
  16.5 108.5 all-gather.1
  530.2 116.9 reduce-scatter.1
